TPU v7x, 32 devices: a whole 2x2x4 slice. The times are simulated.
32 devices in a mesh: dp: 2 (over y), context: 16 (over z, x, core).
Axes of the slice: x: 2, y: 2, z: 4, core: 2. Of those that a mesh axis runs over, the one named last changes fastest.
Arguments:
- query_rows: bfloat16 [4096, 4096], P(('dp', 'context')), parts along dimension 0, may hold values from -6 to 6
- key_rows: bfloat16 [4096, 512], P(('dp', 'context')), parts along dimension 0, may hold values from -6 to 6
- value_rows: bfloat16 [4096, 512], P(('dp', 'context')), parts along dimension 0, may hold values from -6 to 6
- grad_out: bfloat16 [4096, 4096], P(('dp', 'context')), parts along dimension 0, may hold values from -6 to 6
- doc_bounds: int32 [10], P('dp'), parts along dimension 0, may hold values from 0 to 2048, as said below
Outputs:
- attn_out: bfloat16 [4096, 4096], P(('dp', 'context')), parts along dimension 0
- d_query: bfloat16 [4096, 4096], P(('dp', 'context')), parts along dimension 0
- d_key: bfloat16 [4096, 512], P(('dp', 'context')), parts along dimension 0
- d_value: bfloat16 [4096, 512], P(('dp', 'context')), parts along dimension 0
There are 2 independent parts, one for each index of `dp`. A program takes and returns all parts, laid end to end along the dimension named above; each array names one. Nothing has to cross between parts.
Inputs may be any that keep to these rules, and one draw needn't show every extreme that they name: doc_bounds[0] = 0, doc_bounds[4] = 2048, strictly rising; every response is 256 to 1024 tokens long; at least one is exactly 1024 and at least one exactly 256.
All inputs are finite; a program needn't handle non-finite values.
Results may differ from a plain program's by a relative error of at most 0.035.
Values may be sent and summed in bfloat16 or wider, within the bound.
No kernel may reach another device: no remote copies, remote signals or barrier semaphores. Data moves between devices by JAX's collectives and lax.ppermute only.
A program may use at most 64 MiB of HBM per device.

v0:
```python
import jax
import jax.numpy as jnp
from jax import lax
from jax.sharding import PartitionSpec as P

HEAD_DIM = 128
MAXDOC = 1024
QBLOCK = 512


masked_score = -1e30


def segment_ids(positions, doc_bounds):
    inner_bounds = doc_bounds[1:-1]
    return jnp.sum((positions[:, None] >= inner_bounds[None, :]).astype(jnp.int32), axis=1)


def block_pass(q_block, k_window, v_window, o_grad, allowed, softmax_scale):
    scores = (
        jnp.einsum("qhd,kd->hqk", q_block, k_window, preferred_element_type=jnp.float32)
        * softmax_scale
    )
    scores = jnp.where(allowed[None], scores, masked_score)
    top_score = jnp.max(scores, axis=-1, keepdims=True)
    expd = jnp.where(allowed[None], jnp.exp(scores - top_score), 0.0)
    probs = expd / jnp.sum(expd, axis=-1, keepdims=True)
    weights = probs.astype(jnp.bfloat16)
    attended = jnp.einsum(
        "hqk,kd->qhd", weights, v_window, preferred_element_type=jnp.float32
    ).astype(jnp.bfloat16)
    inner_prod = jnp.sum(o_grad.astype(jnp.float32) * attended.astype(jnp.float32), axis=-1)
    prob_grad = jnp.einsum("qhd,kd->hqk", o_grad, v_window, preferred_element_type=jnp.float32)
    score_grad = (probs * (prob_grad - jnp.transpose(inner_prod)[:, :, None])).astype(jnp.bfloat16)
    q_grad = (
        softmax_scale
        * jnp.einsum("hqk,kd->qhd", score_grad, k_window, preferred_element_type=jnp.float32)
    ).astype(jnp.bfloat16)
    k_grad = softmax_scale * jnp.einsum(
        "hqk,qhd->kd", score_grad, q_block, preferred_element_type=jnp.float32
    )
    v_grad = jnp.einsum("hqk,qhd->kd", weights, o_grad, preferred_element_type=jnp.float32)
    return (attended, q_grad, k_grad, v_grad)


def head_pass(q_heads, k_head, v_head, g_heads, doc_bounds, softmax_scale):
    length = q_heads.shape[0]
    width = k_head.shape[1]
    span = QBLOCK + MAXDOC
    k_pad = jnp.concatenate([jnp.zeros((MAXDOC, width), k_head.dtype), k_head], axis=0)
    v_pad = jnp.concatenate([jnp.zeros((MAXDOC, width), v_head.dtype), v_head], axis=0)
    seg_all = segment_ids(jnp.arange(length + MAXDOC, dtype=jnp.int32) - MAXDOC, doc_bounds)

    def step(carry, start):
        k_acc, v_acc = carry
        q_block = lax.dynamic_slice_in_dim(q_heads, start, QBLOCK, 0)
        g_block = lax.dynamic_slice_in_dim(g_heads, start, QBLOCK, 0)
        k_window = lax.dynamic_slice_in_dim(k_pad, start, span, 0)
        v_window = lax.dynamic_slice_in_dim(v_pad, start, span, 0)
        q_pos = start + jnp.arange(QBLOCK, dtype=jnp.int32)
        k_pos = start - MAXDOC + jnp.arange(span, dtype=jnp.int32)
        q_seg = lax.dynamic_slice_in_dim(seg_all, start + MAXDOC, QBLOCK, 0)
        k_seg = lax.dynamic_slice_in_dim(seg_all, start, span, 0)
        allowed = (
            (q_seg[:, None] == k_seg[None, :])
            & (k_pos[None, :] <= q_pos[:, None])
            & (k_pos[None, :] >= 0)
        )
        attended, q_grad, k_grad, v_grad = block_pass(
            q_block, k_window, v_window, g_block, allowed, softmax_scale
        )
        k_acc = lax.dynamic_update_slice_in_dim(
            k_acc, lax.dynamic_slice_in_dim(k_acc, start, span, 0) + k_grad, start, 0
        )
        v_acc = lax.dynamic_update_slice_in_dim(
            v_acc, lax.dynamic_slice_in_dim(v_acc, start, span, 0) + v_grad, start, 0
        )
        return ((k_acc, v_acc), (attended, q_grad))

    starts = jnp.arange(0, length, QBLOCK, dtype=jnp.int32)
    empty = jnp.zeros((length + MAXDOC, width), jnp.float32)
    (k_acc, v_acc), (attended, q_grad) = lax.scan(step, (empty, empty), starts)
    heads_here = q_heads.shape[1]
    return (
        attended.reshape(length, heads_here, width),
        q_grad.reshape(length, heads_here, width),
        k_acc[MAXDOC:],
        v_acc[MAXDOC:],
    )


def body(query_rows, key_rows, value_rows, grad_out, doc_bounds):
    tok_rows = query_rows.shape[0]
    width = HEAD_DIM
    kv_count = key_rows.shape[1] // width
    softmax_scale = HEAD_DIM ** (-0.5)
    devices = lax.axis_size("context")
    per_slot = devices // kv_count
    k_slots = jnp.broadcast_to(
        key_rows.reshape(tok_rows, kv_count, 1, width), (tok_rows, kv_count, per_slot, width)
    ).reshape(tok_rows, devices * width)
    v_slots = jnp.broadcast_to(
        value_rows.reshape(tok_rows, kv_count, 1, width), (tok_rows, kv_count, per_slot, width)
    ).reshape(tok_rows, devices * width)
    q_cols, k_cols, v_cols, g_cols = (
        lax.all_to_all(query_rows, "context", split_axis=1, concat_axis=0, tiled=True),
        lax.all_to_all(k_slots, "context", split_axis=1, concat_axis=0, tiled=True),
        lax.all_to_all(v_slots, "context", split_axis=1, concat_axis=0, tiled=True),
        lax.all_to_all(grad_out, "context", split_axis=1, concat_axis=0, tiled=True),
    )
    length = q_cols.shape[0]
    heads_here = q_cols.shape[1] // width
    attended, q_grad, k_grad, v_grad = head_pass(
        q_cols.reshape(length, heads_here, width),
        k_cols,
        v_cols,
        g_cols.reshape(length, heads_here, width),
        doc_bounds,
        softmax_scale,
    )
    attn_out, d_query = (
        lax.all_to_all(
            attended.reshape(length, heads_here * width),
            "context",
            split_axis=0,
            concat_axis=1,
            tiled=True,
        ),
        lax.all_to_all(
            q_grad.reshape(length, heads_here * width),
            "context",
            split_axis=0,
            concat_axis=1,
            tiled=True,
        ),
    )
    k_back, v_back = (
        lax.all_to_all(
            k_grad.astype(jnp.bfloat16), "context", split_axis=0, concat_axis=1, tiled=True
        ).astype(k_grad.dtype),
        lax.all_to_all(
            v_grad.astype(jnp.bfloat16), "context", split_axis=0, concat_axis=1, tiled=True
        ).astype(v_grad.dtype),
    )
    d_key = (
        k_back.reshape(tok_rows, kv_count, per_slot, width)
        .sum(axis=2)
        .reshape(tok_rows, kv_count * width)
    )
    d_value = (
        v_back.reshape(tok_rows, kv_count, per_slot, width)
        .sum(axis=2)
        .reshape(tok_rows, kv_count * width)
    )
    return (attn_out, d_query, d_key.astype(jnp.bfloat16), d_value.astype(jnp.bfloat16))


def solution(mesh):
    return jax.shard_map(
        body,
        mesh=mesh,
        in_specs=(
            P(("dp", "context"), None),
            P(("dp", "context"), None),
            P(("dp", "context"), None),
            P(("dp", "context"), None),
            P("dp"),
        ),
        out_specs=(
            P(("dp", "context"), None),
            P(("dp", "context"), None),
            P(("dp", "context"), None),
            P(("dp", "context"), None),
        ),
        check_vma=False,
    )
```

profile of v0, /device:TPU:0, one launch (start us, length us, event | category | flops | bytes accessed | tf_op | source)
XLA Modules:
  0.0 353.9 jit_solution(15612836167336642508)
XLA Ops:
  2.5 7.4 %all-to-all-start.2 = ((bf16[128,16,128]{2,0,1:T(8,128)(2,1)}), bf16[128,16,128]{2,0,1:T(8,128)(2,1)S(1)}, u32[]{:S(2)}, u32[]{:S(2)}) async-start(bf16[128,16,128]{2,0,1:T(8,128)(2,1)} %bitcast.19), calls=%async_computation.2 | async-start | bytes 1048576 | tf_op jit(solution)/shard_map/all_to_all | solution.py:108
  10.9 13.4 %all-to-all-done.2 = bf16[128,16,128]{2,0,1:T(8,128)(2,1)S(1)} async-done(((bf16[128,16,128]{2,0,1:T(8,128)(2,1)}), bf16[128,16,128]{2,0,1:T(8,128)(2,1)S(1)}, u32[]{:S(2)}, u32[]{:S(2)}) %all-to-all-start.2) | async-done | bytes 524320 | tf_op jit(solution)/shard_map/all_to_all | solution.py:108
  25.2 4.1 %all-to-all-start = ((bf16[128,16,128]{2,0,1:T(8,128)(2,1)}), bf16[128,16,128]{2,0,1:T(8,128)(2,1)S(1)}, u32[]{:S(2)}, u32[]{:S(2)}) async-start(bf16[128,16,128]{2,0,1:T(8,128)(2,1)} %bitcast.14), calls=%async_computation | async-start | bytes 1048576 | tf_op jit(solution)/shard_map/all_to_all | solution.py:107
  30.6 13.1 %all-to-all-done = bf16[128,16,128]{2,0,1:T(8,128)(2,1)S(1)} async-done(((bf16[128,16,128]{2,0,1:T(8,128)(2,1)}), bf16[128,16,128]{2,0,1:T(8,128)(2,1)S(1)}, u32[]{:S(2)}, u32[]{:S(2)}) %all-to-all-start) | async-done | bytes 524320 | tf_op jit(solution)/shard_map/all_to_all | solution.py:107
  43.8 4.2 %all-to-all-start.1 = ((bf16[128,16,256]{0,2,1:T(8,128)(2,1)}), bf16[128,16,256]{0,2,1:T(8,128)(2,1)S(1)}, u32[]{:S(2)}, u32[]{:S(2)}) async-start(bf16[128,16,256]{0,2,1:T(8,128)(2,1)} %bitcast.17), calls=%async_computation.1 | async-start | bytes 2097152 | tf_op jit(solution)/shard_map/all_to_all | solution.py:106
  49.3 21.6 %all-to-all-done.1 = bf16[128,16,256]{0,2,1:T(8,128)(2,1)S(1)} async-done(((bf16[128,16,256]{0,2,1:T(8,128)(2,1)}), bf16[128,16,256]{0,2,1:T(8,128)(2,1)S(1)}, u32[]{:S(2)}, u32[]{:S(2)}) %all-to-all-start.1) | async-done | bytes 1048608 | tf_op jit(solution)/shard_map/all_to_all | solution.py:106
  71.0 6.9 %all-to-all-start.3 = ((bf16[128,16,256]{0,2,1:T(8,128)(2,1)}), bf16[128,16,256]{0,2,1:T(8,128)(2,1)S(1)}, u32[]{:S(2)}, u32[]{:S(2)}) async-start(bf16[128,16,256]{0,2,1:T(8,128)(2,1)} %bitcast.22), calls=%async_computation.3 | async-start | bytes 2097152 | tf_op jit(solution)/shard_map/all_to_all | solution.py:109
  84.1 16.7 %all-to-all-done.3 = bf16[128,16,256]{0,2,1:T(8,128)(2,1)S(1)} async-done(((bf16[128,16,256]{0,2,1:T(8,128)(2,1)}), bf16[128,16,256]{0,2,1:T(8,128)(2,1)S(1)}, u32[]{:S(2)}, u32[]{:S(2)}) %all-to-all-start.3) | async-done | bytes 1048608 | tf_op jit(solution)/shard_map/all_to_all | solution.py:109
  105.3 147.7 %while.18 = (s32[]{:T(128)}, f32[3072,128]{1,0:T(8,128)}, f32[3072,128]{1,0:T(8,128)}, bf16[4,512,2,128]{3,2,1,0:T(2,128)(2,1)}, bf16[4,512,2,128]{3,2,1,0:T(2,1...) while((s32[]{:T(128)}, f32[3072,128]{1,0:T(8,128)}, ...), condition=%wide.region_5.6_spmd, body=%wide.region_1.5_spmd.sunk | while | flops 2437879296 | bytes 77659576 | solution.py:82
  114.7 7.0 %fusion.84 = (f32[2,512]{1,0:T(2,128)S(1)}, f32[2,512,1536]{1,2,0:T(8,128)}) fusion(pred[512,1536]{0,1:T(8,128)(4,1)S(1)} %and_and_fusion.2, bf16[3072,128]{1,0:T(8,128)(2,1)} %get-tuple-element.381, s32[]{:T(128)S(6)} %select_n.52, bf16[2048,2,128]{0,2,1:T(8,128)(2,1)} %get-tuple-element.382, s32[]{:T(128)S(6)} %select_n.50), kind=kOutput, calls=%fused_computation.61.clone.1 | convolution fusion | flops 410519040 | bytes 8523784 | tf_op jit(solution)/shard_map/while/body/eval_jaxpr/sub | solution.py:26
  121.7 3.8 %fusion.85 = bf16[2,512,1536]{1,2,0:T(8,128)(2,1)S(1)} fusion(f32[2,512,1536]{1,2,0:T(8,128)} %get-tuple-element.332, f32[2,512]{1,0:T(2,128)S(1)} %get-tuple-element.333), kind=kLoop, calls=%fused_computation.12.clone.1 | loop fusion | flops 3145728 | bytes 9441280 | tf_op jit(solution)/shard_map/while/body/eval_jaxpr/convert_element_type | solution.py:28
  151.9 7.0 %fusion.84 = (f32[2,512]{1,0:T(2,128)S(1)}, f32[2,512,1536]{1,2,0:T(8,128)}) fusion(pred[512,1536]{0,1:T(8,128)(4,1)S(1)} %and_and_fusion.2, bf16[3072,128]{1,0:T(8,128)(2,1)} %get-tuple-element.381, s32[]{:T(128)S(6)} %select_n.52, bf16[2048,2,128]{0,2,1:T(8,128)(2,1)} %get-tuple-element.382, s32[]{:T(128)S(6)} %select_n.50), kind=kOutput, calls=%fused_computation.61.clone.1 | convolution fusion | flops 410519040 | bytes 8523784 | tf_op jit(solution)/shard_map/while/body/eval_jaxpr/sub | solution.py:26
  158.9 3.8 %fusion.85 = bf16[2,512,1536]{1,2,0:T(8,128)(2,1)S(1)} fusion(f32[2,512,1536]{1,2,0:T(8,128)} %get-tuple-element.332, f32[2,512]{1,0:T(2,128)S(1)} %get-tuple-element.333), kind=kLoop, calls=%fused_computation.12.clone.1 | loop fusion | flops 3145728 | bytes 9441280 | tf_op jit(solution)/shard_map/while/body/eval_jaxpr/convert_element_type | solution.py:28
  189.1 7.0 %fusion.84 = (f32[2,512]{1,0:T(2,128)S(1)}, f32[2,512,1536]{1,2,0:T(8,128)}) fusion(pred[512,1536]{0,1:T(8,128)(4,1)S(1)} %and_and_fusion.2, bf16[3072,128]{1,0:T(8,128)(2,1)} %get-tuple-element.381, s32[]{:T(128)S(6)} %select_n.52, bf16[2048,2,128]{0,2,1:T(8,128)(2,1)} %get-tuple-element.382, s32[]{:T(128)S(6)} %select_n.50), kind=kOutput, calls=%fused_computation.61.clone.1 | convolution fusion | flops 410519040 | bytes 8523784 | tf_op jit(solution)/shard_map/while/body/eval_jaxpr/sub | solution.py:26
  196.1 3.8 %fusion.85 = bf16[2,512,1536]{1,2,0:T(8,128)(2,1)S(1)} fusion(f32[2,512,1536]{1,2,0:T(8,128)} %get-tuple-element.332, f32[2,512]{1,0:T(2,128)S(1)} %get-tuple-element.333), kind=kLoop, calls=%fused_computation.12.clone.1 | loop fusion | flops 3145728 | bytes 9441280 | tf_op jit(solution)/shard_map/while/body/eval_jaxpr/convert_element_type | solution.py:28
  226.3 6.9 %fusion.84 = (f32[2,512]{1,0:T(2,128)S(1)}, f32[2,512,1536]{1,2,0:T(8,128)}) fusion(pred[512,1536]{0,1:T(8,128)(4,1)S(1)} %and_and_fusion.2, bf16[3072,128]{1,0:T(8,128)(2,1)} %get-tuple-element.381, s32[]{:T(128)S(6)} %select_n.52, bf16[2048,2,128]{0,2,1:T(8,128)(2,1)} %get-tuple-element.382, s32[]{:T(128)S(6)} %select_n.50), kind=kOutput, calls=%fused_computation.61.clone.1 | convolution fusion | flops 410519040 | bytes 8523784 | tf_op jit(solution)/shard_map/while/body/eval_jaxpr/sub | solution.py:26
  255.1 6.9 %all-to-all-start.6 = ((bf16[16,128,128]{2,1,0:T(8,128)(2,1)}), bf16[16,128,128]{2,1,0:T(8,128)(2,1)S(1)}, u32[]{:S(2)}, u32[]{:S(2)}) async-start(bf16[16,128,128]{2,1,0:T(8,128)(2,1)} %bitcast.28), calls=%async_computation.6 | async-start | bytes 1048576 | tf_op jit(solution)/shard_map/all_to_all | solution.py:138
  264.3 12.3 %all-to-all-done.6 = bf16[16,128,128]{2,1,0:T(8,128)(2,1)S(1)} async-done(((bf16[16,128,128]{2,1,0:T(8,128)(2,1)}), bf16[16,128,128]{2,1,0:T(8,128)(2,1)S(1)}, u32[]{:S(2)}, u32[]{:S(2)}) %all-to-all-start.6) | async-done | bytes 524320 | tf_op jit(solution)/shard_map/all_to_all | solution.py:138
  276.5 4.1 %all-to-all-start.7 = ((bf16[16,128,128]{2,1,0:T(8,128)(2,1)}), bf16[16,128,128]{2,1,0:T(8,128)(2,1)S(1)}, u32[]{:S(2)}, u32[]{:S(2)}) async-start(bf16[16,128,128]{2,1,0:T(8,128)(2,1)} %bitcast.32), calls=%async_computation.7 | async-start | bytes 1048576 | tf_op jit(solution)/shard_map/all_to_all | solution.py:141
  282.1 13.0 %all-to-all-done.7 = bf16[16,128,128]{2,1,0:T(8,128)(2,1)S(1)} async-done(((bf16[16,128,128]{2,1,0:T(8,128)(2,1)}), bf16[16,128,128]{2,1,0:T(8,128)(2,1)S(1)}, u32[]{:S(2)}, u32[]{:S(2)}) %all-to-all-start.7) | async-done | bytes 524320 | tf_op jit(solution)/shard_map/all_to_all | solution.py:141
  295.1 4.1 %all-to-all-start.5 = ((bf16[16,128,256]{2,1,0:T(8,128)(2,1)}), bf16[16,128,256]{2,1,0:T(8,128)(2,1)S(1)}, u32[]{:S(2)}, u32[]{:S(2)}) async-start(bf16[16,128,256]{2,1,0:T(8,128)(2,1)} %all_to_all.118), calls=%async_computation.5 | async-start | bytes 2097152 | tf_op jit(solution)/shard_map/all_to_all | solution.py:129
  300.7 21.4 %all-to-all-done.5 = bf16[16,128,256]{2,1,0:T(8,128)(2,1)S(1)} async-done(((bf16[16,128,256]{2,1,0:T(8,128)(2,1)}), bf16[16,128,256]{2,1,0:T(8,128)(2,1)S(1)}, u32[]{:S(2)}, u32[]{:S(2)}) %all-to-all-start.5) | async-done | bytes 1048608 | tf_op jit(solution)/shard_map/all_to_all | solution.py:129
  322.1 6.9 %all-to-all-start.4 = ((bf16[16,128,256]{2,1,0:T(8,128)(2,1)}), bf16[16,128,256]{2,1,0:T(8,128)(2,1)S(1)}, u32[]{:S(2)}, u32[]{:S(2)}) async-start(bf16[16,128,256]{2,1,0:T(8,128)(2,1)} %all_to_all.114), calls=%async_computation.4 | async-start | bytes 2097152 | tf_op jit(solution)/shard_map/all_to_all | solution.py:122
  333.0 19.0 %all-to-all-done.4 = bf16[16,128,256]{2,1,0:T(8,128)(2,1)S(1)} async-done(((bf16[16,128,256]{2,1,0:T(8,128)(2,1)}), bf16[16,128,256]{2,1,0:T(8,128)(2,1)S(1)}, u32[]{:S(2)}, u32[]{:S(2)}) %all-to-all-start.4) | async-done | bytes 1048608 | tf_op jit(solution)/shard_map/all_to_all | solution.py:122
  (149 shorter events, 117.5 us)
Async XLA Ops:
  0.6 28.7 %copy-start.3 = (bf16[128,4096]{1,0:T(8,128)(2,1)S(1)}, bf16[128,4096]{1,0:T(8,128)(2,1)}, u32[]{:S(2)}) copy-start(bf16[128,4096]{1,0:T(8,128)(2,1)} %param.7) | copy-start | bytes 3145732
  2.5 21.8 %all-to-all-start.2 = ((bf16[128,16,128]{2,0,1:T(8,128)(2,1)}), bf16[128,16,128]{2,0,1:T(8,128)(2,1)S(1)}, u32[]{:S(2)}, u32[]{:S(2)}) async-start(bf16[128,16,128]{2,0,1:T(8,128)(2,1)} %bitcast.19), calls=%async_computation.2 | async-start | bytes 1048576 | tf_op jit(solution)/shard_map/all_to_all | solution.py:108
  9.8 38.2 %copy-start.4 = (bf16[128,4096]{1,0:T(8,128)(2,1)S(1)}, bf16[128,4096]{1,0:T(8,128)(2,1)}, u32[]{:S(2)}) copy-start(bf16[128,4096]{1,0:T(8,128)(2,1)} %param.10) | copy-start | bytes 3145732
  25.2 18.6 %all-to-all-start = ((bf16[128,16,128]{2,0,1:T(8,128)(2,1)}), bf16[128,16,128]{2,0,1:T(8,128)(2,1)S(1)}, u32[]{:S(2)}, u32[]{:S(2)}) async-start(bf16[128,16,128]{2,0,1:T(8,128)(2,1)} %bitcast.14), calls=%async_computation | async-start | bytes 1048576 | tf_op jit(solution)/shard_map/all_to_all | solution.py:107
  43.8 27.2 %copy-start.2 = (bf16[128,16,128]{2,0,1:T(8,128)(2,1)}, bf16[128,16,128]{2,0,1:T(8,128)(2,1)S(1)}, u32[]{:S(2)}) copy-start(bf16[128,16,128]{2,0,1:T(8,128)(2,1)S(1)} %all-to-all-done) | copy-start | bytes 1572868
  43.8 34.1 %copy-start.7 = (s32[5]{0:T(128)S(1)}, s32[5]{0:T(128)}, u32[]{:S(2)}) copy-start(s32[5]{0:T(128)} %param.11) | copy-start | bytes 64
  43.8 27.2 %all-to-all-start.1 = ((bf16[128,16,256]{0,2,1:T(8,128)(2,1)}), bf16[128,16,256]{0,2,1:T(8,128)(2,1)S(1)}, u32[]{:S(2)}, u32[]{:S(2)}) async-start(bf16[128,16,256]{0,2,1:T(8,128)(2,1)} %bitcast.17), calls=%async_computation.1 | async-start | bytes 2097152 | tf_op jit(solution)/shard_map/all_to_all | solution.py:106
  71.0 29.8 %all-to-all-start.3 = ((bf16[128,16,256]{0,2,1:T(8,128)(2,1)}), bf16[128,16,256]{0,2,1:T(8,128)(2,1)S(1)}, u32[]{:S(2)}, u32[]{:S(2)}) async-start(bf16[128,16,256]{0,2,1:T(8,128)(2,1)} %bitcast.22), calls=%async_computation.3 | async-start | bytes 2097152 | tf_op jit(solution)/shard_map/all_to_all | solution.py:109
  121.7 7.5 %slice-start = ((s8[6291456]{0:T(1024)(128)(4,1)}), s8[4194304]{0:T(1024)(128)(4,1)S(1)}, s32[]{:S(2)}) async-start(s8[6291456]{0:T(1024)(128)(4,1)} %bitcast.140), calls=%async_computation.8 | async-start | bytes 8388608 | tf_op jit(solution)/shard_map/while
  125.6 3.6 %slice-start.1 = ((s8[6291456]{0:T(1024)(128)(4,1)}), s8[2097152]{0:T(1024)(128)(4,1)S(1)}, s32[]{:S(2)}) async-start(s8[6291456]{0:T(1024)(128)(4,1)} %bitcast.140), calls=%async_computation.9 | async-start | bytes 4194304 | tf_op jit(solution)/shard_map/while
  158.9 7.5 %slice-start = ((s8[6291456]{0:T(1024)(128)(4,1)}), s8[4194304]{0:T(1024)(128)(4,1)S(1)}, s32[]{:S(2)}) async-start(s8[6291456]{0:T(1024)(128)(4,1)} %bitcast.140), calls=%async_computation.8 | async-start | bytes 8388608 | tf_op jit(solution)/shard_map/while
  162.8 3.6 %slice-start.1 = ((s8[6291456]{0:T(1024)(128)(4,1)}), s8[2097152]{0:T(1024)(128)(4,1)S(1)}, s32[]{:S(2)}) async-start(s8[6291456]{0:T(1024)(128)(4,1)} %bitcast.140), calls=%async_computation.9 | async-start | bytes 4194304 | tf_op jit(solution)/shard_map/while
  167.5 1.7 copy-start.1
  196.1 7.5 %slice-start = ((s8[6291456]{0:T(1024)(128)(4,1)}), s8[4194304]{0:T(1024)(128)(4,1)S(1)}, s32[]{:S(2)}) async-start(s8[6291456]{0:T(1024)(128)(4,1)} %bitcast.140), calls=%async_computation.8 | async-start | bytes 8388608 | tf_op jit(solution)/shard_map/while
  200.0 3.6 %slice-start.1 = ((s8[6291456]{0:T(1024)(128)(4,1)}), s8[2097152]{0:T(1024)(128)(4,1)S(1)}, s32[]{:S(2)}) async-start(s8[6291456]{0:T(1024)(128)(4,1)} %bitcast.140), calls=%async_computation.9 | async-start | bytes 4194304 | tf_op jit(solution)/shard_map/while
  233.3 7.5 %slice-start = ((s8[6291456]{0:T(1024)(128)(4,1)}), s8[4194304]{0:T(1024)(128)(4,1)S(1)}, s32[]{:S(2)}) async-start(s8[6291456]{0:T(1024)(128)(4,1)} %bitcast.140), calls=%async_computation.8 | async-start | bytes 8388608 | tf_op jit(solution)/shard_map/while
  237.1 3.6 %slice-start.1 = ((s8[6291456]{0:T(1024)(128)(4,1)}), s8[2097152]{0:T(1024)(128)(4,1)S(1)}, s32[]{:S(2)}) async-start(s8[6291456]{0:T(1024)(128)(4,1)} %bitcast.140), calls=%async_computation.9 | async-start | bytes 4194304 | tf_op jit(solution)/shard_map/while
  241.8 1.7 copy-start.1
  253.0 27.6 %copy-start.5 = (bf16[4,512,2,128]{3,2,1,0:T(2,128)(2,1)S(1)}, bf16[4,512,2,128]{3,2,1,0:T(2,128)(2,1)}, u32[]{:S(2)}) copy-start(bf16[4,512,2,128]{3,2,1,0:T(2,128)(2,1)} %get-tuple-element.146) | copy-start | bytes 3145732
  255.1 21.4 %all-to-all-start.6 = ((bf16[16,128,128]{2,1,0:T(8,128)(2,1)}), bf16[16,128,128]{2,1,0:T(8,128)(2,1)S(1)}, u32[]{:S(2)}, u32[]{:S(2)}) async-start(bf16[16,128,128]{2,1,0:T(8,128)(2,1)} %bitcast.28), calls=%async_computation.6 | async-start | bytes 1048576 | tf_op jit(solution)/shard_map/all_to_all | solution.py:138
  262.0 37.1 %copy-start.6 = (bf16[4,512,2,128]{3,2,1,0:T(2,128)(2,1)S(1)}, bf16[4,512,2,128]{3,2,1,0:T(2,128)(2,1)}, u32[]{:S(2)}) copy-start(bf16[4,512,2,128]{3,2,1,0:T(2,128)(2,1)} %get-tuple-element.145) | copy-start | bytes 3145732
  276.5 18.6 %all-to-all-start.7 = ((bf16[16,128,128]{2,1,0:T(8,128)(2,1)}), bf16[16,128,128]{2,1,0:T(8,128)(2,1)S(1)}, u32[]{:S(2)}, u32[]{:S(2)}) async-start(bf16[16,128,128]{2,1,0:T(8,128)(2,1)} %bitcast.32), calls=%async_computation.7 | async-start | bytes 1048576 | tf_op jit(solution)/shard_map/all_to_all | solution.py:141
  295.1 27.0 %all-to-all-start.5 = ((bf16[16,128,256]{2,1,0:T(8,128)(2,1)}), bf16[16,128,256]{2,1,0:T(8,128)(2,1)S(1)}, u32[]{:S(2)}, u32[]{:S(2)}) async-start(bf16[16,128,256]{2,1,0:T(8,128)(2,1)} %all_to_all.118), calls=%async_computation.5 | async-start | bytes 2097152 | tf_op jit(solution)/shard_map/all_to_all | solution.py:129
  322.1 29.8 %all-to-all-start.4 = ((bf16[16,128,256]{2,1,0:T(8,128)(2,1)}), bf16[16,128,256]{2,1,0:T(8,128)(2,1)S(1)}, u32[]{:S(2)}, u32[]{:S(2)}) async-start(bf16[16,128,256]{2,1,0:T(8,128)(2,1)} %all_to_all.114), calls=%async_computation.4 | async-start | bytes 2097152 | tf_op jit(solution)/shard_map/all_to_all | solution.py:122
  (3 other events, 4.4 us)
where the time goes:
time: 357 us; the launch traced here: 354 us
  waiting for transfers between devices  131 us (37%)
  local copies, waits for them, and re-layouts  70.9 us (20%)
  matrix products  61.6 us (17%)
  starting transfers between devices  44.5 us (12%)
  other arithmetic  24.4 us (7%)
  loops' own time  21.2 us (6%)
    sub x4, matrix products, block_pass(): expd = jnp.where(allowed[None], jnp.exp(scores - top_score), 0.0)  27.8 us
    all_to_all x1, waiting for transfers between devices, body(): lax.all_to_all(query_rows, 'context', split_axis=1, concat_axis=0, tiled=...  21.6 us
    all_to_all x1, waiting for transfers between devices, body(): lax.all_to_all(q_grad.reshape(length, heads_here * width), 'context', spl...  21.4 us
    another operation x1, loops' own time, head_pass(): (k_acc, v_acc), (attended, q_grad) = lax.scan(step, (empty, empty), starts)  21.2 us
    all_to_all x1, waiting for transfers between devices, body(): lax.all_to_all(attended.reshape(length, heads_here * width), 'context', s...  19 us
    all_to_all x1, waiting for transfers between devices, body(): lax.all_to_all(grad_out, 'context', split_axis=1, concat_axis=0, tiled=True)  16.7 us
    convert_element_type x4, other arithmetic, block_pass(): weights = probs.astype(jnp.bfloat16)  15.4 us
    dynamic_update_slice x4, local copies, waits for them, and re-layouts, step(): lax.dynamic_update_slice_in_dim(v_acc, lax.dynamic_slice_in_dim(v_acc, st...  13.5 us
  transfers between devices with their start and end apart: 8, of which 8 were waited for; matrix products, arithmetic and copies ran while one was open for 5% of the time, Pallas kernels for 0%

commit v1 on v0

v1 whole, which is shorter than its diff:
```python
import functools
import math

import jax
import jax.numpy as jnp
from jax import lax
from jax.experimental import pallas as pl
from jax.experimental.pallas import tpu as pltpu
from jax.sharding import PartitionSpec as P

HEAD_DIM = 128
MASKED = -1e30
CHUNKS = 5
NT = (((1,), (1,)), ((), ()))
NN = (((1,), (0,)), ((), ()))
BF = jnp.bfloat16
F32 = jnp.float32
VMEM = pl.BlockSpec(memory_space=pltpu.VMEM)
ANYWHERE = pl.BlockSpec(memory_space=pl.ANY)


def dot(a, b, dims=NN):
    return lax.dot_general(a, b, dims, preferred_element_type=F32)


def in_hbm(x):
    return pltpu.with_memory_space_constraint(x, pltpu.HBM)


def position():
    me = lax.axis_index("context").astype(jnp.int32)
    return lax.rem(me, 2), lax.div(me, 2)


def run(moves, sems):
    copies = [pltpu.make_async_copy(a, b, sems.at[i]) for i, (a, b) in enumerate(moves)]
    for copy in copies:
        copy.start()
    return copies


def share_kernel(k, v, q, g, own, theirs, sent, sems):
    core, _ = position()
    moves = []
    for out, owner, left, right in ((theirs, 1 - core, k, v), (own, core, k, v), (sent, 1 - core, q, g)):
        width = out.shape[1] // 2
        cols = pl.ds(pl.multiple_of(owner * width, width), width)
        moves += [
            (left.at[:, cols], out.at[:, pl.ds(0, width)]),
            (right.at[:, cols], out.at[:, pl.ds(width, width)]),
        ]
    for copy in run(moves, sems):
        copy.wait()


def payload_kernel(heads, kv_own, kv_oth, sent_in, sent, *kv):
    core, _ = position()
    rows = kv_own.shape[0]
    width = HEAD_DIM
    for block, part in ((core, kv_own), (1 - core, kv_oth)):
        at = pl.ds(pl.multiple_of(block * rows, rows), rows)
        for s, out in enumerate(kv):
            out[at, :width] = part[:, s * width:(s + 1) * width]
            out[at, width:] = part[:, (heads + s) * width:(heads + s + 1) * width]


def stage_kernel(
    heads, bounds_in, q_all, g_all, other, q_st, g_st, q_t, g_t, k_seg, q_own, g_own, bounds, sems
):
    core, chip = position()
    rows = q_own.shape[0]
    width = HEAD_DIM
    units = q_t.shape[0] // heads
    pairs = units // 2
    two = 2 * rows
    share = q_own.shape[1]
    own = pl.ds(pl.multiple_of(core * share, share), share)
    copies = run([(bounds_in, bounds), (q_all.at[:, own], q_own), (g_all.at[:, own], g_own)], sems)
    copies[0].wait()

    def segment(pos):
        seg = jnp.zeros(pos.shape, jnp.int32)
        for b in range(1, bounds.shape[0] - 1):
            seg += (pos >= bounds[b]).astype(jnp.int32)
        return seg

    sub = lax.broadcasted_iota(jnp.int32, (rows, width), 0)
    seg_lane = lax.broadcasted_iota(jnp.int32, (rows, width), 1)
    for b in range(2 * CHUNKS):
        pos = (2 * (chip + 1 - CHUNKS) + b) * rows + sub
        seg = jnp.where(pos >= 0, segment(pos), width - 1)
        k_seg[b * rows:(b + 1) * rows] = (seg_lane == seg).astype(BF)
    for copy in copies[1:]:
        copy.wait()
    for s in range(heads):
        for p in range(pairs):
            for i in range(2):
                col = ((s * pairs + p) * 2 + i) * width
                cols = slice(col, col + width)
                for block, q, g in ((core, q_own, g_own), (1 - core, other, other.at[:, pl.ds(share, share)])):
                    at = pl.multiple_of((s * units + block * pairs + p) * two + i * rows, rows)
                    q_st[pl.ds(at, rows)] = q[:, cols]
                    g_st[pl.ds(at, rows)] = g[:, cols]
    lane = lax.broadcasted_iota(jnp.int32, (width, two), 1)
    lane = jnp.where(lane >= rows, lane - rows, lane)
    row = lax.broadcasted_iota(jnp.int32, (width, two), 0)
    for block in range(2):
        away = jnp.where(row == segment((2 * chip + block) * rows + lane), 0.0, MASKED).astype(BF)
        for s in range(heads):
            for p in range(pairs):
                u = s * units + block * pairs + p
                q_t[u, :width] = q_st[u * two:(u + 1) * two].T
                q_t[u, width:] = away
                g_t[u] = g_st[u * two:(u + 1) * two].T


def attention_kernel(
    slot, heads, q_st, g_st, q_t, g_t, k_seg, kv4, kv_edge, kv2, kv_middle, kv0, *refs
):
    o_all, dq_all, sent, d4, d_edge, d2, d_middle, d0 = refs[-22:-14]
    (k_aug, v_win, k_t, v_t, qs_st, gs_st, s_scr, p_scr, d_scr, dk_acc, dv_acc, o_scr, dq_scr,
     sems) = refs[-14:]
    width = HEAD_DIM
    scale = width ** -0.5
    core, chip = position()
    units = q_t.shape[0] // heads
    pairs = units // 2
    two = q_t.shape[2]
    rows = two // 2
    wide = 2 * pairs * width
    blocks = 2 * CHUNKS - 1
    span = blocks * rows
    base = slot * units
    even = lax.rem(chip, 2) == 0
    edge = pl.multiple_of(jnp.where(even, two, 3 * two), two)
    middle = pl.multiple_of(jnp.where(even, 3 * two, two), two)
    places = [pl.ds(at, two) for at in (0, edge, 2 * two, middle, 4 * two)]

    k_aug[:, width:] = k_seg[...]
    for at, kv in zip(places, (kv4, kv_edge, kv2, kv_middle, kv0)):
        k_aug[at, :width] = kv[:, :width]
        v_win[at] = kv[:, width:]
        k_t[:, at] = kv[:, :width].T
        v_t[:width, at] = kv[:, width:].T

    v_t[width:] = jnp.ones((v_t.shape[0] - width, v_t.shape[1]), BF)

    lane = lax.broadcasted_iota(jnp.int32, (rows, two), 1)
    causal = lax.broadcasted_iota(jnp.int32, (rows, two), 0) <= jnp.where(lane >= rows, lane - rows, lane)

    def window(u):
        first = (u // pairs) * rows
        return first, slice(first, first + span)

    def columns(u):
        return slice(u * two, (u + 1) * two)

    def fold(x, op):
        return op(x.reshape(x.shape[0] // 8, 8, x.shape[1]), axis=0)

    def scores(u, b, top):
        first, _ = window(u)
        s = dot(k_aug[first + b * rows:first + (b + 3) * rows], q_t[base + u])
        for i in range(3):
            part = s[i * rows:(i + 1) * rows]
            if b + i == blocks - 1:
                part = jnp.where(causal, part, MASKED)
            s_scr[u % 2, (b + i) * rows:(b + i + 1) * rows] = part
            top = jnp.maximum(top, fold(part, jnp.max))
        return top

    def weights(u, b, peak):
        first, _ = window(u)
        e = jnp.exp2((s_scr[u % 2, b * rows:(b + 1) * rows] - peak) * (scale * math.log2(math.e)))
        p_scr[first + b * rows:first + (b + 1) * rows, columns(u)] = e.astype(BF)

    def score_grads(u, b, inner):
        first, _ = window(u)
        keys = slice(first + b * rows, first + (b + 3) * rows)
        dp = dot(v_win[keys], g_t[base + u])
        d_scr[keys, columns(u)] = p_scr[keys, columns(u)] * (dp - inner).astype(BF)

    def store(x, out, u):
        block, p = u // pairs, u % pairs
        x = x.T
        for i in range(2):
            out[block * rows:(block + 1) * rows, (2 * p + i) * width:(2 * p + i + 1) * width] = (
                x[i * rows:(i + 1) * rows]
            )

    def query_grad(u, inv):
        _, keys = window(u)
        store((dot(k_t[:, keys], d_scr[keys, columns(u)]) * (inv * scale)).astype(BF), dq_scr, u)

    half = pairs * two
    part = (3 * pairs // 2) * two
    sums = ((p_scr, gs_st, dv_acc), (d_scr, qs_st, dk_acc))
    first_group = [(b * rows, *one) for b in range(0, blocks, 3) for one in sums]
    second_group = [(rows + b * rows, *one) for b in range(0, blocks, 3) for one in sums]
    for _, _, acc in sums:
        acc[span:] = jnp.zeros((rows, width), F32)

    def key_grads(u):
        if u > pairs and first_group:
            at, left, right, acc = first_group.pop(0)
            at = slice(at, at + 3 * rows)
            acc[at] = dot(left[at, :half], right[:half])
        elif u > 3 * pairs // 2 and second_group:
            at, left, right, acc = second_group.pop(0)
            at = slice(at, at + 3 * rows)
            acc[at] += dot(left[at, half:part], right[half:part])

    def one_unit(u, peak, inv_before, more):
        _, keys = window(u)
        top = jnp.full((8, two), MASKED, F32)
        for b in range(0, blocks, 3):
            if more:
                top = scores(u + 1, b, top)
            key_grads(u)
            for i in range(3):
                weights(u, b + i, peak)
        peak = jnp.max(top, axis=0, keepdims=True)
        o = dot(v_t[:, keys], p_scr[keys, columns(u)])
        if u > 0:
            query_grad(u - 1, inv_before)
        inv = 1.0 / o[width:width + 1]
        o = (o[:width] * inv).astype(BF)
        store(o, o_scr, u)
        inner = jnp.sum(g_t[base + u].astype(F32) * o.astype(F32), axis=0, keepdims=True)
        for b in range(0, blocks, 3):
            key_grads(u)
            score_grads(u, b, inner)
        column = jnp.broadcast_to(inv, (8, two)).T[:, :1]
        here, there = slice(u * two, (u + 1) * two), slice((base + u) * two, (base + u + 1) * two)
        qs_st[here] = (q_st[there].astype(F32) * column).astype(BF)
        gs_st[here] = (g_st[there].astype(F32) * column).astype(BF)
        return peak, inv

    top = jnp.full((8, two), MASKED, F32)
    for b in range(0, blocks, 3):
        top = scores(0, b, top)
    peak, inv = jnp.max(top, axis=0, keepdims=True), None
    for u in range(units):
        peak, inv = one_unit(u, peak, inv, u + 1 < units)
    query_grad(units - 1, inv)

    mine = pl.ds(pl.multiple_of(core * rows, rows), rows)
    other = pl.ds(pl.multiple_of((1 - core) * rows, rows), rows)
    cols = pl.ds(pl.multiple_of((core * heads + slot) * wide, wide), wide)
    moves = [
        (o_scr.at[other], sent.at[:, pl.ds(0, wide)]),
        (dq_scr.at[other], sent.at[:, pl.ds(wide, wide)]),
        (o_scr.at[mine], o_all.at[:, cols]),
        (dq_scr.at[mine], dq_all.at[:, cols]),
    ]
    copies = run(moves, sems)

    for left, right, acc, factor, col in (
        (d_scr, qs_st, dk_acc, scale, 0), (p_scr, gs_st, dv_acc, 1.0, width)
    ):
        cols = slice(col, col + width)

        def total(keys):
            return factor * (acc[keys] + dot(left[keys, part:], right[part:]))

        d4[:rows, cols] = (factor * acc[:rows]).astype(d4.dtype)
        d4[rows:, cols] = total(slice(rows, two)).astype(d4.dtype)
        for at, out in zip(places[1:], (d_edge, d2, d_middle, d0)):
            out[:, cols] = total(at).astype(out.dtype)
    for copy in copies:
        copy.wait()


def place_kernel(heads, o_in, dq_in, *refs):
    backs = refs[:heads]
    mine, theirs, o, dq, dk, dv, sems = refs[heads:]
    core, _ = position()
    wide = backs[0].shape[1] // 2
    half = mine.shape[1] // 2
    moves = []
    for s, back in enumerate(backs):
        cols = pl.ds(pl.multiple_of(((1 - core) * heads + s) * wide, wide), wide)
        moves += [(back.at[:, pl.ds(0, wide)], o.at[:, cols]), (back.at[:, pl.ds(wide, wide)], dq.at[:, cols])]
    for part, owner in ((mine, core), (theirs, 1 - core)):
        cols = pl.ds(pl.multiple_of(owner * half, half), half)
        moves += [(part.at[:, pl.ds(0, half)], dk.at[:, cols]), (part.at[:, pl.ds(half, half)], dv.at[:, cols])]
    for copy in run(moves, sems):
        copy.wait()


def shares(k, v, q, g):
    return pl.pallas_call(
        share_kernel,
        in_specs=[ANYWHERE] * 4,
        out_specs=[VMEM] * 3,
        out_shape=[jax.ShapeDtypeStruct(x.shape, BF) for x in (k, v, q)],
        scratch_shapes=[pltpu.SemaphoreType.DMA((6,))],
        compiler_params=pltpu.CompilerParams(vmem_limit_bytes=4 * 1024 * 1024),
        name="share",
    )(in_hbm(k), in_hbm(v), in_hbm(q), in_hbm(g))


def payloads(kv_own, kv_oth, sent, heads):
    kv = jax.ShapeDtypeStruct((2 * kv_own.shape[0], 2 * HEAD_DIM), BF)
    return pl.pallas_call(
        functools.partial(payload_kernel, heads),
        in_specs=[VMEM] * 2 + [ANYWHERE],
        out_specs=[ANYWHERE] + [VMEM] * heads,
        out_shape=[jax.ShapeDtypeStruct(sent.shape, BF)] + [kv] * heads,
        input_output_aliases={2: 0},
        compiler_params=pltpu.CompilerParams(vmem_limit_bytes=4 * 1024 * 1024),
        name="payload",
    )(kv_own, kv_oth, sent)


def staged(bounds, q, g, other, heads):
    rows = q.shape[0]
    width = HEAD_DIM
    units = q.shape[1] // (2 * width)
    return pl.pallas_call(
        functools.partial(stage_kernel, heads),
        in_specs=[ANYWHERE, ANYWHERE, ANYWHERE, VMEM],
        out_specs=[VMEM] * 5,
        out_shape=[
            jax.ShapeDtypeStruct((units * 2 * rows, width), BF),
            jax.ShapeDtypeStruct((units * 2 * rows, width), BF),
            jax.ShapeDtypeStruct((units, 2 * width, 2 * rows), BF),
            jax.ShapeDtypeStruct((units, width, 2 * rows), BF),
            jax.ShapeDtypeStruct((2 * CHUNKS * rows, width), BF),
        ],
        scratch_shapes=[
            pltpu.VMEM((rows, q.shape[1] // 2), BF),
            pltpu.VMEM((rows, q.shape[1] // 2), BF),
            pltpu.SMEM(bounds.shape, jnp.int32),
            pltpu.SemaphoreType.DMA((3,)),
        ],
        compiler_params=pltpu.CompilerParams(vmem_limit_bytes=16 * 1024 * 1024),
        cost_estimate=pl.CostEstimate(flops=0, bytes_accessed=8 * q.size, transcendentals=0),
        name="stage",
    )(in_hbm(bounds), in_hbm(q), in_hbm(g), other)


def head_attention(slot, heads, q, stage, window, so_far):
    rows = q.shape[0]
    width = HEAD_DIM
    two = 2 * rows
    units = stage[2].shape[0] // heads
    wide = q.shape[1] // (2 * heads)
    span = CHUNKS * two
    short = span - rows
    chunk = window[0].shape
    return pl.pallas_call(
        functools.partial(attention_kernel, slot, heads),
        in_specs=[VMEM] * 10 + [ANYWHERE] * len(so_far),
        out_specs=[ANYWHERE] * 3 + [VMEM] * 5,
        scratch_shapes=[
            pltpu.VMEM((span, 2 * width), BF),
            pltpu.VMEM((span, width), BF),
            pltpu.VMEM((width, span), BF),
            pltpu.VMEM((width + 16, span), BF),
            pltpu.VMEM((units * two, width), BF),
            pltpu.VMEM((units * two, width), BF),
            pltpu.VMEM((2, short, two), F32),
            pltpu.VMEM((span, units * two), BF),
            pltpu.VMEM((span, units * two), BF),
            pltpu.VMEM((span, width), F32),
            pltpu.VMEM((span, width), F32),
            pltpu.VMEM((two, wide), BF),
            pltpu.VMEM((two, wide), BF),
            pltpu.SemaphoreType.DMA((4,)),
        ],
        out_shape=[
            jax.ShapeDtypeStruct(q.shape, BF),
            jax.ShapeDtypeStruct(q.shape, BF),
            jax.ShapeDtypeStruct((rows, 2 * wide), BF),
        ] + [jax.ShapeDtypeStruct(chunk, t) for t in (BF, BF, F32, BF, F32)],
        input_output_aliases={10 + i: i for i in range(len(so_far))},
        compiler_params=pltpu.CompilerParams(vmem_limit_bytes=36 * 1024 * 1024),
        cost_estimate=pl.CostEstimate(
            flops=20 * rows * span * wide,
            bytes_accessed=24 * rows * wide,
            transcendentals=2 * rows * span * wide // width,
        ),
        name="attention%d" % slot,
    )(*stage, *window, *so_far)


def place(o, dq, backs, mine, theirs):
    heads = len(backs)
    return pl.pallas_call(
        functools.partial(place_kernel, heads),
        in_specs=[ANYWHERE] * (4 + heads),
        out_specs=[ANYWHERE] * 4,
        scratch_shapes=[pltpu.SemaphoreType.DMA((2 * heads + 4,))],
        out_shape=[
            jax.ShapeDtypeStruct(o.shape, BF),
            jax.ShapeDtypeStruct(dq.shape, BF),
            jax.ShapeDtypeStruct(mine.shape, BF),
            jax.ShapeDtypeStruct(mine.shape, BF),
        ],
        input_output_aliases={0: 0, 1: 1},
        compiler_params=pltpu.CompilerParams(vmem_limit_bytes=1024 * 1024),
        name="place",
    )(o, dq, *backs, mine, theirs)


def body(query_rows, key_rows, value_rows, grad_out, doc_bounds):
    core, chip = position()
    n = lax.axis_size("context")
    even = lax.rem(chip, 2) == 0
    rows = query_rows.shape[0]
    width = HEAD_DIM
    heads = key_rows.shape[1] // (2 * width)

    def shift(x, by):
        return lax.ppermute(x, "context", [(i, (i + by) % n) for i in range(n)])

    def swap(x):
        return lax.ppermute(x, "context", [(i, i ^ 1) for i in range(n)])

    def across(x):
        return lax.ppermute(x, "context", [(i, i ^ 2) for i in range(n)])

    kv_own, kv_sent, sent = shares(key_rows, value_rows, query_rows, grad_out)
    sent, *kv = payloads(kv_own, swap(kv_sent), sent, heads)
    stage = staged(doc_bounds, query_rows, grad_out, swap(sent), heads)

    o, dq, outs = None, None, []
    for s in range(heads):
        back2 = shift(kv[s], 4)
        edge = shift(jnp.where(even, kv[s], back2), 2)
        middle = across(back2)
        back4 = shift(back2, 4)
        o, dq, *rest = head_attention(
            s, heads, query_rows, stage, (back4, edge, back2, middle, kv[s]), () if s == 0 else (o, dq)
        )
        outs.append(rest)
    grads, backs = [], []
    for sent, d4, d_edge, d2, d_middle, d0 in outs:
        from_edge = shift(d_edge, -2)
        from_four = shift(d4, -4)
        from_middle = across(d_middle)
        d2 = jnp.where(even, d2, d2 + from_edge)
        from_two = shift((d2 + from_middle + from_four).astype(BF), -4)
        total = jnp.where(even, d0 + from_edge, d0) + from_two.astype(F32)
        grads.append(total.astype(BF))
        backs.append(swap(sent))
    total = jnp.concatenate([g[:, :width] for g in grads] + [g[:, width:] for g in grads], axis=1)
    mine = lax.dynamic_slice_in_dim(total, core * rows, rows, 0)
    theirs = swap(lax.dynamic_slice_in_dim(total, (1 - core) * rows, rows, 0))
    return place(o, dq, backs, mine, theirs)


def solution(mesh):
    rows = P(("dp", "context"), None)
    return jax.shard_map(
        body,
        mesh=mesh,
        in_specs=(rows, rows, rows, rows, P("dp")),
        out_specs=(rows, rows, rows, rows),
        check_vma=False,
    )
```

time: 357 us -> 64.9 us (0.18)
  waiting for transfers between devices: 131 us -> 12.7 us
  local copies, waits for them, and re-layouts: 70.9 us -> 0.05 us
  matrix products: 61.6 us -> 0 us
  Pallas kernels: 0 us -> 24.1 us
  other arithmetic: 24.4 us -> 0.3 us
  loops' own time: 21.2 us -> 0 us
  starting transfers between devices: 44.5 us -> 26.2 us
    all_to_all x8 -> x0, waiting for transfers between devices: 131 us -> none  [the longest x1 21.6 us: body(): lax.all_to_all(query_rows, 'context', split_axis=1, concat_axis=0, tiled=...]
    all_to_all x8 -> x0, starting transfers between devices: 44.5 us -> none  [the longest x1 7.36 us: body(): lax.all_to_all(v_slots, 'context', split_axis=1, concat_axis=0, tiled=True)]
    dot_general x20 -> x0, matrix products: 33.7 us -> none  [the longest x4 8.47 us: block_pass(): jnp.einsum('hqk,qhd->kd', weights, o_grad, preferred_element_type=jnp.flo...]
    dynamic_update_slice x16 -> x0, local copies, waits for them, and re-layouts: 32.6 us -> none  [the longest x4 13.5 us: step(): lax.dynamic_update_slice_in_dim(v_acc, lax.dynamic_slice_in_dim(v_acc, st...]
    sub x4 -> x0, matrix products: 27.8 us -> none  [block_pass(): expd = jnp.where(allowed[None], jnp.exp(scores - top_score), 0.0)]
    ppermute x0 -> x21, starting transfers between devices: none -> 26.2 us  [the longest x12 20.1 us: shift(): return lax.ppermute(x, 'context', [(i, (i + by) % n) for i in range(n)])]
    pallas_call x0 -> x6, Pallas kernels: none -> 24.1 us  [the longest x2 19.2 us: head_attention(): pl.pallas_call(functools.partial(attention_kernel, slot, heads), in_specs...]
    another operation x1 -> x0, loops' own time: 21.2 us -> none  [head_pass(): (k_acc, v_acc), (attended, q_grad) = lax.scan(step, (empty, empty), starts)]
  transfers between devices with their start and end apart: 8 -> 21, of which waited for: 8 -> 7; matrix products, arithmetic and copies ran while one was open for 5% -> 1% of each run, Pallas kernels for 0% -> 33%
where the time goes in v1:
time: 64.9 us; the launch traced here: 64.3 us
  starting transfers between devices  26.2 us (40%)
  Pallas kernels  24.1 us (37%)
  waiting for transfers between devices  12.7 us (20%)
  between operations  0.91 us (1%)
    ppermute x12, starting transfers between devices, shift(): return lax.ppermute(x, 'context', [(i, (i + by) % n) for i in range(n)])  20.1 us
    pallas_call x2, Pallas kernels, head_attention(): pl.pallas_call(functools.partial(attention_kernel, slot, heads), in_specs...  19.2 us
    ppermute x12, waiting for transfers between devices, shift(): return lax.ppermute(x, 'context', [(i, (i + by) % n) for i in range(n)])  10.4 us
    ppermute x4, starting transfers between devices, across(): return lax.ppermute(x, 'context', [(i, i ^ 2) for i in range(n)])  4.62 us
    ppermute x5, waiting for transfers between devices, swap(): return lax.ppermute(x, 'context', [(i, i ^ 1) for i in range(n)])  2.33 us
    pallas_call x1, Pallas kernels, staged(): pl.pallas_call(functools.partial(stage_kernel, heads), in_specs=[ANYWHERE...  2.29 us
    ppermute x5, starting transfers between devices, swap(): return lax.ppermute(x, 'context', [(i, i ^ 1) for i in range(n)])  1.52 us
    pallas_call x1, Pallas kernels, shares(): pl.pallas_call(share_kernel, in_specs=[ANYWHERE] * 4, out_specs=[VMEM] *...  1.41 us
  transfers between devices with their start and end apart: 21, of which 7 were waited for; matrix products, arithmetic and copies ran while one was open for 1% of the time, Pallas kernels for 33%

profile of v1, /device:TPU:0, one launch (start us, length us, event | category | flops | bytes accessed | tf_op | source)
XLA Modules:
  0.0 64.3 jit_solution(17020297980940377951)
XLA Ops:
  0.6 1.4 %share.1 = (bf16[128,512]{1,0:T(8,128)(2,1)S(1)}, bf16[128,512]{1,0:T(8,128)(2,1)S(1)}, bf16[128,4096]{1,0:T(8,128)(2,1)S(1)}) custom-call(bf16[128,512]{1,0:T(8,128)(2,1)} %k.1, bf16[128,512]{1,0:T(8,128)(2,1)} %v.1, bf16[128,4096]{1,0:T(8,128)(2,1)} %q_all.1, bf16[128,4096]{1,0:T(8,128)(2,1)} %g_all.1), custom_call_target="tpu_custom_call" | custom-call | tf_op jit(solution)/shard_map/share/pallas_call | solution.py:292
  2.6 1.0 %collective-permute-done.kv_oth = bf16[128,512]{1,0:T(8,128)(2,1)S(1)} collective-permute-done((bf16[128,512]{1,0:T(8,128)(2,1)S(1)}, bf16[128,512]{1,0:T(8,128)(2,1)S(1)}, u32[]{:S(2)}, u32[]{:S(2)}) %collective-permute-start) | collective-permute-done | bytes 131104 | tf_op jit(solution)/shard_map/ppermute | solution.py:419
  4.0 2.7 %collective-permute-start.6 = (bf16[256,256]{1,0:T(8,128)(2,1)S(1)}, bf16[256,256]{1,0:T(8,128)(2,1)S(1)}, u32[]{:S(2)}, u32[]{:S(2)}) collective-permute-start(bf16[256,256]{1,0:T(8,128)(2,1)S(1)} %get-tuple-element.41.kv0), channel_id=1, source_target_pairs={{0,4},{1,5},{2,6},{3,7},{4,8},{5,9},{6,10},{7,11},{8,12},{9,13},{1... | collective-permute-start | bytes 393224 | tf_op jit(solution)/shard_map/ppermute | solution.py:416
  6.8 1.6 %collective-permute-start.2 = (bf16[256,256]{1,0:T(8,128)(2,1)S(1)}, bf16[256,256]{1,0:T(8,128)(2,1)S(1)}, u32[]{:S(2)}, u32[]{:S(2)}) collective-permute-start(bf16[256,256]{1,0:T(8,128)(2,1)S(1)} %get-tuple-element.40.kv0), channel_id=1, source_target_pairs={{0,4},{1,5},{2,6},{3,7},{4,8},{5,9},{6,10},{7,11},{8,12},{9,13},{1... | collective-permute-start | bytes 393224 | tf_op jit(solution)/shard_map/ppermute | solution.py:416
  8.3 4.8 %collective-permute-done.6.kv2 = bf16[256,256]{1,0:T(8,128)(2,1)S(1)} collective-permute-done((bf16[256,256]{1,0:T(8,128)(2,1)S(1)}, bf16[256,256]{1,0:T(8,128)(2,1)S(1)}, u32[]{:S(2)}, u32[]{:S(2)}) %collective-permute-start.6) | collective-permute-done | bytes 131104 | tf_op jit(solution)/shard_map/ppermute | solution.py:416
  13.1 1.7 %collective-permute-start.8 = (bf16[256,256]{1,0:T(8,128)(2,1)S(1)}, bf16[256,256]{1,0:T(8,128)(2,1)S(1)}, u32[]{:S(2)}, u32[]{:S(2)}) collective-permute-start(bf16[256,256]{1,0:T(8,128)(2,1)S(1)} %broadcast_select_fusion), channel_id=1, source_target_pairs={{0,2},{1,3},{2,4},{3,5},{4,6},{5,7},{6,8},{7,9},{8,10},{9,11},{10,... | collective-permute-start | bytes 393224 | tf_op jit(solution)/shard_map/ppermute | solution.py:416
  14.9 1.3 %collective-permute-start.9 = (bf16[256,256]{1,0:T(8,128)(2,1)S(1)}, bf16[256,256]{1,0:T(8,128)(2,1)S(1)}, u32[]{:S(2)}, u32[]{:S(2)}) collective-permute-start(bf16[256,256]{1,0:T(8,128)(2,1)S(1)} %collective-permute-done.6.kv2), channel_id=1, source_target_pairs={{0,2},{1,3},{2,0},{3,1},{4,6},{5,7},{6,4},{7,5},{8,10},{9,11},{10,... | collective-permute-start | bytes 393224 | tf_op jit(solution)/shard_map/ppermute | solution.py:422
  16.2 1.0 %collective-permute-start.4 = (bf16[256,256]{1,0:T(8,128)(2,1)S(1)}, bf16[256,256]{1,0:T(8,128)(2,1)S(1)}, u32[]{:S(2)}, u32[]{:S(2)}) collective-permute-start(bf16[256,256]{1,0:T(8,128)(2,1)S(1)} %broadcast_select_fusion.1), channel_id=1, source_target_pairs={{0,2},{1,3},{2,4},{3,5},{4,6},{5,7},{6,8},{7,9},{8,10},{9,11},{10,... | collective-permute-start | bytes 393224 | tf_op jit(solution)/shard_map/ppermute | solution.py:416
  17.2 1.2 %collective-permute-start.3 = (bf16[256,256]{1,0:T(8,128)(2,1)S(1)}, bf16[256,256]{1,0:T(8,128)(2,1)S(1)}, u32[]{:S(2)}, u32[]{:S(2)}) collective-permute-start(bf16[256,256]{1,0:T(8,128)(2,1)S(1)} %collective-permute-done.2.kv2), channel_id=1, source_target_pairs={{0,4},{1,5},{2,6},{3,7},{4,8},{5,9},{6,10},{7,11},{8,12},{9,13},{1... | collective-permute-start | bytes 393224 | tf_op jit(solution)/shard_map/ppermute | solution.py:416
  18.3 2.3 %stage.1 = (bf16[4096,128]{1,0:T(8,128)(2,1)S(1)}, bf16[4096,128]{1,0:T(8,128)(2,1)S(1)}, bf16[16,256,256]{2,1,0:T(8,128)(2,1)S(1)}, bf16[16,128,256]{2,1,0:T(8,128)(2,1)S(1)}, bf16[1280,128]{1,0:T(8,128)(2,1)S(1)}) custom-call(s32[5]{0:T(128)} %bounds_in.1, bf16[128,4096]{1,0:T(8,128)(2,1)} %q_all.1, bf16[128,4096]{1,0:T(8,128)(2,1)} %g_all.1, ...), custom_call_target="tpu_custom_call" | custom-call | bytes 4194304 | tf_op jit(solution)/shard_map/stage/pallas_call | solution.py:320
  20.6 1.7 %collective-permute-done.8.kv_edge = bf16[256,256]{1,0:T(8,128)(2,1)S(1)} collective-permute-done((bf16[256,256]{1,0:T(8,128)(2,1)S(1)}, bf16[256,256]{1,0:T(8,128)(2,1)S(1)}, u32[]{:S(2)}, u32[]{:S(2)}) %collective-permute-start.8) | collective-permute-done | bytes 131104 | tf_op jit(solution)/shard_map/ppermute | solution.py:416
  22.3 1.2 %collective-permute-start.5 = (bf16[256,256]{1,0:T(8,128)(2,1)S(1)}, bf16[256,256]{1,0:T(8,128)(2,1)S(1)}, u32[]{:S(2)}, u32[]{:S(2)}) collective-permute-start(bf16[256,256]{1,0:T(8,128)(2,1)S(1)} %collective-permute-done.2.kv2), channel_id=1, source_target_pairs={{0,2},{1,3},{2,0},{3,1},{4,6},{5,7},{6,4},{7,5},{8,10},{9,11},{10,... | collective-permute-start | bytes 393224 | tf_op jit(solution)/shard_map/ppermute | solution.py:422
  23.5 9.6 %attention0.1 = (bf16[128,4096]{1,0:T(8,128)(2,1)}, bf16[128,4096]{1,0:T(8,128)(2,1)}, bf16[128,2048]{1,0:T(8,128)(2,1)S(1)}, bf16[256,256]{1,0:T(8,128)(2,1)S(1...) custom-call(bf16[4096,128]{1,0:T(8,128)(2,1)S(1)} %get-tuple-element, ...), custom_call_target="tpu_custom_call" | custom-call | flops 3355443200 | bytes 3145728 | tf_op jit(solution)/shard_map/attention0/pallas_call | solution.py:352
  33.2 1.8 %collective-permute-start.12 = (bf16[256,256]{1,0:T(8,128)(2,1)S(1)}, bf16[256,256]{1,0:T(8,128)(2,1)S(1)}, u32[]{:S(2)}, u32[]{:S(2)}) collective-permute-start(bf16[256,256]{1,0:T(8,128)(2,1)S(1)} %get-tuple-element.49), channel_id=1, source_target_pairs={{0,14},{1,15},{2,0},{3,1},{4,2},{5,3},{6,4},{7,5},{8,6},{9,7},{10,... | collective-permute-start | bytes 393224 | tf_op jit(solution)/shard_map/ppermute | solution.py:416
  35.5 1.9 %collective-permute-start.14 = (bf16[256,256]{1,0:T(8,128)(2,1)S(1)}, bf16[256,256]{1,0:T(8,128)(2,1)S(1)}, u32[]{:S(2)}, u32[]{:S(2)}) collective-permute-start(bf16[256,256]{1,0:T(8,128)(2,1)S(1)} %get-tuple-element.52), channel_id=1, source_target_pairs={{0,12},{1,13},{2,14},{3,15},{4,0},{5,1},{6,2},{7,3},{8,4},{9,5},{1... | collective-permute-start | bytes 393224 | tf_op jit(solution)/shard_map/ppermute | solution.py:416
  37.4 9.6 %attention1.1 = (bf16[128,4096]{1,0:T(8,128)(2,1)}, bf16[128,4096]{1,0:T(8,128)(2,1)}, bf16[128,2048]{1,0:T(8,128)(2,1)S(1)}, bf16[256,256]{1,0:T(8,128)(2,1)S(1...) custom-call(bf16[4096,128]{1,0:T(8,128)(2,1)S(1)} %get-tuple-element, ...), custom_call_target="tpu_custom_call", output_to_operand_aliasing={{0}: (10, {}), {1}: (11, {})} | custom-call | flops 3355443200 | bytes 3145728 | tf_op jit(solution)/shard_map/attention1/pallas_call | solution.py:352
  47.5 1.6 %collective-permute-start.17 = (bf16[256,256]{1,0:T(8,128)(2,1)S(1)}, bf16[256,256]{1,0:T(8,128)(2,1)S(1)}, u32[]{:S(2)}, u32[]{:S(2)}) collective-permute-start(bf16[256,256]{1,0:T(8,128)(2,1)S(1)} %get-tuple-element.56), channel_id=1, source_target_pairs={{0,2},{1,3},{2,0},{3,1},{4,6},{5,7},{6,4},{7,5},{8,10},{9,11},{10,... | collective-permute-start | bytes 393224 | tf_op jit(solution)/shard_map/ppermute | solution.py:422
  49.1 1.8 %collective-permute-start.18 = (bf16[256,256]{1,0:T(8,128)(2,1)S(1)}, bf16[256,256]{1,0:T(8,128)(2,1)S(1)}, u32[]{:S(2)}, u32[]{:S(2)}) collective-permute-start(bf16[256,256]{1,0:T(8,128)(2,1)S(1)} %get-tuple-element.57), channel_id=1, source_target_pairs={{0,12},{1,13},{2,14},{3,15},{4,0},{5,1},{6,2},{7,3},{8,4},{9,5},{1... | collective-permute-start | bytes 393224 | tf_op jit(solution)/shard_map/ppermute | solution.py:416
  52.1 1.6 %collective-permute-start.15 = (bf16[256,256]{1,0:T(8,128)(2,1)S(1)}, bf16[256,256]{1,0:T(8,128)(2,1)S(1)}, u32[]{:S(2)}, u32[]{:S(2)}) collective-permute-start(bf16[256,256]{1,0:T(8,128)(2,1)S(1)} %fusion.4), channel_id=1, source_target_pairs={{0,12},{1,13},{2,14},{3,15},{4,0},{5,1},{6,2},{7,3},{8,4},{9,5},{1... | collective-permute-start | bytes 393224 | tf_op jit(solution)/shard_map/ppermute | solution.py:416
  53.6 0.9 %collective-permute-done.18 = bf16[256,256]{1,0:T(8,128)(2,1)S(1)} collective-permute-done((bf16[256,256]{1,0:T(8,128)(2,1)S(1)}, bf16[256,256]{1,0:T(8,128)(2,1)S(1)}, u32[]{:S(2)}, u32[]{:S(2)}) %collective-permute-start.18) | collective-permute-done | bytes 131104 | tf_op jit(solution)/shard_map/ppermute | solution.py:416
  54.6 4.3 %collective-permute-start.19 = (bf16[256,256]{1,0:T(8,128)(2,1)S(1)}, bf16[256,256]{1,0:T(8,128)(2,1)S(1)}, u32[]{:S(2)}, u32[]{:S(2)}) collective-permute-start(bf16[256,256]{1,0:T(8,128)(2,1)S(1)} %fusion.9), channel_id=1, source_target_pairs={{0,12},{1,13},{2,14},{3,15},{4,0},{5,1},{6,2},{7,3},{8,4},{9,5},{1... | collective-permute-start | bytes 393224 | tf_op jit(solution)/shard_map/ppermute | solution.py:416
  59.0 2.4 %collective-permute-done.19 = bf16[256,256]{1,0:T(8,128)(2,1)S(1)} collective-permute-done((bf16[256,256]{1,0:T(8,128)(2,1)S(1)}, bf16[256,256]{1,0:T(8,128)(2,1)S(1)}, u32[]{:S(2)}, u32[]{:S(2)}) %collective-permute-start.19) | collective-permute-done | bytes 131104 | tf_op jit(solution)/shard_map/ppermute | solution.py:416
  61.7 1.3 %collective-permute-done.20.refs_3_ = bf16[128,512]{1,0:T(8,128)(2,1)S(1)} collective-permute-done((bf16[128,512]{1,0:T(8,128)(2,1)S(1)}, bf16[128,512]{1,0:T(8,128)(2,1)S(1)}, u32[]{:S(2)}, u32[]{:S(2)}) %collective-permute-start.20) | collective-permute-done | bytes 131104 | tf_op jit(solution)/shard_map/ppermute | solution.py:419
  63.0 1.1 %place.1 = (bf16[128,4096]{1,0:T(8,128)(2,1)}, bf16[128,4096]{1,0:T(8,128)(2,1)}, bf16[128,512]{1,0:T(8,128)(2,1)}, bf16[128,512]{1,0:T(8,128)(2,1)}) custom-call(bf16[128,4096]{1,0:T(8,128)(2,1)} %get-tuple-element.44.o_in, bf16[128,4096]{1,0:T(8,128)(2,1)} %get-tuple-element.45.dq_in, ...), custom_call_target="tpu_custom_call", output_to_operand_aliasing={{0}: (0, {}), {1}: (1, {})} | custom-call | tf_op jit(solution)/shard_map/place/pallas_call | solution.py:390
  (34 shorter events, 3.5 us)
Async XLA Ops:
  2.0 1.5 %collective-permute-start = (bf16[128,512]{1,0:T(8,128)(2,1)S(1)}, bf16[128,512]{1,0:T(8,128)(2,1)S(1)}, u32[]{:S(2)}, u32[]{:S(2)}) collective-permute-start(bf16[128,512]{1,0:T(8,128)(2,1)S(1)} %get-tuple-element.32), channel_id=1, source_target_pairs={{0,1},{1,0},{2,3},{3,2},{4,5},{5,4},{6,7},{7,6},{8,9},{9,8},{10,11... | collective-permute-start | bytes 393224 | tf_op jit(solution)/shard_map/ppermute | solution.py:419
  3.6 13.6 %collective-permute-start.1 = (bf16[128,4096]{1,0:T(8,128)(2,1)S(1)}, bf16[128,4096]{1,0:T(8,128)(2,1)S(1)}, u32[]{:S(2)}, u32[]{:S(2)}) collective-permute-start(bf16[128,4096]{1,0:T(8,128)(2,1)S(1)} %get-tuple-element.34), channel_id=1, source_target_pairs={{0,1},{1,0},{2,3},{3,2},{4,5},{5,4},{6,7},{7,6},{8,9},{9,8},{10,11... | collective-permute-start | bytes 3145736 | tf_op jit(solution)/shard_map/ppermute | solution.py:419
  4.0 9.1 %collective-permute-start.6 = (bf16[256,256]{1,0:T(8,128)(2,1)S(1)}, bf16[256,256]{1,0:T(8,128)(2,1)S(1)}, u32[]{:S(2)}, u32[]{:S(2)}) collective-permute-start(bf16[256,256]{1,0:T(8,128)(2,1)S(1)} %get-tuple-element.41.kv0), channel_id=1, source_target_pairs={{0,4},{1,5},{2,6},{3,7},{4,8},{5,9},{6,10},{7,11},{8,12},{9,13},{1... | collective-permute-start | bytes 393224 | tf_op jit(solution)/shard_map/ppermute | solution.py:416
  6.8 9.4 %collective-permute-start.2 = (bf16[256,256]{1,0:T(8,128)(2,1)S(1)}, bf16[256,256]{1,0:T(8,128)(2,1)S(1)}, u32[]{:S(2)}, u32[]{:S(2)}) collective-permute-start(bf16[256,256]{1,0:T(8,128)(2,1)S(1)} %get-tuple-element.40.kv0), channel_id=1, source_target_pairs={{0,4},{1,5},{2,6},{3,7},{4,8},{5,9},{6,10},{7,11},{8,12},{9,13},{1... | collective-permute-start | bytes 393224 | tf_op jit(solution)/shard_map/ppermute | solution.py:416
  13.1 9.2 %collective-permute-start.8 = (bf16[256,256]{1,0:T(8,128)(2,1)S(1)}, bf16[256,256]{1,0:T(8,128)(2,1)S(1)}, u32[]{:S(2)}, u32[]{:S(2)}) collective-permute-start(bf16[256,256]{1,0:T(8,128)(2,1)S(1)} %broadcast_select_fusion), channel_id=1, source_target_pairs={{0,2},{1,3},{2,4},{3,5},{4,6},{5,7},{6,8},{7,9},{8,10},{9,11},{10,... | collective-permute-start | bytes 393224 | tf_op jit(solution)/shard_map/ppermute | solution.py:416
  14.9 8.7 %collective-permute-start.7 = (bf16[256,256]{1,0:T(8,128)(2,1)S(1)}, bf16[256,256]{1,0:T(8,128)(2,1)S(1)}, u32[]{:S(2)}, u32[]{:S(2)}) collective-permute-start(bf16[256,256]{1,0:T(8,128)(2,1)S(1)} %collective-permute-done.6.kv2), channel_id=1, source_target_pairs={{0,4},{1,5},{2,6},{3,7},{4,8},{5,9},{6,10},{7,11},{8,12},{9,13},{1... | collective-permute-start | bytes 393224 | tf_op jit(solution)/shard_map/ppermute | solution.py:416
  14.9 8.7 %collective-permute-start.9 = (bf16[256,256]{1,0:T(8,128)(2,1)S(1)}, bf16[256,256]{1,0:T(8,128)(2,1)S(1)}, u32[]{:S(2)}, u32[]{:S(2)}) collective-permute-start(bf16[256,256]{1,0:T(8,128)(2,1)S(1)} %collective-permute-done.6.kv2), channel_id=1, source_target_pairs={{0,2},{1,3},{2,0},{3,1},{4,6},{5,7},{6,4},{7,5},{8,10},{9,11},{10,... | collective-permute-start | bytes 393224 | tf_op jit(solution)/shard_map/ppermute | solution.py:422
  16.2 19.3 %collective-permute-start.4 = (bf16[256,256]{1,0:T(8,128)(2,1)S(1)}, bf16[256,256]{1,0:T(8,128)(2,1)S(1)}, u32[]{:S(2)}, u32[]{:S(2)}) collective-permute-start(bf16[256,256]{1,0:T(8,128)(2,1)S(1)} %broadcast_select_fusion.1), channel_id=1, source_target_pairs={{0,2},{1,3},{2,4},{3,5},{4,6},{5,7},{6,8},{7,9},{8,10},{9,11},{10,... | collective-permute-start | bytes 393224 | tf_op jit(solution)/shard_map/ppermute | solution.py:416
  17.2 20.2 %collective-permute-start.3 = (bf16[256,256]{1,0:T(8,128)(2,1)S(1)}, bf16[256,256]{1,0:T(8,128)(2,1)S(1)}, u32[]{:S(2)}, u32[]{:S(2)}) collective-permute-start(bf16[256,256]{1,0:T(8,128)(2,1)S(1)} %collective-permute-done.2.kv2), channel_id=1, source_target_pairs={{0,4},{1,5},{2,6},{3,7},{4,8},{5,9},{6,10},{7,11},{8,12},{9,13},{1... | collective-permute-start | bytes 393224 | tf_op jit(solution)/shard_map/ppermute | solution.py:416
  22.3 15.1 %collective-permute-start.5 = (bf16[256,256]{1,0:T(8,128)(2,1)S(1)}, bf16[256,256]{1,0:T(8,128)(2,1)S(1)}, u32[]{:S(2)}, u32[]{:S(2)}) collective-permute-start(bf16[256,256]{1,0:T(8,128)(2,1)S(1)} %collective-permute-done.2.kv2), channel_id=1, source_target_pairs={{0,2},{1,3},{2,0},{3,1},{4,6},{5,7},{6,4},{7,5},{8,10},{9,11},{10,... | collective-permute-start | bytes 393224 | tf_op jit(solution)/shard_map/ppermute | solution.py:422
  33.2 16.0 %collective-permute-start.12 = (bf16[256,256]{1,0:T(8,128)(2,1)S(1)}, bf16[256,256]{1,0:T(8,128)(2,1)S(1)}, u32[]{:S(2)}, u32[]{:S(2)}) collective-permute-start(bf16[256,256]{1,0:T(8,128)(2,1)S(1)} %get-tuple-element.49), channel_id=1, source_target_pairs={{0,14},{1,15},{2,0},{3,1},{4,2},{5,3},{6,4},{7,5},{8,6},{9,7},{10,... | collective-permute-start | bytes 393224 | tf_op jit(solution)/shard_map/ppermute | solution.py:416
  35.0 16.0 %collective-permute-start.13 = (bf16[256,256]{1,0:T(8,128)(2,1)S(1)}, bf16[256,256]{1,0:T(8,128)(2,1)S(1)}, u32[]{:S(2)}, u32[]{:S(2)}) collective-permute-start(bf16[256,256]{1,0:T(8,128)(2,1)S(1)} %get-tuple-element.51), channel_id=1, source_target_pairs={{0,2},{1,3},{2,0},{3,1},{4,6},{5,7},{6,4},{7,5},{8,10},{9,11},{10,... | collective-permute-start | bytes 393224 | tf_op jit(solution)/shard_map/ppermute | solution.py:422
  35.5 15.5 %collective-permute-start.14 = (bf16[256,256]{1,0:T(8,128)(2,1)S(1)}, bf16[256,256]{1,0:T(8,128)(2,1)S(1)}, u32[]{:S(2)}, u32[]{:S(2)}) collective-permute-start(bf16[256,256]{1,0:T(8,128)(2,1)S(1)} %get-tuple-element.52), channel_id=1, source_target_pairs={{0,12},{1,13},{2,14},{3,15},{4,0},{5,1},{6,2},{7,3},{8,4},{9,5},{1... | collective-permute-start | bytes 393224 | tf_op jit(solution)/shard_map/ppermute | solution.py:416
  47.0 5.0 %collective-permute-start.16 = (bf16[256,256]{1,0:T(8,128)(2,1)S(1)}, bf16[256,256]{1,0:T(8,128)(2,1)S(1)}, u32[]{:S(2)}, u32[]{:S(2)}) collective-permute-start(bf16[256,256]{1,0:T(8,128)(2,1)S(1)} %get-tuple-element.54), channel_id=1, source_target_pairs={{0,14},{1,15},{2,0},{3,1},{4,2},{5,3},{6,4},{7,5},{8,6},{9,7},{10,... | collective-permute-start | bytes 393224 | tf_op jit(solution)/shard_map/ppermute | solution.py:416
  47.5 6.1 %collective-permute-start.17 = (bf16[256,256]{1,0:T(8,128)(2,1)S(1)}, bf16[256,256]{1,0:T(8,128)(2,1)S(1)}, u32[]{:S(2)}, u32[]{:S(2)}) collective-permute-start(bf16[256,256]{1,0:T(8,128)(2,1)S(1)} %get-tuple-element.56), channel_id=1, source_target_pairs={{0,2},{1,3},{2,0},{3,1},{4,6},{5,7},{6,4},{7,5},{8,10},{9,11},{10,... | collective-permute-start | bytes 393224 | tf_op jit(solution)/shard_map/ppermute | solution.py:422
  49.1 5.4 %collective-permute-start.18 = (bf16[256,256]{1,0:T(8,128)(2,1)S(1)}, bf16[256,256]{1,0:T(8,128)(2,1)S(1)}, u32[]{:S(2)}, u32[]{:S(2)}) collective-permute-start(bf16[256,256]{1,0:T(8,128)(2,1)S(1)} %get-tuple-element.57), channel_id=1, source_target_pairs={{0,12},{1,13},{2,14},{3,15},{4,0},{5,1},{6,2},{7,3},{8,4},{9,5},{1... | collective-permute-start | bytes 393224 | tf_op jit(solution)/shard_map/ppermute | solution.py:416
  50.9 12.1 %collective-permute-start.11 = (bf16[128,2048]{1,0:T(8,128)(2,1)S(1)}, bf16[128,2048]{1,0:T(8,128)(2,1)S(1)}, u32[]{:S(2)}, u32[]{:S(2)}) collective-permute-start(bf16[128,2048]{1,0:T(8,128)(2,1)S(1)} %get-tuple-element.47), channel_id=1, source_target_pairs={{0,1},{1,0},{2,3},{3,2},{4,5},{5,4},{6,7},{7,6},{8,9},{9,8},{10,11... | collective-permute-start | bytes 1572872 | tf_op jit(solution)/shard_map/ppermute | solution.py:419
  51.0 12.1 %collective-permute-start.10 = (bf16[128,2048]{1,0:T(8,128)(2,1)S(1)}, bf16[128,2048]{1,0:T(8,128)(2,1)S(1)}, u32[]{:S(2)}, u32[]{:S(2)}) collective-permute-start(bf16[128,2048]{1,0:T(8,128)(2,1)S(1)} %get-tuple-element.46), channel_id=1, source_target_pairs={{0,1},{1,0},{2,3},{3,2},{4,5},{5,4},{6,7},{7,6},{8,9},{9,8},{10,11... | collective-permute-start | bytes 1572872 | tf_op jit(solution)/shard_map/ppermute | solution.py:419
  52.1 6.9 %collective-permute-start.15 = (bf16[256,256]{1,0:T(8,128)(2,1)S(1)}, bf16[256,256]{1,0:T(8,128)(2,1)S(1)}, u32[]{:S(2)}, u32[]{:S(2)}) collective-permute-start(bf16[256,256]{1,0:T(8,128)(2,1)S(1)} %fusion.4), channel_id=1, source_target_pairs={{0,12},{1,13},{2,14},{3,15},{4,0},{5,1},{6,2},{7,3},{8,4},{9,5},{1... | collective-permute-start | bytes 393224 | tf_op jit(solution)/shard_map/ppermute | solution.py:416
  54.6 6.9 %collective-permute-start.19 = (bf16[256,256]{1,0:T(8,128)(2,1)S(1)}, bf16[256,256]{1,0:T(8,128)(2,1)S(1)}, u32[]{:S(2)}, u32[]{:S(2)}) collective-permute-start(bf16[256,256]{1,0:T(8,128)(2,1)S(1)} %fusion.9), channel_id=1, source_target_pairs={{0,12},{1,13},{2,14},{3,15},{4,0},{5,1},{6,2},{7,3},{8,4},{9,5},{1... | collective-permute-start | bytes 393224 | tf_op jit(solution)/shard_map/ppermute | solution.py:416
  61.6 1.4 %collective-permute-start.20 = (bf16[128,512]{1,0:T(8,128)(2,1)S(1)}, bf16[128,512]{1,0:T(8,128)(2,1)S(1)}, u32[]{:S(2)}, u32[]{:S(2)}) collective-permute-start(bf16[128,512]{1,0:T(8,128)(2,1)S(1)} %get-tuple-element.58), channel_id=1, source_target_pairs={{0,1},{1,0},{2,3},{3,2},{4,5},{5,4},{6,7},{7,6},{8,9},{9,8},{10,11... | collective-permute-start | bytes 393224 | tf_op jit(solution)/shard_map/ppermute | solution.py:419

commit v2 on v1

--- a/solution.py
+++ b/solution.py
@@ -128,147 +128,161 @@
     two = q_t.shape[2]
     rows = two // 2
     wide = 2 * pairs * width
-    blocks = 2 * CHUNKS - 1
-    span = blocks * rows
     base = slot * units
+    half = pairs * two
+    part = (3 * pairs // 2) * two
+    sums = ((d_scr, qs_st, dk_acc, scale, 0), (p_scr, gs_st, dv_acc, 1.0, width))
     even = lax.rem(chip, 2) == 0
     edge = pl.multiple_of(jnp.where(even, two, 3 * two), two)
     middle = pl.multiple_of(jnp.where(even, 3 * two, two), two)
     places = [pl.ds(at, two) for at in (0, edge, 2 * two, middle, 4 * two)]
 
-    k_aug[:, width:] = k_seg[...]
-    for at, kv in zip(places, (kv4, kv_edge, kv2, kv_middle, kv0)):
-        k_aug[at, :width] = kv[:, :width]
-        v_win[at] = kv[:, width:]
-        k_t[:, at] = kv[:, :width].T
-        v_t[:width, at] = kv[:, width:].T
-
-    v_t[width:] = jnp.ones((v_t.shape[0] - width, v_t.shape[1]), BF)
-
-    lane = lax.broadcasted_iota(jnp.int32, (rows, two), 1)
-    causal = lax.broadcasted_iota(jnp.int32, (rows, two), 0) <= jnp.where(lane >= rows, lane - rows, lane)
-
-    def window(u):
-        first = (u // pairs) * rows
-        return first, slice(first, first + span)
-
-    def columns(u):
-        return slice(u * two, (u + 1) * two)
-
-    def fold(x, op):
-        return op(x.reshape(x.shape[0] // 8, 8, x.shape[1]), axis=0)
-
-    def scores(u, b, top):
-        first, _ = window(u)
-        s = dot(k_aug[first + b * rows:first + (b + 3) * rows], q_t[base + u])
-        for i in range(3):
-            part = s[i * rows:(i + 1) * rows]
-            if b + i == blocks - 1:
-                part = jnp.where(causal, part, MASKED)
-            s_scr[u % 2, (b + i) * rows:(b + i + 1) * rows] = part
-            top = jnp.maximum(top, fold(part, jnp.max))
-        return top
-
-    def weights(u, b, peak):
-        first, _ = window(u)
-        e = jnp.exp2((s_scr[u % 2, b * rows:(b + 1) * rows] - peak) * (scale * math.log2(math.e)))
-        p_scr[first + b * rows:first + (b + 1) * rows, columns(u)] = e.astype(BF)
-
-    def score_grads(u, b, inner):
-        first, _ = window(u)
-        keys = slice(first + b * rows, first + (b + 3) * rows)
-        dp = dot(v_win[keys], g_t[base + u])
-        d_scr[keys, columns(u)] = p_scr[keys, columns(u)] * (dp - inner).astype(BF)
-
-    def store(x, out, u):
-        block, p = u // pairs, u % pairs
-        x = x.T
-        for i in range(2):
-            out[block * rows:(block + 1) * rows, (2 * p + i) * width:(2 * p + i + 1) * width] = (
-                x[i * rows:(i + 1) * rows]
-            )
-
-    def query_grad(u, inv):
-        _, keys = window(u)
-        store((dot(k_t[:, keys], d_scr[keys, columns(u)]) * (inv * scale)).astype(BF), dq_scr, u)
-
-    half = pairs * two
-    part = (3 * pairs // 2) * two
-    sums = ((p_scr, gs_st, dv_acc), (d_scr, qs_st, dk_acc))
-    first_group = [(b * rows, *one) for b in range(0, blocks, 3) for one in sums]
-    second_group = [(rows + b * rows, *one) for b in range(0, blocks, 3) for one in sums]
-    for _, _, acc in sums:
-        acc[span:] = jnp.zeros((rows, width), F32)
-
-    def key_grads(u):
-        if u > pairs and first_group:
-            at, left, right, acc = first_group.pop(0)
-            at = slice(at, at + 3 * rows)
-            acc[at] = dot(left[at, :half], right[:half])
-        elif u > 3 * pairs // 2 and second_group:
-            at, left, right, acc = second_group.pop(0)
-            at = slice(at, at + 3 * rows)
-            acc[at] += dot(left[at, half:part], right[half:part])
-
-    def one_unit(u, peak, inv_before, more):
-        _, keys = window(u)
-        top = jnp.full((8, two), MASKED, F32)
-        for b in range(0, blocks, 3):
-            if more:
-                top = scores(u + 1, b, top)
-            key_grads(u)
-            for i in range(3):
-                weights(u, b + i, peak)
-        peak = jnp.max(top, axis=0, keepdims=True)
-        o = dot(v_t[:, keys], p_scr[keys, columns(u)])
-        if u > 0:
-            query_grad(u - 1, inv_before)
-        inv = 1.0 / o[width:width + 1]
-        o = (o[:width] * inv).astype(BF)
-        store(o, o_scr, u)
-        inner = jnp.sum(g_t[base + u].astype(F32) * o.astype(F32), axis=0, keepdims=True)
-        for b in range(0, blocks, 3):
-            key_grads(u)
-            score_grads(u, b, inner)
-        column = jnp.broadcast_to(inv, (8, two)).T[:, :1]
-        here, there = slice(u * two, (u + 1) * two), slice((base + u) * two, (base + u + 1) * two)
-        qs_st[here] = (q_st[there].astype(F32) * column).astype(BF)
-        gs_st[here] = (g_st[there].astype(F32) * column).astype(BF)
-        return peak, inv
-
-    top = jnp.full((8, two), MASKED, F32)
-    for b in range(0, blocks, 3):
-        top = scores(0, b, top)
-    peak, inv = jnp.max(top, axis=0, keepdims=True), None
-    for u in range(units):
-        peak, inv = one_unit(u, peak, inv, u + 1 < units)
-    query_grad(units - 1, inv)
-
-    mine = pl.ds(pl.multiple_of(core * rows, rows), rows)
-    other = pl.ds(pl.multiple_of((1 - core) * rows, rows), rows)
-    cols = pl.ds(pl.multiple_of((core * heads + slot) * wide, wide), wide)
-    moves = [
-        (o_scr.at[other], sent.at[:, pl.ds(0, wide)]),
-        (dq_scr.at[other], sent.at[:, pl.ds(wide, wide)]),
-        (o_scr.at[mine], o_all.at[:, cols]),
-        (dq_scr.at[mine], dq_all.at[:, cols]),
-    ]
-    copies = run(moves, sems)
-
-    for left, right, acc, factor, col in (
-        (d_scr, qs_st, dk_acc, scale, 0), (p_scr, gs_st, dv_acc, 1.0, width)
-    ):
-        cols = slice(col, col + width)
-
-        def total(keys):
-            return factor * (acc[keys] + dot(left[keys, part:], right[part:]))
-
-        d4[:rows, cols] = (factor * acc[:rows]).astype(d4.dtype)
-        d4[rows:, cols] = total(slice(rows, two)).astype(d4.dtype)
-        for at, out in zip(places[1:], (d_edge, d2, d_middle, d0)):
-            out[:, cols] = total(at).astype(out.dtype)
-    for copy in copies:
-        copy.wait()
+    def attend(blocks, step):
+        whole = blocks == 2 * CHUNKS - 1
+        k_aug[:, width:] = k_seg[...]
+        for at, kv in zip(places, (kv4, kv_edge, kv2, kv_middle, kv0)):
+            k_aug[at, :width] = kv[:, :width]
+            v_win[at] = kv[:, width:]
+            k_t[:, at] = kv[:, :width].T
+            v_t[:width, at] = kv[:, width:].T
+
+        v_t[width:] = jnp.ones((v_t.shape[0] - width, v_t.shape[1]), BF)
+
+        lane = lax.broadcasted_iota(jnp.int32, (rows, two), 1)
+        causal = lax.broadcasted_iota(jnp.int32, (rows, two), 0) <= jnp.where(lane >= rows, lane - rows, lane)
+
+        def window(u):
+            first = (u // pairs + 2 * CHUNKS - 1 - blocks) * rows
+            return first, slice(first, first + blocks * rows)
+
+        def columns(u):
+            return slice(u * two, (u + 1) * two)
+
+        def fold(x, op):
+            return op(x.reshape(x.shape[0] // 8, 8, x.shape[1]), axis=0)
+
+        def scores(u, b, top):
+            first, _ = window(u)
+            s = dot(k_aug[first + b * rows:first + (b + step) * rows], q_t[base + u])
+            for i in range(step):
+                part = s[i * rows:(i + 1) * rows]
+                if b + i == blocks - 1:
+                    part = jnp.where(causal, part, MASKED)
+                s_scr[u % 2, (b + i) * rows:(b + i + 1) * rows] = part
+                top = jnp.maximum(top, fold(part, jnp.max))
+            return top
+
+        def weights(u, b, peak):
+            first, _ = window(u)
+            e = jnp.exp2((s_scr[u % 2, b * rows:(b + 1) * rows] - peak) * (scale * math.log2(math.e)))
+            p_scr[first + b * rows:first + (b + 1) * rows, columns(u)] = e.astype(BF)
+
+        def score_grads(u, b, inner):
+            first, _ = window(u)
+            keys = slice(first + b * rows, first + (b + step) * rows)
+            dp = dot(v_win[keys], g_t[base + u])
+            d_scr[keys, columns(u)] = p_scr[keys, columns(u)] * (dp - inner).astype(BF)
+
+        def store(x, out, u):
+            block, p = u // pairs, u % pairs
+            x = x.T
+            for i in range(2):
+                out[block * rows:(block + 1) * rows, (2 * p + i) * width:(2 * p + i + 1) * width] = (
+                    x[i * rows:(i + 1) * rows]
+                )
+
+        def query_grad(u, inv):
+            _, keys = window(u)
+            store((dot(k_t[:, keys], d_scr[keys, columns(u)]) * (inv * scale)).astype(BF), dq_scr, u)
+
+        first_group = [(b * rows, *one[:3]) for b in range(0, blocks, 3) for one in sums] if whole else []
+        second_group = [(rows + b * rows, *one[:3]) for b in range(0, blocks, 3) for one in sums] if whole else []
+
+        def key_grads(turn):
+            if turn > pairs and first_group:
+                at, left, right, acc = first_group.pop(0)
+                at = slice(at, at + 3 * rows)
+                acc[at] = dot(left[at, :half], right[:half])
+            elif turn > 3 * pairs // 2 and second_group:
+                at, left, right, acc = second_group.pop(0)
+                at = slice(at, at + 3 * rows)
+                acc[at] += dot(left[at, half:part], right[half:part])
+
+        def outputs(u):
+            _, keys = window(u)
+            o = dot(v_t[:, keys], p_scr[keys, columns(u)])
+            inv = 1.0 / o[width:width + 1]
+            o = (o[:width] * inv).astype(BF)
+            store(o, o_scr, u)
+            inner = jnp.sum(g_t[base + u].astype(F32) * o.astype(F32), axis=0, keepdims=True)
+            column = jnp.broadcast_to(inv, (8, two)).T[:, :1]
+            here, there = slice(u * two, (u + 1) * two), slice((base + u) * two, (base + u + 1) * two)
+            qs_st[here] = (q_st[there].astype(F32) * column).astype(BF)
+            gs_st[here] = (g_st[there].astype(F32) * column).astype(BF)
+            return inv, inner
+
+        def turn(u, peak, inv, inner):
+            top = jnp.full((8, two), MASKED, F32)
+            for b in range(0, blocks, step):
+                if u + 1 < units:
+                    top = scores(u + 1, b, top)
+                if 0 <= u < units:
+                    for i in range(step):
+                        weights(u, b + i, peak)
+                if u > 0:
+                    score_grads(u - 1, b, inner)
+                key_grads(u)
+                if u + 1 >= units:
+                    key_grads(u)
+            if u > 0:
+                query_grad(u - 1, inv)
+            if 0 <= u < units:
+                inv, inner = outputs(u)
+            return jnp.max(top, axis=0, keepdims=True), inv, inner
+
+        if whole:
+            for one in sums:
+                one[2][blocks * rows:] = jnp.zeros((rows, width), F32)
+        state = (None, None, None)
+        for u in range(-1, units + 1):
+            state = turn(u, *state)
+
+        mine = pl.ds(pl.multiple_of(core * rows, rows), rows)
+        other = pl.ds(pl.multiple_of((1 - core) * rows, rows), rows)
+        cols = pl.ds(pl.multiple_of((core * heads + slot) * wide, wide), wide)
+        moves = [
+            (o_scr.at[other], sent.at[:, pl.ds(0, wide)]),
+            (dq_scr.at[other], sent.at[:, pl.ds(wide, wide)]),
+            (o_scr.at[mine], o_all.at[:, cols]),
+            (dq_scr.at[mine], dq_all.at[:, cols]),
+        ]
+        copies = run(moves, sems)
+
+        for left, right, acc, factor, col in sums:
+            cols = slice(col, col + width)
+            late = 3 * two
+            if not whole:
+                acc[:late] = jnp.zeros((late, width), F32)
+                acc[late:] = dot(left[late:, half:], right[half:])
+                acc[late:late + 3 * rows] += dot(left[late:late + 3 * rows, :half], right[:half])
+
+            def total(keys):
+                return factor * (acc[keys] + dot(left[keys, part:], right[part:]) if whole else acc[keys])
+
+            d4[:rows, cols] = (factor * acc[:rows]).astype(d4.dtype)
+            d4[rows:, cols] = total(slice(rows, two)).astype(d4.dtype)
+            for at, out in zip(places[1:], (d_edge, d2, d_middle, d0)):
+                out[:, cols] = total(at).astype(out.dtype)
+        for copy in copies:
+            copy.wait()
+
+    @pl.when(chip >= 2)
+    def _():
+        attend(2 * CHUNKS - 1, 3)
+
+    @pl.when(chip < 2)
+    def _():
+        attend(4, 2)
 
 
 def place_kernel(heads, o_in, dq_in, *refs):

time: 64.9 us -> 62.2 us (0.958)
  Pallas kernels: 24.1 us -> 15.3 us
  starting transfers between devices: 26.2 us -> 33.9 us
  waiting for transfers between devices: 12.7 us -> 11.5 us
    ppermute x12, starting transfers between devices: 20.1 us -> 29.8 us  [shift(): return lax.ppermute(x, 'context', [(i, (i + by) % n) for i in range(n)])]
    pallas_call x2, Pallas kernels: 19.2 us -> 10.5 us  [head_attention(): pl.pallas_call(functools.partial(attention_kernel, slot, heads), in_specs...]
    ppermute x4, starting transfers between devices: 4.62 us -> 2.54 us  [across(): return lax.ppermute(x, 'context', [(i, i ^ 2) for i in range(n)])]
    ppermute x12, waiting for transfers between devices: 10.4 us -> 9.17 us  [shift(): return lax.ppermute(x, 'context', [(i, (i + by) % n) for i in range(n)])]
  transfers between devices with their start and end apart: 21 -> 21, of which waited for: 7 -> 5; matrix products, arithmetic and copies ran while one was open for 1% -> 1% of each run, Pallas kernels for 33% -> 21%
where the time goes in v2:
time: 62.2 us; the launch traced here: 62 us
  starting transfers between devices  33.9 us (55%)
  Pallas kernels  15.3 us (25%)
  waiting for transfers between devices  11.5 us (18%)
  between operations  0.94 us (2%)
    ppermute x12, starting transfers between devices, shift(): return lax.ppermute(x, 'context', [(i, (i + by) % n) for i in range(n)])  29.8 us
    pallas_call x2, Pallas kernels, head_attention(): pl.pallas_call(functools.partial(attention_kernel, slot, heads), in_specs...  10.5 us
    ppermute x12, waiting for transfers between devices, shift(): return lax.ppermute(x, 'context', [(i, (i + by) % n) for i in range(n)])  9.17 us
    ppermute x4, starting transfers between devices, across(): return lax.ppermute(x, 'context', [(i, i ^ 2) for i in range(n)])  2.54 us
    ppermute x5, waiting for transfers between devices, swap(): return lax.ppermute(x, 'context', [(i, i ^ 1) for i in range(n)])  2.33 us
    pallas_call x1, Pallas kernels, staged(): pl.pallas_call(functools.partial(stage_kernel, heads), in_specs=[ANYWHERE...  2.29 us
    ppermute x5, starting transfers between devices, swap(): return lax.ppermute(x, 'context', [(i, i ^ 1) for i in range(n)])  1.52 us
    pallas_call x1, Pallas kernels, shares(): pl.pallas_call(share_kernel, in_specs=[ANYWHERE] * 4, out_specs=[VMEM] *...  1.41 us
  transfers between devices with their start and end apart: 21, of which 5 were waited for; matrix products, arithmetic and copies ran while one was open for 1% of the time, Pallas kernels for 21%

profile of v2, /device:TPU:0, one launch (start us, length us, event | category | flops | bytes accessed | tf_op | source)
XLA Modules:
  0.0 62.0 jit_solution(7081964144027404182)
XLA Ops:
  0.6 1.4 %share.1 = (bf16[128,512]{1,0:T(8,128)(2,1)S(1)}, bf16[128,512]{1,0:T(8,128)(2,1)S(1)}, bf16[128,4096]{1,0:T(8,128)(2,1)S(1)}) custom-call(bf16[128,512]{1,0:T(8,128)(2,1)} %k.1, bf16[128,512]{1,0:T(8,128)(2,1)} %v.1, bf16[128,4096]{1,0:T(8,128)(2,1)} %q_all.1, bf16[128,4096]{1,0:T(8,128)(2,1)} %g_all.1), custom_call_target="tpu_custom_call" | custom-call | tf_op jit(solution)/shard_map/share/pallas_call | solution.py:306
  2.0 0.5 collective-permute-start
  2.6 1.0 %collective-permute-done.kv_oth = bf16[128,512]{1,0:T(8,128)(2,1)S(1)} collective-permute-done((bf16[128,512]{1,0:T(8,128)(2,1)S(1)}, bf16[128,512]{1,0:T(8,128)(2,1)S(1)}, u32[]{:S(2)}, u32[]{:S(2)}) %collective-permute-start) | collective-permute-done | bytes 131104 | tf_op jit(solution)/shard_map/ppermute | solution.py:433
  4.0 2.7 %collective-permute-start.6 = (bf16[256,256]{1,0:T(8,128)(2,1)S(1)}, bf16[256,256]{1,0:T(8,128)(2,1)S(1)}, u32[]{:S(2)}, u32[]{:S(2)}) collective-permute-start(bf16[256,256]{1,0:T(8,128)(2,1)S(1)} %get-tuple-element.41.kv0), channel_id=1, source_target_pairs={{0,4},{1,5},{2,6},{3,7},{4,8},{5,9},{6,10},{7,11},{8,12},{9,13},{1... | collective-permute-start | bytes 393224 | tf_op jit(solution)/shard_map/ppermute | solution.py:430
  6.8 1.6 %collective-permute-start.2 = (bf16[256,256]{1,0:T(8,128)(2,1)S(1)}, bf16[256,256]{1,0:T(8,128)(2,1)S(1)}, u32[]{:S(2)}, u32[]{:S(2)}) collective-permute-start(bf16[256,256]{1,0:T(8,128)(2,1)S(1)} %get-tuple-element.40.kv0), channel_id=1, source_target_pairs={{0,4},{1,5},{2,6},{3,7},{4,8},{5,9},{6,10},{7,11},{8,12},{9,13},{1... | collective-permute-start | bytes 393224 | tf_op jit(solution)/shard_map/ppermute | solution.py:430
  8.3 4.8 %collective-permute-done.6.kv2 = bf16[256,256]{1,0:T(8,128)(2,1)S(1)} collective-permute-done((bf16[256,256]{1,0:T(8,128)(2,1)S(1)}, bf16[256,256]{1,0:T(8,128)(2,1)S(1)}, u32[]{:S(2)}, u32[]{:S(2)}) %collective-permute-start.6) | collective-permute-done | bytes 131104 | tf_op jit(solution)/shard_map/ppermute | solution.py:430
  13.1 1.7 %collective-permute-start.8 = (bf16[256,256]{1,0:T(8,128)(2,1)S(1)}, bf16[256,256]{1,0:T(8,128)(2,1)S(1)}, u32[]{:S(2)}, u32[]{:S(2)}) collective-permute-start(bf16[256,256]{1,0:T(8,128)(2,1)S(1)} %broadcast_select_fusion), channel_id=1, source_target_pairs={{0,2},{1,3},{2,4},{3,5},{4,6},{5,7},{6,8},{7,9},{8,10},{9,11},{10,... | collective-permute-start | bytes 393224 | tf_op jit(solution)/shard_map/ppermute | solution.py:430
  14.9 1.3 %collective-permute-start.9 = (bf16[256,256]{1,0:T(8,128)(2,1)S(1)}, bf16[256,256]{1,0:T(8,128)(2,1)S(1)}, u32[]{:S(2)}, u32[]{:S(2)}) collective-permute-start(bf16[256,256]{1,0:T(8,128)(2,1)S(1)} %collective-permute-done.6.kv2), channel_id=1, source_target_pairs={{0,2},{1,3},{2,0},{3,1},{4,6},{5,7},{6,4},{7,5},{8,10},{9,11},{10,... | collective-permute-start | bytes 393224 | tf_op jit(solution)/shard_map/ppermute | solution.py:436
  16.2 1.0 %collective-permute-start.4 = (bf16[256,256]{1,0:T(8,128)(2,1)S(1)}, bf16[256,256]{1,0:T(8,128)(2,1)S(1)}, u32[]{:S(2)}, u32[]{:S(2)}) collective-permute-start(bf16[256,256]{1,0:T(8,128)(2,1)S(1)} %broadcast_select_fusion.1), channel_id=1, source_target_pairs={{0,2},{1,3},{2,4},{3,5},{4,6},{5,7},{6,8},{7,9},{8,10},{9,11},{10,... | collective-permute-start | bytes 393224 | tf_op jit(solution)/shard_map/ppermute | solution.py:430
  17.2 1.2 %collective-permute-start.3 = (bf16[256,256]{1,0:T(8,128)(2,1)S(1)}, bf16[256,256]{1,0:T(8,128)(2,1)S(1)}, u32[]{:S(2)}, u32[]{:S(2)}) collective-permute-start(bf16[256,256]{1,0:T(8,128)(2,1)S(1)} %collective-permute-done.2.kv2), channel_id=1, source_target_pairs={{0,4},{1,5},{2,6},{3,7},{4,8},{5,9},{6,10},{7,11},{8,12},{9,13},{1... | collective-permute-start | bytes 393224 | tf_op jit(solution)/shard_map/ppermute | solution.py:430
  18.3 2.3 %stage.1 = (bf16[4096,128]{1,0:T(8,128)(2,1)S(1)}, bf16[4096,128]{1,0:T(8,128)(2,1)S(1)}, bf16[16,256,256]{2,1,0:T(8,128)(2,1)S(1)}, bf16[16,128,256]{2,1,0:T(8,128)(2,1)S(1)}, bf16[1280,128]{1,0:T(8,128)(2,1)S(1)}) custom-call(s32[5]{0:T(128)} %bounds_in.1, bf16[128,4096]{1,0:T(8,128)(2,1)} %q_all.1, bf16[128,4096]{1,0:T(8,128)(2,1)} %g_all.1, ...), custom_call_target="tpu_custom_call" | custom-call | bytes 4194304 | tf_op jit(solution)/shard_map/stage/pallas_call | solution.py:334
  20.6 1.7 %collective-permute-done.8.kv_edge = bf16[256,256]{1,0:T(8,128)(2,1)S(1)} collective-permute-done((bf16[256,256]{1,0:T(8,128)(2,1)S(1)}, bf16[256,256]{1,0:T(8,128)(2,1)S(1)}, u32[]{:S(2)}, u32[]{:S(2)}) %collective-permute-start.8) | collective-permute-done | bytes 131104 | tf_op jit(solution)/shard_map/ppermute | solution.py:430
  22.3 1.2 %collective-permute-start.5 = (bf16[256,256]{1,0:T(8,128)(2,1)S(1)}, bf16[256,256]{1,0:T(8,128)(2,1)S(1)}, u32[]{:S(2)}, u32[]{:S(2)}) collective-permute-start(bf16[256,256]{1,0:T(8,128)(2,1)S(1)} %collective-permute-done.2.kv2), channel_id=1, source_target_pairs={{0,2},{1,3},{2,0},{3,1},{4,6},{5,7},{6,4},{7,5},{8,10},{9,11},{10,... | collective-permute-start | bytes 393224 | tf_op jit(solution)/shard_map/ppermute | solution.py:436
  23.5 5.2 %attention0.1 = (bf16[128,4096]{1,0:T(8,128)(2,1)}, bf16[128,4096]{1,0:T(8,128)(2,1)}, bf16[128,2048]{1,0:T(8,128)(2,1)S(1)}, bf16[256,256]{1,0:T(8,128)(2,1)S(1...) custom-call(bf16[4096,128]{1,0:T(8,128)(2,1)S(1)} %get-tuple-element, ...), custom_call_target="tpu_custom_call" | custom-call | flops 3355443200 | bytes 3145728 | tf_op jit(solution)/shard_map/attention0/pallas_call | solution.py:366
  28.8 6.1 %collective-permute-start.12 = (bf16[256,256]{1,0:T(8,128)(2,1)S(1)}, bf16[256,256]{1,0:T(8,128)(2,1)S(1)}, u32[]{:S(2)}, u32[]{:S(2)}) collective-permute-start(bf16[256,256]{1,0:T(8,128)(2,1)S(1)} %get-tuple-element.49), channel_id=1, source_target_pairs={{0,14},{1,15},{2,0},{3,1},{4,2},{5,3},{6,4},{7,5},{8,6},{9,7},{10,... | collective-permute-start | bytes 393224 | tf_op jit(solution)/shard_map/ppermute | solution.py:430
  34.9 2.4 %collective-permute-start.14 = (bf16[256,256]{1,0:T(8,128)(2,1)S(1)}, bf16[256,256]{1,0:T(8,128)(2,1)S(1)}, u32[]{:S(2)}, u32[]{:S(2)}) collective-permute-start(bf16[256,256]{1,0:T(8,128)(2,1)S(1)} %get-tuple-element.52), channel_id=1, source_target_pairs={{0,12},{1,13},{2,14},{3,15},{4,0},{5,1},{6,2},{7,3},{8,4},{9,5},{1... | collective-permute-start | bytes 393224 | tf_op jit(solution)/shard_map/ppermute | solution.py:430
  37.4 5.2 %attention1.1 = (bf16[128,4096]{1,0:T(8,128)(2,1)}, bf16[128,4096]{1,0:T(8,128)(2,1)}, bf16[128,2048]{1,0:T(8,128)(2,1)S(1)}, bf16[256,256]{1,0:T(8,128)(2,1)S(1...) custom-call(bf16[4096,128]{1,0:T(8,128)(2,1)S(1)} %get-tuple-element, ...), custom_call_target="tpu_custom_call", output_to_operand_aliasing={{0}: (10, {}), {1}: (11, {})} | custom-call | flops 3355443200 | bytes 3145728 | tf_op jit(solution)/shard_map/attention1/pallas_call | solution.py:366
  42.6 4.8 %collective-permute-start.16 = (bf16[256,256]{1,0:T(8,128)(2,1)S(1)}, bf16[256,256]{1,0:T(8,128)(2,1)S(1)}, u32[]{:S(2)}, u32[]{:S(2)}) collective-permute-start(bf16[256,256]{1,0:T(8,128)(2,1)S(1)} %get-tuple-element.54), channel_id=1, source_target_pairs={{0,14},{1,15},{2,0},{3,1},{4,2},{5,3},{6,4},{7,5},{8,6},{9,7},{10,... | collective-permute-start | bytes 393224 | tf_op jit(solution)/shard_map/ppermute | solution.py:430
  47.4 2.0 %collective-permute-start.18 = (bf16[256,256]{1,0:T(8,128)(2,1)S(1)}, bf16[256,256]{1,0:T(8,128)(2,1)S(1)}, u32[]{:S(2)}, u32[]{:S(2)}) collective-permute-start(bf16[256,256]{1,0:T(8,128)(2,1)S(1)} %get-tuple-element.57), channel_id=1, source_target_pairs={{0,12},{1,13},{2,14},{3,15},{4,0},{5,1},{6,2},{7,3},{8,4},{9,5},{1... | collective-permute-start | bytes 393224 | tf_op jit(solution)/shard_map/ppermute | solution.py:430
  50.0 2.3 %collective-permute-start.15 = (bf16[256,256]{1,0:T(8,128)(2,1)S(1)}, bf16[256,256]{1,0:T(8,128)(2,1)S(1)}, u32[]{:S(2)}, u32[]{:S(2)}) collective-permute-start(bf16[256,256]{1,0:T(8,128)(2,1)S(1)} %fusion.4), channel_id=1, source_target_pairs={{0,12},{1,13},{2,14},{3,15},{4,0},{5,1},{6,2},{7,3},{8,4},{9,5},{1... | collective-permute-start | bytes 393224 | tf_op jit(solution)/shard_map/ppermute | solution.py:430
  52.4 4.0 %collective-permute-start.19 = (bf16[256,256]{1,0:T(8,128)(2,1)S(1)}, bf16[256,256]{1,0:T(8,128)(2,1)S(1)}, u32[]{:S(2)}, u32[]{:S(2)}) collective-permute-start(bf16[256,256]{1,0:T(8,128)(2,1)S(1)} %fusion.9), channel_id=1, source_target_pairs={{0,12},{1,13},{2,14},{3,15},{4,0},{5,1},{6,2},{7,3},{8,4},{9,5},{1... | collective-permute-start | bytes 393224 | tf_op jit(solution)/shard_map/ppermute | solution.py:430
  56.5 2.7 %collective-permute-done.19 = bf16[256,256]{1,0:T(8,128)(2,1)S(1)} collective-permute-done((bf16[256,256]{1,0:T(8,128)(2,1)S(1)}, bf16[256,256]{1,0:T(8,128)(2,1)S(1)}, u32[]{:S(2)}, u32[]{:S(2)}) %collective-permute-start.19) | collective-permute-done | bytes 131104 | tf_op jit(solution)/shard_map/ppermute | solution.py:430
  59.4 1.3 %collective-permute-done.20.refs_3_ = bf16[128,512]{1,0:T(8,128)(2,1)S(1)} collective-permute-done((bf16[128,512]{1,0:T(8,128)(2,1)S(1)}, bf16[128,512]{1,0:T(8,128)(2,1)S(1)}, u32[]{:S(2)}, u32[]{:S(2)}) %collective-permute-start.20) | collective-permute-done | bytes 131104 | tf_op jit(solution)/shard_map/ppermute | solution.py:433
  60.7 1.1 %place.1 = (bf16[128,4096]{1,0:T(8,128)(2,1)}, bf16[128,4096]{1,0:T(8,128)(2,1)}, bf16[128,512]{1,0:T(8,128)(2,1)}, bf16[128,512]{1,0:T(8,128)(2,1)}) custom-call(bf16[128,4096]{1,0:T(8,128)(2,1)} %get-tuple-element.44.o_in, bf16[128,4096]{1,0:T(8,128)(2,1)} %get-tuple-element.45.dq_in, ...), custom_call_target="tpu_custom_call", output_to_operand_aliasing={{0}: (0, {}), {1}: (1, {})} | custom-call | tf_op jit(solution)/shard_map/place/pallas_call | solution.py:404
  (34 shorter events, 1.5 us)
Async XLA Ops:
  2.0 1.5 %collective-permute-start = (bf16[128,512]{1,0:T(8,128)(2,1)S(1)}, bf16[128,512]{1,0:T(8,128)(2,1)S(1)}, u32[]{:S(2)}, u32[]{:S(2)}) collective-permute-start(bf16[128,512]{1,0:T(8,128)(2,1)S(1)} %get-tuple-element.32), channel_id=1, source_target_pairs={{0,1},{1,0},{2,3},{3,2},{4,5},{5,4},{6,7},{7,6},{8,9},{9,8},{10,11... | collective-permute-start | bytes 393224 | tf_op jit(solution)/shard_map/ppermute | solution.py:433
  3.6 13.6 %collective-permute-start.1 = (bf16[128,4096]{1,0:T(8,128)(2,1)S(1)}, bf16[128,4096]{1,0:T(8,128)(2,1)S(1)}, u32[]{:S(2)}, u32[]{:S(2)}) collective-permute-start(bf16[128,4096]{1,0:T(8,128)(2,1)S(1)} %get-tuple-element.34), channel_id=1, source_target_pairs={{0,1},{1,0},{2,3},{3,2},{4,5},{5,4},{6,7},{7,6},{8,9},{9,8},{10,11... | collective-permute-start | bytes 3145736 | tf_op jit(solution)/shard_map/ppermute | solution.py:433
  4.0 9.1 %collective-permute-start.6 = (bf16[256,256]{1,0:T(8,128)(2,1)S(1)}, bf16[256,256]{1,0:T(8,128)(2,1)S(1)}, u32[]{:S(2)}, u32[]{:S(2)}) collective-permute-start(bf16[256,256]{1,0:T(8,128)(2,1)S(1)} %get-tuple-element.41.kv0), channel_id=1, source_target_pairs={{0,4},{1,5},{2,6},{3,7},{4,8},{5,9},{6,10},{7,11},{8,12},{9,13},{1... | collective-permute-start | bytes 393224 | tf_op jit(solution)/shard_map/ppermute | solution.py:430
  6.8 9.4 %collective-permute-start.2 = (bf16[256,256]{1,0:T(8,128)(2,1)S(1)}, bf16[256,256]{1,0:T(8,128)(2,1)S(1)}, u32[]{:S(2)}, u32[]{:S(2)}) collective-permute-start(bf16[256,256]{1,0:T(8,128)(2,1)S(1)} %get-tuple-element.40.kv0), channel_id=1, source_target_pairs={{0,4},{1,5},{2,6},{3,7},{4,8},{5,9},{6,10},{7,11},{8,12},{9,13},{1... | collective-permute-start | bytes 393224 | tf_op jit(solution)/shard_map/ppermute | solution.py:430
  13.1 9.2 %collective-permute-start.8 = (bf16[256,256]{1,0:T(8,128)(2,1)S(1)}, bf16[256,256]{1,0:T(8,128)(2,1)S(1)}, u32[]{:S(2)}, u32[]{:S(2)}) collective-permute-start(bf16[256,256]{1,0:T(8,128)(2,1)S(1)} %broadcast_select_fusion), channel_id=1, source_target_pairs={{0,2},{1,3},{2,4},{3,5},{4,6},{5,7},{6,8},{7,9},{8,10},{9,11},{10,... | collective-permute-start | bytes 393224 | tf_op jit(solution)/shard_map/ppermute | solution.py:430
  14.9 8.7 %collective-permute-start.7 = (bf16[256,256]{1,0:T(8,128)(2,1)S(1)}, bf16[256,256]{1,0:T(8,128)(2,1)S(1)}, u32[]{:S(2)}, u32[]{:S(2)}) collective-permute-start(bf16[256,256]{1,0:T(8,128)(2,1)S(1)} %collective-permute-done.6.kv2), channel_id=1, source_target_pairs={{0,4},{1,5},{2,6},{3,7},{4,8},{5,9},{6,10},{7,11},{8,12},{9,13},{1... | collective-permute-start | bytes 393224 | tf_op jit(solution)/shard_map/ppermute | solution.py:430
  14.9 8.7 %collective-permute-start.9 = (bf16[256,256]{1,0:T(8,128)(2,1)S(1)}, bf16[256,256]{1,0:T(8,128)(2,1)S(1)}, u32[]{:S(2)}, u32[]{:S(2)}) collective-permute-start(bf16[256,256]{1,0:T(8,128)(2,1)S(1)} %collective-permute-done.6.kv2), channel_id=1, source_target_pairs={{0,2},{1,3},{2,0},{3,1},{4,6},{5,7},{6,4},{7,5},{8,10},{9,11},{10,... | collective-permute-start | bytes 393224 | tf_op jit(solution)/shard_map/ppermute | solution.py:436
  16.2 18.7 %collective-permute-start.4 = (bf16[256,256]{1,0:T(8,128)(2,1)S(1)}, bf16[256,256]{1,0:T(8,128)(2,1)S(1)}, u32[]{:S(2)}, u32[]{:S(2)}) collective-permute-start(bf16[256,256]{1,0:T(8,128)(2,1)S(1)} %broadcast_select_fusion.1), channel_id=1, source_target_pairs={{0,2},{1,3},{2,4},{3,5},{4,6},{5,7},{6,8},{7,9},{8,10},{9,11},{10,... | collective-permute-start | bytes 393224 | tf_op jit(solution)/shard_map/ppermute | solution.py:430
  17.2 20.2 %collective-permute-start.3 = (bf16[256,256]{1,0:T(8,128)(2,1)S(1)}, bf16[256,256]{1,0:T(8,128)(2,1)S(1)}, u32[]{:S(2)}, u32[]{:S(2)}) collective-permute-start(bf16[256,256]{1,0:T(8,128)(2,1)S(1)} %collective-permute-done.2.kv2), channel_id=1, source_target_pairs={{0,4},{1,5},{2,6},{3,7},{4,8},{5,9},{6,10},{7,11},{8,12},{9,13},{1... | collective-permute-start | bytes 393224 | tf_op jit(solution)/shard_map/ppermute | solution.py:430
  22.3 15.0 %collective-permute-start.5 = (bf16[256,256]{1,0:T(8,128)(2,1)S(1)}, bf16[256,256]{1,0:T(8,128)(2,1)S(1)}, u32[]{:S(2)}, u32[]{:S(2)}) collective-permute-start(bf16[256,256]{1,0:T(8,128)(2,1)S(1)} %collective-permute-done.2.kv2), channel_id=1, source_target_pairs={{0,2},{1,3},{2,0},{3,1},{4,6},{5,7},{6,4},{7,5},{8,10},{9,11},{10,... | collective-permute-start | bytes 393224 | tf_op jit(solution)/shard_map/ppermute | solution.py:436
  28.8 18.6 %collective-permute-start.12 = (bf16[256,256]{1,0:T(8,128)(2,1)S(1)}, bf16[256,256]{1,0:T(8,128)(2,1)S(1)}, u32[]{:S(2)}, u32[]{:S(2)}) collective-permute-start(bf16[256,256]{1,0:T(8,128)(2,1)S(1)} %get-tuple-element.49), channel_id=1, source_target_pairs={{0,14},{1,15},{2,0},{3,1},{4,2},{5,3},{6,4},{7,5},{8,6},{9,7},{10,... | collective-permute-start | bytes 393224 | tf_op jit(solution)/shard_map/ppermute | solution.py:430
  34.9 14.5 %collective-permute-start.13 = (bf16[256,256]{1,0:T(8,128)(2,1)S(1)}, bf16[256,256]{1,0:T(8,128)(2,1)S(1)}, u32[]{:S(2)}, u32[]{:S(2)}) collective-permute-start(bf16[256,256]{1,0:T(8,128)(2,1)S(1)} %get-tuple-element.51), channel_id=1, source_target_pairs={{0,2},{1,3},{2,0},{3,1},{4,6},{5,7},{6,4},{7,5},{8,10},{9,11},{10,... | collective-permute-start | bytes 393224 | tf_op jit(solution)/shard_map/ppermute | solution.py:436
  34.9 14.5 %collective-permute-start.14 = (bf16[256,256]{1,0:T(8,128)(2,1)S(1)}, bf16[256,256]{1,0:T(8,128)(2,1)S(1)}, u32[]{:S(2)}, u32[]{:S(2)}) collective-permute-start(bf16[256,256]{1,0:T(8,128)(2,1)S(1)} %get-tuple-element.52), channel_id=1, source_target_pairs={{0,12},{1,13},{2,14},{3,15},{4,0},{5,1},{6,2},{7,3},{8,4},{9,5},{1... | collective-permute-start | bytes 393224 | tf_op jit(solution)/shard_map/ppermute | solution.py:430
  42.6 7.4 %collective-permute-start.16 = (bf16[256,256]{1,0:T(8,128)(2,1)S(1)}, bf16[256,256]{1,0:T(8,128)(2,1)S(1)}, u32[]{:S(2)}, u32[]{:S(2)}) collective-permute-start(bf16[256,256]{1,0:T(8,128)(2,1)S(1)} %get-tuple-element.54), channel_id=1, source_target_pairs={{0,14},{1,15},{2,0},{3,1},{4,2},{5,3},{6,4},{7,5},{8,6},{9,7},{10,... | collective-permute-start | bytes 393224 | tf_op jit(solution)/shard_map/ppermute | solution.py:430
  47.4 5.0 %collective-permute-start.17 = (bf16[256,256]{1,0:T(8,128)(2,1)S(1)}, bf16[256,256]{1,0:T(8,128)(2,1)S(1)}, u32[]{:S(2)}, u32[]{:S(2)}) collective-permute-start(bf16[256,256]{1,0:T(8,128)(2,1)S(1)} %get-tuple-element.56), channel_id=1, source_target_pairs={{0,2},{1,3},{2,0},{3,1},{4,6},{5,7},{6,4},{7,5},{8,10},{9,11},{10,... | collective-permute-start | bytes 393224 | tf_op jit(solution)/shard_map/ppermute | solution.py:436
  47.4 5.0 %collective-permute-start.18 = (bf16[256,256]{1,0:T(8,128)(2,1)S(1)}, bf16[256,256]{1,0:T(8,128)(2,1)S(1)}, u32[]{:S(2)}, u32[]{:S(2)}) collective-permute-start(bf16[256,256]{1,0:T(8,128)(2,1)S(1)} %get-tuple-element.57), channel_id=1, source_target_pairs={{0,12},{1,13},{2,14},{3,15},{4,0},{5,1},{6,2},{7,3},{8,4},{9,5},{1... | collective-permute-start | bytes 393224 | tf_op jit(solution)/shard_map/ppermute | solution.py:430
  49.4 11.3 %collective-permute-start.11 = (bf16[128,2048]{1,0:T(8,128)(2,1)S(1)}, bf16[128,2048]{1,0:T(8,128)(2,1)S(1)}, u32[]{:S(2)}, u32[]{:S(2)}) collective-permute-start(bf16[128,2048]{1,0:T(8,128)(2,1)S(1)} %get-tuple-element.47), channel_id=1, source_target_pairs={{0,1},{1,0},{2,3},{3,2},{4,5},{5,4},{6,7},{7,6},{8,9},{9,8},{10,11... | collective-permute-start | bytes 1572872 | tf_op jit(solution)/shard_map/ppermute | solution.py:433
  49.4 11.3 %collective-permute-start.10 = (bf16[128,2048]{1,0:T(8,128)(2,1)S(1)}, bf16[128,2048]{1,0:T(8,128)(2,1)S(1)}, u32[]{:S(2)}, u32[]{:S(2)}) collective-permute-start(bf16[128,2048]{1,0:T(8,128)(2,1)S(1)} %get-tuple-element.46), channel_id=1, source_target_pairs={{0,1},{1,0},{2,3},{3,2},{4,5},{5,4},{6,7},{7,6},{8,9},{9,8},{10,11... | collective-permute-start | bytes 1572872 | tf_op jit(solution)/shard_map/ppermute | solution.py:433
  50.0 6.4 %collective-permute-start.15 = (bf16[256,256]{1,0:T(8,128)(2,1)S(1)}, bf16[256,256]{1,0:T(8,128)(2,1)S(1)}, u32[]{:S(2)}, u32[]{:S(2)}) collective-permute-start(bf16[256,256]{1,0:T(8,128)(2,1)S(1)} %fusion.4), channel_id=1, source_target_pairs={{0,12},{1,13},{2,14},{3,15},{4,0},{5,1},{6,2},{7,3},{8,4},{9,5},{1... | collective-permute-start | bytes 393224 | tf_op jit(solution)/shard_map/ppermute | solution.py:430
  52.4 6.7 %collective-permute-start.19 = (bf16[256,256]{1,0:T(8,128)(2,1)S(1)}, bf16[256,256]{1,0:T(8,128)(2,1)S(1)}, u32[]{:S(2)}, u32[]{:S(2)}) collective-permute-start(bf16[256,256]{1,0:T(8,128)(2,1)S(1)} %fusion.9), channel_id=1, source_target_pairs={{0,12},{1,13},{2,14},{3,15},{4,0},{5,1},{6,2},{7,3},{8,4},{9,5},{1... | collective-permute-start | bytes 393224 | tf_op jit(solution)/shard_map/ppermute | solution.py:430
  59.3 1.4 %collective-permute-start.20 = (bf16[128,512]{1,0:T(8,128)(2,1)S(1)}, bf16[128,512]{1,0:T(8,128)(2,1)S(1)}, u32[]{:S(2)}, u32[]{:S(2)}) collective-permute-start(bf16[128,512]{1,0:T(8,128)(2,1)S(1)} %get-tuple-element.58), channel_id=1, source_target_pairs={{0,1},{1,0},{2,3},{3,2},{4,5},{5,4},{6,7},{7,6},{8,9},{9,8},{10,11... | collective-permute-start | bytes 393224 | tf_op jit(solution)/shard_map/ppermute | solution.py:433

commit v3 on v2

--- a/solution.py
+++ b/solution.py
@@ -137,7 +137,7 @@
     middle = pl.multiple_of(jnp.where(even, 3 * two, two), two)
     places = [pl.ds(at, two) for at in (0, edge, 2 * two, middle, 4 * two)]
 
-    def attend(blocks, step):
+    def attend(blocks):
         whole = blocks == 2 * CHUNKS - 1
         k_aug[:, width:] = k_seg[...]
         for at, kv in zip(places, (kv4, kv_edge, kv2, kv_middle, kv0)):
@@ -161,14 +161,15 @@
         def fold(x, op):
             return op(x.reshape(x.shape[0] // 8, 8, x.shape[1]), axis=0)
 
-        def scores(u, b, top):
-            first, _ = window(u)
-            s = dot(k_aug[first + b * rows:first + (b + step) * rows], q_t[base + u])
-            for i in range(step):
-                part = s[i * rows:(i + 1) * rows]
-                if b + i == blocks - 1:
+        def scores(u, top):
+            _, keys = window(u)
+            s = dot(k_aug[keys], q_t[base + u])
+            for b in range(blocks):
+                here = slice(b * rows, (b + 1) * rows)
+                part = s[here]
+                if b == blocks - 1:
                     part = jnp.where(causal, part, MASKED)
-                s_scr[u % 2, (b + i) * rows:(b + i + 1) * rows] = part
+                s_scr[u % 2, here] = part
                 top = jnp.maximum(top, fold(part, jnp.max))
             return top
 
@@ -177,9 +178,8 @@
             e = jnp.exp2((s_scr[u % 2, b * rows:(b + 1) * rows] - peak) * (scale * math.log2(math.e)))
             p_scr[first + b * rows:first + (b + 1) * rows, columns(u)] = e.astype(BF)
 
-        def score_grads(u, b, inner):
-            first, _ = window(u)
-            keys = slice(first + b * rows, first + (b + step) * rows)
+        def score_grads(u, inner):
+            _, keys = window(u)
             dp = dot(v_win[keys], g_t[base + u])
             d_scr[keys, columns(u)] = p_scr[keys, columns(u)] * (dp - inner).astype(BF)
 
@@ -223,17 +223,19 @@
 
         def turn(u, peak, inv, inner):
             top = jnp.full((8, two), MASKED, F32)
-            for b in range(0, blocks, step):
-                if u + 1 < units:
-                    top = scores(u + 1, b, top)
-                if 0 <= u < units:
-                    for i in range(step):
-                        weights(u, b + i, peak)
-                if u > 0:
-                    score_grads(u - 1, b, inner)
+            if u + 1 < units:
+                top = scores(u + 1, top)
+            key_grads(u)
+            if 0 <= u < units:
+                for b in range(blocks):
+                    weights(u, b, peak)
+                    if b % 3 == 2:
+                        key_grads(u)
+            if u > 0:
+                score_grads(u - 1, inner)
+            if u + 1 >= units:
                 key_grads(u)
-                if u + 1 >= units:
-                    key_grads(u)
+                key_grads(u)
             if u > 0:
                 query_grad(u - 1, inv)
             if 0 <= u < units:
@@ -261,28 +263,24 @@
         for left, right, acc, factor, col in sums:
             cols = slice(col, col + width)
             late = 3 * two
-            if not whole:
+            if whole:
+                acc[rows:] += dot(left[rows:, part:], right[part:])
+            else:
                 acc[:late] = jnp.zeros((late, width), F32)
                 acc[late:] = dot(left[late:, half:], right[half:])
                 acc[late:late + 3 * rows] += dot(left[late:late + 3 * rows, :half], right[:half])
-
-            def total(keys):
-                return factor * (acc[keys] + dot(left[keys, part:], right[part:]) if whole else acc[keys])
-
-            d4[:rows, cols] = (factor * acc[:rows]).astype(d4.dtype)
-            d4[rows:, cols] = total(slice(rows, two)).astype(d4.dtype)
-            for at, out in zip(places[1:], (d_edge, d2, d_middle, d0)):
-                out[:, cols] = total(at).astype(out.dtype)
+            for at, out in zip(places, (d4, d_edge, d2, d_middle, d0)):
+                out[:, cols] = (factor * acc[at]).astype(out.dtype)
         for copy in copies:
             copy.wait()
 
     @pl.when(chip >= 2)
     def _():
-        attend(2 * CHUNKS - 1, 3)
+        attend(2 * CHUNKS - 1)
 
     @pl.when(chip < 2)
     def _():
-        attend(4, 2)
+        attend(4)
 
 
 def place_kernel(heads, o_in, dq_in, *refs):

time: 62.2 us -> 63.1 us (1.014)
    ppermute x12, starting transfers between devices: 29.8 us -> 30.5 us  [shift(): return lax.ppermute(x, 'context', [(i, (i + by) % n) for i in range(n)])]
where the time goes in v3:
time: 63.1 us; the launch traced here: 62.9 us
  starting transfers between devices  34.5 us (55%)
  Pallas kernels  15.6 us (25%)
  waiting for transfers between devices  11.5 us (18%)
  between operations  0.94 us (1%)
    ppermute x12, starting transfers between devices, shift(): return lax.ppermute(x, 'context', [(i, (i + by) % n) for i in range(n)])  30.5 us
    pallas_call x2, Pallas kernels, head_attention(): pl.pallas_call(functools.partial(attention_kernel, slot, heads), in_specs...  10.8 us
    ppermute x12, waiting for transfers between devices, shift(): return lax.ppermute(x, 'context', [(i, (i + by) % n) for i in range(n)])  9.14 us
    ppermute x4, starting transfers between devices, across(): return lax.ppermute(x, 'context', [(i, i ^ 2) for i in range(n)])  2.54 us
    ppermute x5, waiting for transfers between devices, swap(): return lax.ppermute(x, 'context', [(i, i ^ 1) for i in range(n)])  2.33 us
    pallas_call x1, Pallas kernels, staged(): pl.pallas_call(functools.partial(stage_kernel, heads), in_specs=[ANYWHERE...  2.29 us
    ppermute x5, starting transfers between devices, swap(): return lax.ppermute(x, 'context', [(i, i ^ 1) for i in range(n)])  1.52 us
    pallas_call x1, Pallas kernels, shares(): pl.pallas_call(share_kernel, in_specs=[ANYWHERE] * 4, out_specs=[VMEM] *...  1.41 us
  transfers between devices with their start and end apart: 21, of which 5 were waited for; matrix products, arithmetic and copies ran while one was open for 1% of the time, Pallas kernels for 21%

profile of v3, /device:TPU:0, one launch (start us, length us, event | category | flops | bytes accessed | tf_op | source)
XLA Modules:
  0.0 62.9 jit_solution(3427410551899880406)
XLA Ops:
  0.6 1.4 %share.1 = (bf16[128,512]{1,0:T(8,128)(2,1)S(1)}, bf16[128,512]{1,0:T(8,128)(2,1)S(1)}, bf16[128,4096]{1,0:T(8,128)(2,1)S(1)}) custom-call(bf16[128,512]{1,0:T(8,128)(2,1)} %k.1, bf16[128,512]{1,0:T(8,128)(2,1)} %v.1, bf16[128,4096]{1,0:T(8,128)(2,1)} %q_all.1, bf16[128,4096]{1,0:T(8,128)(2,1)} %g_all.1), custom_call_target="tpu_custom_call" | custom-call | tf_op jit(solution)/shard_map/share/pallas_call | solution.py:304
  2.0 0.5 collective-permute-start
  2.6 1.0 %collective-permute-done.kv_oth = bf16[128,512]{1,0:T(8,128)(2,1)S(1)} collective-permute-done((bf16[128,512]{1,0:T(8,128)(2,1)S(1)}, bf16[128,512]{1,0:T(8,128)(2,1)S(1)}, u32[]{:S(2)}, u32[]{:S(2)}) %collective-permute-start) | collective-permute-done | bytes 131104 | tf_op jit(solution)/shard_map/ppermute | solution.py:431
  4.0 2.7 %collective-permute-start.6 = (bf16[256,256]{1,0:T(8,128)(2,1)S(1)}, bf16[256,256]{1,0:T(8,128)(2,1)S(1)}, u32[]{:S(2)}, u32[]{:S(2)}) collective-permute-start(bf16[256,256]{1,0:T(8,128)(2,1)S(1)} %get-tuple-element.41.kv0), channel_id=1, source_target_pairs={{0,4},{1,5},{2,6},{3,7},{4,8},{5,9},{6,10},{7,11},{8,12},{9,13},{1... | collective-permute-start | bytes 393224 | tf_op jit(solution)/shard_map/ppermute | solution.py:428
  6.8 1.6 %collective-permute-start.2 = (bf16[256,256]{1,0:T(8,128)(2,1)S(1)}, bf16[256,256]{1,0:T(8,128)(2,1)S(1)}, u32[]{:S(2)}, u32[]{:S(2)}) collective-permute-start(bf16[256,256]{1,0:T(8,128)(2,1)S(1)} %get-tuple-element.40.kv0), channel_id=1, source_target_pairs={{0,4},{1,5},{2,6},{3,7},{4,8},{5,9},{6,10},{7,11},{8,12},{9,13},{1... | collective-permute-start | bytes 393224 | tf_op jit(solution)/shard_map/ppermute | solution.py:428
  8.3 4.8 %collective-permute-done.6.kv2 = bf16[256,256]{1,0:T(8,128)(2,1)S(1)} collective-permute-done((bf16[256,256]{1,0:T(8,128)(2,1)S(1)}, bf16[256,256]{1,0:T(8,128)(2,1)S(1)}, u32[]{:S(2)}, u32[]{:S(2)}) %collective-permute-start.6) | collective-permute-done | bytes 131104 | tf_op jit(solution)/shard_map/ppermute | solution.py:428
  13.1 1.7 %collective-permute-start.8 = (bf16[256,256]{1,0:T(8,128)(2,1)S(1)}, bf16[256,256]{1,0:T(8,128)(2,1)S(1)}, u32[]{:S(2)}, u32[]{:S(2)}) collective-permute-start(bf16[256,256]{1,0:T(8,128)(2,1)S(1)} %broadcast_select_fusion), channel_id=1, source_target_pairs={{0,2},{1,3},{2,4},{3,5},{4,6},{5,7},{6,8},{7,9},{8,10},{9,11},{10,... | collective-permute-start | bytes 393224 | tf_op jit(solution)/shard_map/ppermute | solution.py:428
  14.9 1.3 %collective-permute-start.9 = (bf16[256,256]{1,0:T(8,128)(2,1)S(1)}, bf16[256,256]{1,0:T(8,128)(2,1)S(1)}, u32[]{:S(2)}, u32[]{:S(2)}) collective-permute-start(bf16[256,256]{1,0:T(8,128)(2,1)S(1)} %collective-permute-done.6.kv2), channel_id=1, source_target_pairs={{0,2},{1,3},{2,0},{3,1},{4,6},{5,7},{6,4},{7,5},{8,10},{9,11},{10,... | collective-permute-start | bytes 393224 | tf_op jit(solution)/shard_map/ppermute | solution.py:434
  16.2 1.0 %collective-permute-start.4 = (bf16[256,256]{1,0:T(8,128)(2,1)S(1)}, bf16[256,256]{1,0:T(8,128)(2,1)S(1)}, u32[]{:S(2)}, u32[]{:S(2)}) collective-permute-start(bf16[256,256]{1,0:T(8,128)(2,1)S(1)} %broadcast_select_fusion.1), channel_id=1, source_target_pairs={{0,2},{1,3},{2,4},{3,5},{4,6},{5,7},{6,8},{7,9},{8,10},{9,11},{10,... | collective-permute-start | bytes 393224 | tf_op jit(solution)/shard_map/ppermute | solution.py:428
  17.2 1.2 %collective-permute-start.3 = (bf16[256,256]{1,0:T(8,128)(2,1)S(1)}, bf16[256,256]{1,0:T(8,128)(2,1)S(1)}, u32[]{:S(2)}, u32[]{:S(2)}) collective-permute-start(bf16[256,256]{1,0:T(8,128)(2,1)S(1)} %collective-permute-done.2.kv2), channel_id=1, source_target_pairs={{0,4},{1,5},{2,6},{3,7},{4,8},{5,9},{6,10},{7,11},{8,12},{9,13},{1... | collective-permute-start | bytes 393224 | tf_op jit(solution)/shard_map/ppermute | solution.py:428
  18.3 2.3 %stage.1 = (bf16[4096,128]{1,0:T(8,128)(2,1)S(1)}, bf16[4096,128]{1,0:T(8,128)(2,1)S(1)}, bf16[16,256,256]{2,1,0:T(8,128)(2,1)S(1)}, bf16[16,128,256]{2,1,0:T(8,128)(2,1)S(1)}, bf16[1280,128]{1,0:T(8,128)(2,1)S(1)}) custom-call(s32[5]{0:T(128)} %bounds_in.1, bf16[128,4096]{1,0:T(8,128)(2,1)} %q_all.1, bf16[128,4096]{1,0:T(8,128)(2,1)} %g_all.1, ...), custom_call_target="tpu_custom_call" | custom-call | bytes 4194304 | tf_op jit(solution)/shard_map/stage/pallas_call | solution.py:332
  20.6 1.7 %collective-permute-done.8.kv_edge = bf16[256,256]{1,0:T(8,128)(2,1)S(1)} collective-permute-done((bf16[256,256]{1,0:T(8,128)(2,1)S(1)}, bf16[256,256]{1,0:T(8,128)(2,1)S(1)}, u32[]{:S(2)}, u32[]{:S(2)}) %collective-permute-start.8) | collective-permute-done | bytes 131104 | tf_op jit(solution)/shard_map/ppermute | solution.py:428
  22.3 1.2 %collective-permute-start.5 = (bf16[256,256]{1,0:T(8,128)(2,1)S(1)}, bf16[256,256]{1,0:T(8,128)(2,1)S(1)}, u32[]{:S(2)}, u32[]{:S(2)}) collective-permute-start(bf16[256,256]{1,0:T(8,128)(2,1)S(1)} %collective-permute-done.2.kv2), channel_id=1, source_target_pairs={{0,2},{1,3},{2,0},{3,1},{4,6},{5,7},{6,4},{7,5},{8,10},{9,11},{10,... | collective-permute-start | bytes 393224 | tf_op jit(solution)/shard_map/ppermute | solution.py:434
  23.5 5.4 %attention0.1 = (bf16[128,4096]{1,0:T(8,128)(2,1)}, bf16[128,4096]{1,0:T(8,128)(2,1)}, bf16[128,2048]{1,0:T(8,128)(2,1)S(1)}, bf16[256,256]{1,0:T(8,128)(2,1)S(1...) custom-call(bf16[4096,128]{1,0:T(8,128)(2,1)S(1)} %get-tuple-element, ...), custom_call_target="tpu_custom_call" | custom-call | flops 3355443200 | bytes 3145728 | tf_op jit(solution)/shard_map/attention0/pallas_call | solution.py:364
  28.9 6.5 %collective-permute-start.12 = (bf16[256,256]{1,0:T(8,128)(2,1)S(1)}, bf16[256,256]{1,0:T(8,128)(2,1)S(1)}, u32[]{:S(2)}, u32[]{:S(2)}) collective-permute-start(bf16[256,256]{1,0:T(8,128)(2,1)S(1)} %get-tuple-element.49), channel_id=1, source_target_pairs={{0,14},{1,15},{2,0},{3,1},{4,2},{5,3},{6,4},{7,5},{8,6},{9,7},{10,... | collective-permute-start | bytes 393224 | tf_op jit(solution)/shard_map/ppermute | solution.py:428
  35.4 2.4 %collective-permute-start.14 = (bf16[256,256]{1,0:T(8,128)(2,1)S(1)}, bf16[256,256]{1,0:T(8,128)(2,1)S(1)}, u32[]{:S(2)}, u32[]{:S(2)}) collective-permute-start(bf16[256,256]{1,0:T(8,128)(2,1)S(1)} %get-tuple-element.52), channel_id=1, source_target_pairs={{0,12},{1,13},{2,14},{3,15},{4,0},{5,1},{6,2},{7,3},{8,4},{9,5},{1... | collective-permute-start | bytes 393224 | tf_op jit(solution)/shard_map/ppermute | solution.py:428
  37.8 5.4 %attention1.1 = (bf16[128,4096]{1,0:T(8,128)(2,1)}, bf16[128,4096]{1,0:T(8,128)(2,1)}, bf16[128,2048]{1,0:T(8,128)(2,1)S(1)}, bf16[256,256]{1,0:T(8,128)(2,1)S(1...) custom-call(bf16[4096,128]{1,0:T(8,128)(2,1)S(1)} %get-tuple-element, ...), custom_call_target="tpu_custom_call", output_to_operand_aliasing={{0}: (10, {}), {1}: (11, {})} | custom-call | flops 3355443200 | bytes 3145728 | tf_op jit(solution)/shard_map/attention1/pallas_call | solution.py:364
  43.2 5.0 %collective-permute-start.16 = (bf16[256,256]{1,0:T(8,128)(2,1)S(1)}, bf16[256,256]{1,0:T(8,128)(2,1)S(1)}, u32[]{:S(2)}, u32[]{:S(2)}) collective-permute-start(bf16[256,256]{1,0:T(8,128)(2,1)S(1)} %get-tuple-element.54), channel_id=1, source_target_pairs={{0,14},{1,15},{2,0},{3,1},{4,2},{5,3},{6,4},{7,5},{8,6},{9,7},{10,... | collective-permute-start | bytes 393224 | tf_op jit(solution)/shard_map/ppermute | solution.py:428
  48.3 2.1 %collective-permute-start.18 = (bf16[256,256]{1,0:T(8,128)(2,1)S(1)}, bf16[256,256]{1,0:T(8,128)(2,1)S(1)}, u32[]{:S(2)}, u32[]{:S(2)}) collective-permute-start(bf16[256,256]{1,0:T(8,128)(2,1)S(1)} %get-tuple-element.57), channel_id=1, source_target_pairs={{0,12},{1,13},{2,14},{3,15},{4,0},{5,1},{6,2},{7,3},{8,4},{9,5},{1... | collective-permute-start | bytes 393224 | tf_op jit(solution)/shard_map/ppermute | solution.py:428
  50.9 2.3 %collective-permute-start.15 = (bf16[256,256]{1,0:T(8,128)(2,1)S(1)}, bf16[256,256]{1,0:T(8,128)(2,1)S(1)}, u32[]{:S(2)}, u32[]{:S(2)}) collective-permute-start(bf16[256,256]{1,0:T(8,128)(2,1)S(1)} %fusion.4), channel_id=1, source_target_pairs={{0,12},{1,13},{2,14},{3,15},{4,0},{5,1},{6,2},{7,3},{8,4},{9,5},{1... | collective-permute-start | bytes 393224 | tf_op jit(solution)/shard_map/ppermute | solution.py:428
  53.4 4.0 %collective-permute-start.19 = (bf16[256,256]{1,0:T(8,128)(2,1)S(1)}, bf16[256,256]{1,0:T(8,128)(2,1)S(1)}, u32[]{:S(2)}, u32[]{:S(2)}) collective-permute-start(bf16[256,256]{1,0:T(8,128)(2,1)S(1)} %fusion.9), channel_id=1, source_target_pairs={{0,12},{1,13},{2,14},{3,15},{4,0},{5,1},{6,2},{7,3},{8,4},{9,5},{1... | collective-permute-start | bytes 393224 | tf_op jit(solution)/shard_map/ppermute | solution.py:428
  57.4 2.6 %collective-permute-done.19 = bf16[256,256]{1,0:T(8,128)(2,1)S(1)} collective-permute-done((bf16[256,256]{1,0:T(8,128)(2,1)S(1)}, bf16[256,256]{1,0:T(8,128)(2,1)S(1)}, u32[]{:S(2)}, u32[]{:S(2)}) %collective-permute-start.19) | collective-permute-done | bytes 131104 | tf_op jit(solution)/shard_map/ppermute | solution.py:428
  60.3 1.3 %collective-permute-done.20.refs_3_ = bf16[128,512]{1,0:T(8,128)(2,1)S(1)} collective-permute-done((bf16[128,512]{1,0:T(8,128)(2,1)S(1)}, bf16[128,512]{1,0:T(8,128)(2,1)S(1)}, u32[]{:S(2)}, u32[]{:S(2)}) %collective-permute-start.20) | collective-permute-done | bytes 131104 | tf_op jit(solution)/shard_map/ppermute | solution.py:431
  61.6 1.1 %place.1 = (bf16[128,4096]{1,0:T(8,128)(2,1)}, bf16[128,4096]{1,0:T(8,128)(2,1)}, bf16[128,512]{1,0:T(8,128)(2,1)}, bf16[128,512]{1,0:T(8,128)(2,1)}) custom-call(bf16[128,4096]{1,0:T(8,128)(2,1)} %get-tuple-element.44.o_in, bf16[128,4096]{1,0:T(8,128)(2,1)} %get-tuple-element.45.dq_in, ...), custom_call_target="tpu_custom_call", output_to_operand_aliasing={{0}: (0, {}), {1}: (1, {})} | custom-call | tf_op jit(solution)/shard_map/place/pallas_call | solution.py:402
  (34 shorter events, 1.5 us)
Async XLA Ops:
  2.0 1.5 %collective-permute-start = (bf16[128,512]{1,0:T(8,128)(2,1)S(1)}, bf16[128,512]{1,0:T(8,128)(2,1)S(1)}, u32[]{:S(2)}, u32[]{:S(2)}) collective-permute-start(bf16[128,512]{1,0:T(8,128)(2,1)S(1)} %get-tuple-element.32), channel_id=1, source_target_pairs={{0,1},{1,0},{2,3},{3,2},{4,5},{5,4},{6,7},{7,6},{8,9},{9,8},{10,11... | collective-permute-start | bytes 393224 | tf_op jit(solution)/shard_map/ppermute | solution.py:431
  3.6 13.6 %collective-permute-start.1 = (bf16[128,4096]{1,0:T(8,128)(2,1)S(1)}, bf16[128,4096]{1,0:T(8,128)(2,1)S(1)}, u32[]{:S(2)}, u32[]{:S(2)}) collective-permute-start(bf16[128,4096]{1,0:T(8,128)(2,1)S(1)} %get-tuple-element.34), channel_id=1, source_target_pairs={{0,1},{1,0},{2,3},{3,2},{4,5},{5,4},{6,7},{7,6},{8,9},{9,8},{10,11... | collective-permute-start | bytes 3145736 | tf_op jit(solution)/shard_map/ppermute | solution.py:431
  4.0 9.1 %collective-permute-start.6 = (bf16[256,256]{1,0:T(8,128)(2,1)S(1)}, bf16[256,256]{1,0:T(8,128)(2,1)S(1)}, u32[]{:S(2)}, u32[]{:S(2)}) collective-permute-start(bf16[256,256]{1,0:T(8,128)(2,1)S(1)} %get-tuple-element.41.kv0), channel_id=1, source_target_pairs={{0,4},{1,5},{2,6},{3,7},{4,8},{5,9},{6,10},{7,11},{8,12},{9,13},{1... | collective-permute-start | bytes 393224 | tf_op jit(solution)/shard_map/ppermute | solution.py:428
  6.8 9.4 %collective-permute-start.2 = (bf16[256,256]{1,0:T(8,128)(2,1)S(1)}, bf16[256,256]{1,0:T(8,128)(2,1)S(1)}, u32[]{:S(2)}, u32[]{:S(2)}) collective-permute-start(bf16[256,256]{1,0:T(8,128)(2,1)S(1)} %get-tuple-element.40.kv0), channel_id=1, source_target_pairs={{0,4},{1,5},{2,6},{3,7},{4,8},{5,9},{6,10},{7,11},{8,12},{9,13},{1... | collective-permute-start | bytes 393224 | tf_op jit(solution)/shard_map/ppermute | solution.py:428
  13.1 9.2 %collective-permute-start.8 = (bf16[256,256]{1,0:T(8,128)(2,1)S(1)}, bf16[256,256]{1,0:T(8,128)(2,1)S(1)}, u32[]{:S(2)}, u32[]{:S(2)}) collective-permute-start(bf16[256,256]{1,0:T(8,128)(2,1)S(1)} %broadcast_select_fusion), channel_id=1, source_target_pairs={{0,2},{1,3},{2,4},{3,5},{4,6},{5,7},{6,8},{7,9},{8,10},{9,11},{10,... | collective-permute-start | bytes 393224 | tf_op jit(solution)/shard_map/ppermute | solution.py:428
  14.9 8.7 %collective-permute-start.7 = (bf16[256,256]{1,0:T(8,128)(2,1)S(1)}, bf16[256,256]{1,0:T(8,128)(2,1)S(1)}, u32[]{:S(2)}, u32[]{:S(2)}) collective-permute-start(bf16[256,256]{1,0:T(8,128)(2,1)S(1)} %collective-permute-done.6.kv2), channel_id=1, source_target_pairs={{0,4},{1,5},{2,6},{3,7},{4,8},{5,9},{6,10},{7,11},{8,12},{9,13},{1... | collective-permute-start | bytes 393224 | tf_op jit(solution)/shard_map/ppermute | solution.py:428
  14.9 8.7 %collective-permute-start.9 = (bf16[256,256]{1,0:T(8,128)(2,1)S(1)}, bf16[256,256]{1,0:T(8,128)(2,1)S(1)}, u32[]{:S(2)}, u32[]{:S(2)}) collective-permute-start(bf16[256,256]{1,0:T(8,128)(2,1)S(1)} %collective-permute-done.6.kv2), channel_id=1, source_target_pairs={{0,2},{1,3},{2,0},{3,1},{4,6},{5,7},{6,4},{7,5},{8,10},{9,11},{10,... | collective-permute-start | bytes 393224 | tf_op jit(solution)/shard_map/ppermute | solution.py:434
  16.2 19.2 %collective-permute-start.4 = (bf16[256,256]{1,0:T(8,128)(2,1)S(1)}, bf16[256,256]{1,0:T(8,128)(2,1)S(1)}, u32[]{:S(2)}, u32[]{:S(2)}) collective-permute-start(bf16[256,256]{1,0:T(8,128)(2,1)S(1)} %broadcast_select_fusion.1), channel_id=1, source_target_pairs={{0,2},{1,3},{2,4},{3,5},{4,6},{5,7},{6,8},{7,9},{8,10},{9,11},{10,... | collective-permute-start | bytes 393224 | tf_op jit(solution)/shard_map/ppermute | solution.py:428
  17.2 20.7 %collective-permute-start.3 = (bf16[256,256]{1,0:T(8,128)(2,1)S(1)}, bf16[256,256]{1,0:T(8,128)(2,1)S(1)}, u32[]{:S(2)}, u32[]{:S(2)}) collective-permute-start(bf16[256,256]{1,0:T(8,128)(2,1)S(1)} %collective-permute-done.2.kv2), channel_id=1, source_target_pairs={{0,4},{1,5},{2,6},{3,7},{4,8},{5,9},{6,10},{7,11},{8,12},{9,13},{1... | collective-permute-start | bytes 393224 | tf_op jit(solution)/shard_map/ppermute | solution.py:428
  22.3 15.5 %collective-permute-start.5 = (bf16[256,256]{1,0:T(8,128)(2,1)S(1)}, bf16[256,256]{1,0:T(8,128)(2,1)S(1)}, u32[]{:S(2)}, u32[]{:S(2)}) collective-permute-start(bf16[256,256]{1,0:T(8,128)(2,1)S(1)} %collective-permute-done.2.kv2), channel_id=1, source_target_pairs={{0,2},{1,3},{2,0},{3,1},{4,6},{5,7},{6,4},{7,5},{8,10},{9,11},{10,... | collective-permute-start | bytes 393224 | tf_op jit(solution)/shard_map/ppermute | solution.py:434
  28.9 19.4 %collective-permute-start.12 = (bf16[256,256]{1,0:T(8,128)(2,1)S(1)}, bf16[256,256]{1,0:T(8,128)(2,1)S(1)}, u32[]{:S(2)}, u32[]{:S(2)}) collective-permute-start(bf16[256,256]{1,0:T(8,128)(2,1)S(1)} %get-tuple-element.49), channel_id=1, source_target_pairs={{0,14},{1,15},{2,0},{3,1},{4,2},{5,3},{6,4},{7,5},{8,6},{9,7},{10,... | collective-permute-start | bytes 393224 | tf_op jit(solution)/shard_map/ppermute | solution.py:428
  35.4 15.0 %collective-permute-start.13 = (bf16[256,256]{1,0:T(8,128)(2,1)S(1)}, bf16[256,256]{1,0:T(8,128)(2,1)S(1)}, u32[]{:S(2)}, u32[]{:S(2)}) collective-permute-start(bf16[256,256]{1,0:T(8,128)(2,1)S(1)} %get-tuple-element.51), channel_id=1, source_target_pairs={{0,2},{1,3},{2,0},{3,1},{4,6},{5,7},{6,4},{7,5},{8,10},{9,11},{10,... | collective-permute-start | bytes 393224 | tf_op jit(solution)/shard_map/ppermute | solution.py:434
  35.4 15.0 %collective-permute-start.14 = (bf16[256,256]{1,0:T(8,128)(2,1)S(1)}, bf16[256,256]{1,0:T(8,128)(2,1)S(1)}, u32[]{:S(2)}, u32[]{:S(2)}) collective-permute-start(bf16[256,256]{1,0:T(8,128)(2,1)S(1)} %get-tuple-element.52), channel_id=1, source_target_pairs={{0,12},{1,13},{2,14},{3,15},{4,0},{5,1},{6,2},{7,3},{8,4},{9,5},{1... | collective-permute-start | bytes 393224 | tf_op jit(solution)/shard_map/ppermute | solution.py:428
  43.2 7.7 %collective-permute-start.16 = (bf16[256,256]{1,0:T(8,128)(2,1)S(1)}, bf16[256,256]{1,0:T(8,128)(2,1)S(1)}, u32[]{:S(2)}, u32[]{:S(2)}) collective-permute-start(bf16[256,256]{1,0:T(8,128)(2,1)S(1)} %get-tuple-element.54), channel_id=1, source_target_pairs={{0,14},{1,15},{2,0},{3,1},{4,2},{5,3},{6,4},{7,5},{8,6},{9,7},{10,... | collective-permute-start | bytes 393224 | tf_op jit(solution)/shard_map/ppermute | solution.py:428
  48.3 5.0 %collective-permute-start.17 = (bf16[256,256]{1,0:T(8,128)(2,1)S(1)}, bf16[256,256]{1,0:T(8,128)(2,1)S(1)}, u32[]{:S(2)}, u32[]{:S(2)}) collective-permute-start(bf16[256,256]{1,0:T(8,128)(2,1)S(1)} %get-tuple-element.56), channel_id=1, source_target_pairs={{0,2},{1,3},{2,0},{3,1},{4,6},{5,7},{6,4},{7,5},{8,10},{9,11},{10,... | collective-permute-start | bytes 393224 | tf_op jit(solution)/shard_map/ppermute | solution.py:434
  48.3 5.0 %collective-permute-start.18 = (bf16[256,256]{1,0:T(8,128)(2,1)S(1)}, bf16[256,256]{1,0:T(8,128)(2,1)S(1)}, u32[]{:S(2)}, u32[]{:S(2)}) collective-permute-start(bf16[256,256]{1,0:T(8,128)(2,1)S(1)} %get-tuple-element.57), channel_id=1, source_target_pairs={{0,12},{1,13},{2,14},{3,15},{4,0},{5,1},{6,2},{7,3},{8,4},{9,5},{1... | collective-permute-start | bytes 393224 | tf_op jit(solution)/shard_map/ppermute | solution.py:428
  50.3 11.3 %collective-permute-start.11 = (bf16[128,2048]{1,0:T(8,128)(2,1)S(1)}, bf16[128,2048]{1,0:T(8,128)(2,1)S(1)}, u32[]{:S(2)}, u32[]{:S(2)}) collective-permute-start(bf16[128,2048]{1,0:T(8,128)(2,1)S(1)} %get-tuple-element.47), channel_id=1, source_target_pairs={{0,1},{1,0},{2,3},{3,2},{4,5},{5,4},{6,7},{7,6},{8,9},{9,8},{10,11... | collective-permute-start | bytes 1572872 | tf_op jit(solution)/shard_map/ppermute | solution.py:431
  50.4 11.3 %collective-permute-start.10 = (bf16[128,2048]{1,0:T(8,128)(2,1)S(1)}, bf16[128,2048]{1,0:T(8,128)(2,1)S(1)}, u32[]{:S(2)}, u32[]{:S(2)}) collective-permute-start(bf16[128,2048]{1,0:T(8,128)(2,1)S(1)} %get-tuple-element.46), channel_id=1, source_target_pairs={{0,1},{1,0},{2,3},{3,2},{4,5},{5,4},{6,7},{7,6},{8,9},{9,8},{10,11... | collective-permute-start | bytes 1572872 | tf_op jit(solution)/shard_map/ppermute | solution.py:431
  50.9 6.4 %collective-permute-start.15 = (bf16[256,256]{1,0:T(8,128)(2,1)S(1)}, bf16[256,256]{1,0:T(8,128)(2,1)S(1)}, u32[]{:S(2)}, u32[]{:S(2)}) collective-permute-start(bf16[256,256]{1,0:T(8,128)(2,1)S(1)} %fusion.4), channel_id=1, source_target_pairs={{0,12},{1,13},{2,14},{3,15},{4,0},{5,1},{6,2},{7,3},{8,4},{9,5},{1... | collective-permute-start | bytes 393224 | tf_op jit(solution)/shard_map/ppermute | solution.py:428
  53.4 6.7 %collective-permute-start.19 = (bf16[256,256]{1,0:T(8,128)(2,1)S(1)}, bf16[256,256]{1,0:T(8,128)(2,1)S(1)}, u32[]{:S(2)}, u32[]{:S(2)}) collective-permute-start(bf16[256,256]{1,0:T(8,128)(2,1)S(1)} %fusion.9), channel_id=1, source_target_pairs={{0,12},{1,13},{2,14},{3,15},{4,0},{5,1},{6,2},{7,3},{8,4},{9,5},{1... | collective-permute-start | bytes 393224 | tf_op jit(solution)/shard_map/ppermute | solution.py:428
  60.2 1.4 %collective-permute-start.20 = (bf16[128,512]{1,0:T(8,128)(2,1)S(1)}, bf16[128,512]{1,0:T(8,128)(2,1)S(1)}, u32[]{:S(2)}, u32[]{:S(2)}) collective-permute-start(bf16[128,512]{1,0:T(8,128)(2,1)S(1)} %get-tuple-element.58), channel_id=1, source_target_pairs={{0,1},{1,0},{2,3},{3,2},{4,5},{5,4},{6,7},{7,6},{8,9},{9,8},{10,11... | collective-permute-start | bytes 393224 | tf_op jit(solution)/shard_map/ppermute | solution.py:431

commit v4 on v2

--- a/solution.py
+++ b/solution.py
@@ -231,9 +231,10 @@
                         weights(u, b + i, peak)
                 if u > 0:
                     score_grads(u - 1, b, inner)
-                key_grads(u)
-                if u + 1 >= units:
+                if b % 3 == 0:
                     key_grads(u)
+                    if u + 1 >= units:
+                        key_grads(u)
             if u > 0:
                 query_grad(u - 1, inv)
             if 0 <= u < units:
@@ -278,11 +279,11 @@
 
     @pl.when(chip >= 2)
     def _():
-        attend(2 * CHUNKS - 1, 3)
+        attend(2 * CHUNKS - 1, 1)
 
     @pl.when(chip < 2)
     def _():
-        attend(4, 2)
+        attend(4, 1)
 
 
 def place_kernel(heads, o_in, dq_in, *refs):

time: 62.2 us -> 61.8 us (level)
  Pallas kernels: 15.3 us -> 14.5 us
    pallas_call x2, Pallas kernels: 10.5 us -> 9.62 us  [head_attention(): pl.pallas_call(functools.partial(attention_kernel, slot, heads), in_specs...]
  transfers between devices with their start and end apart: 21 -> 21, of which waited for: 5 -> 5; matrix products, arithmetic and copies ran while one was open for 1% -> 1% of each run, Pallas kernels for 21% -> 19%
where the time goes in v4:
time: 61.8 us; the launch traced here: 61.7 us
  starting transfers between devices  34.4 us (56%)
  Pallas kernels  14.5 us (23%)
  waiting for transfers between devices  11.5 us (19%)
  between operations  0.94 us (2%)
    ppermute x12, starting transfers between devices, shift(): return lax.ppermute(x, 'context', [(i, (i + by) % n) for i in range(n)])  30.3 us
    pallas_call x2, Pallas kernels, head_attention(): pl.pallas_call(functools.partial(attention_kernel, slot, heads), in_specs...  9.62 us
    ppermute x12, waiting for transfers between devices, shift(): return lax.ppermute(x, 'context', [(i, (i + by) % n) for i in range(n)])  9.16 us
    ppermute x4, starting transfers between devices, across(): return lax.ppermute(x, 'context', [(i, i ^ 2) for i in range(n)])  2.54 us
    ppermute x5, waiting for transfers between devices, swap(): return lax.ppermute(x, 'context', [(i, i ^ 1) for i in range(n)])  2.33 us
    pallas_call x1, Pallas kernels, staged(): pl.pallas_call(functools.partial(stage_kernel, heads), in_specs=[ANYWHERE...  2.29 us
    ppermute x5, starting transfers between devices, swap(): return lax.ppermute(x, 'context', [(i, i ^ 1) for i in range(n)])  1.52 us
    pallas_call x1, Pallas kernels, shares(): pl.pallas_call(share_kernel, in_specs=[ANYWHERE] * 4, out_specs=[VMEM] *...  1.41 us
  transfers between devices with their start and end apart: 21, of which 5 were waited for; matrix products, arithmetic and copies ran while one was open for 1% of the time, Pallas kernels for 19%

profile of v4, /device:TPU:0, one launch (start us, length us, event | category | flops | bytes accessed | tf_op | source)
XLA Modules:
  0.0 61.7 jit_solution(13277723062031145423)
XLA Ops:
  0.6 1.4 %share.1 = (bf16[128,512]{1,0:T(8,128)(2,1)S(1)}, bf16[128,512]{1,0:T(8,128)(2,1)S(1)}, bf16[128,4096]{1,0:T(8,128)(2,1)S(1)}) custom-call(bf16[128,512]{1,0:T(8,128)(2,1)} %k.1, bf16[128,512]{1,0:T(8,128)(2,1)} %v.1, bf16[128,4096]{1,0:T(8,128)(2,1)} %q_all.1, bf16[128,4096]{1,0:T(8,128)(2,1)} %g_all.1), custom_call_target="tpu_custom_call" | custom-call | tf_op jit(solution)/shard_map/share/pallas_call | solution.py:307
  2.0 0.5 collective-permute-start
  2.6 1.0 %collective-permute-done.kv_oth = bf16[128,512]{1,0:T(8,128)(2,1)S(1)} collective-permute-done((bf16[128,512]{1,0:T(8,128)(2,1)S(1)}, bf16[128,512]{1,0:T(8,128)(2,1)S(1)}, u32[]{:S(2)}, u32[]{:S(2)}) %collective-permute-start) | collective-permute-done | bytes 131104 | tf_op jit(solution)/shard_map/ppermute | solution.py:434
  4.0 2.7 %collective-permute-start.6 = (bf16[256,256]{1,0:T(8,128)(2,1)S(1)}, bf16[256,256]{1,0:T(8,128)(2,1)S(1)}, u32[]{:S(2)}, u32[]{:S(2)}) collective-permute-start(bf16[256,256]{1,0:T(8,128)(2,1)S(1)} %get-tuple-element.41.kv0), channel_id=1, source_target_pairs={{0,4},{1,5},{2,6},{3,7},{4,8},{5,9},{6,10},{7,11},{8,12},{9,13},{1... | collective-permute-start | bytes 393224 | tf_op jit(solution)/shard_map/ppermute | solution.py:431
  6.8 1.6 %collective-permute-start.2 = (bf16[256,256]{1,0:T(8,128)(2,1)S(1)}, bf16[256,256]{1,0:T(8,128)(2,1)S(1)}, u32[]{:S(2)}, u32[]{:S(2)}) collective-permute-start(bf16[256,256]{1,0:T(8,128)(2,1)S(1)} %get-tuple-element.40.kv0), channel_id=1, source_target_pairs={{0,4},{1,5},{2,6},{3,7},{4,8},{5,9},{6,10},{7,11},{8,12},{9,13},{1... | collective-permute-start | bytes 393224 | tf_op jit(solution)/shard_map/ppermute | solution.py:431
  8.3 4.8 %collective-permute-done.6.kv2 = bf16[256,256]{1,0:T(8,128)(2,1)S(1)} collective-permute-done((bf16[256,256]{1,0:T(8,128)(2,1)S(1)}, bf16[256,256]{1,0:T(8,128)(2,1)S(1)}, u32[]{:S(2)}, u32[]{:S(2)}) %collective-permute-start.6) | collective-permute-done | bytes 131104 | tf_op jit(solution)/shard_map/ppermute | solution.py:431
  13.1 1.7 %collective-permute-start.8 = (bf16[256,256]{1,0:T(8,128)(2,1)S(1)}, bf16[256,256]{1,0:T(8,128)(2,1)S(1)}, u32[]{:S(2)}, u32[]{:S(2)}) collective-permute-start(bf16[256,256]{1,0:T(8,128)(2,1)S(1)} %broadcast_select_fusion), channel_id=1, source_target_pairs={{0,2},{1,3},{2,4},{3,5},{4,6},{5,7},{6,8},{7,9},{8,10},{9,11},{10,... | collective-permute-start | bytes 393224 | tf_op jit(solution)/shard_map/ppermute | solution.py:431
  14.9 1.3 %collective-permute-start.9 = (bf16[256,256]{1,0:T(8,128)(2,1)S(1)}, bf16[256,256]{1,0:T(8,128)(2,1)S(1)}, u32[]{:S(2)}, u32[]{:S(2)}) collective-permute-start(bf16[256,256]{1,0:T(8,128)(2,1)S(1)} %collective-permute-done.6.kv2), channel_id=1, source_target_pairs={{0,2},{1,3},{2,0},{3,1},{4,6},{5,7},{6,4},{7,5},{8,10},{9,11},{10,... | collective-permute-start | bytes 393224 | tf_op jit(solution)/shard_map/ppermute | solution.py:437
  16.2 1.0 %collective-permute-start.4 = (bf16[256,256]{1,0:T(8,128)(2,1)S(1)}, bf16[256,256]{1,0:T(8,128)(2,1)S(1)}, u32[]{:S(2)}, u32[]{:S(2)}) collective-permute-start(bf16[256,256]{1,0:T(8,128)(2,1)S(1)} %broadcast_select_fusion.1), channel_id=1, source_target_pairs={{0,2},{1,3},{2,4},{3,5},{4,6},{5,7},{6,8},{7,9},{8,10},{9,11},{10,... | collective-permute-start | bytes 393224 | tf_op jit(solution)/shard_map/ppermute | solution.py:431
  17.2 1.2 %collective-permute-start.3 = (bf16[256,256]{1,0:T(8,128)(2,1)S(1)}, bf16[256,256]{1,0:T(8,128)(2,1)S(1)}, u32[]{:S(2)}, u32[]{:S(2)}) collective-permute-start(bf16[256,256]{1,0:T(8,128)(2,1)S(1)} %collective-permute-done.2.kv2), channel_id=1, source_target_pairs={{0,4},{1,5},{2,6},{3,7},{4,8},{5,9},{6,10},{7,11},{8,12},{9,13},{1... | collective-permute-start | bytes 393224 | tf_op jit(solution)/shard_map/ppermute | solution.py:431
  18.3 2.3 %stage.1 = (bf16[4096,128]{1,0:T(8,128)(2,1)S(1)}, bf16[4096,128]{1,0:T(8,128)(2,1)S(1)}, bf16[16,256,256]{2,1,0:T(8,128)(2,1)S(1)}, bf16[16,128,256]{2,1,0:T(8,128)(2,1)S(1)}, bf16[1280,128]{1,0:T(8,128)(2,1)S(1)}) custom-call(s32[5]{0:T(128)} %bounds_in.1, bf16[128,4096]{1,0:T(8,128)(2,1)} %q_all.1, bf16[128,4096]{1,0:T(8,128)(2,1)} %g_all.1, ...), custom_call_target="tpu_custom_call" | custom-call | bytes 4194304 | tf_op jit(solution)/shard_map/stage/pallas_call | solution.py:335
  20.6 1.7 %collective-permute-done.8.kv_edge = bf16[256,256]{1,0:T(8,128)(2,1)S(1)} collective-permute-done((bf16[256,256]{1,0:T(8,128)(2,1)S(1)}, bf16[256,256]{1,0:T(8,128)(2,1)S(1)}, u32[]{:S(2)}, u32[]{:S(2)}) %collective-permute-start.8) | collective-permute-done | bytes 131104 | tf_op jit(solution)/shard_map/ppermute | solution.py:431
  22.3 1.2 %collective-permute-start.5 = (bf16[256,256]{1,0:T(8,128)(2,1)S(1)}, bf16[256,256]{1,0:T(8,128)(2,1)S(1)}, u32[]{:S(2)}, u32[]{:S(2)}) collective-permute-start(bf16[256,256]{1,0:T(8,128)(2,1)S(1)} %collective-permute-done.2.kv2), channel_id=1, source_target_pairs={{0,2},{1,3},{2,0},{3,1},{4,6},{5,7},{6,4},{7,5},{8,10},{9,11},{10,... | collective-permute-start | bytes 393224 | tf_op jit(solution)/shard_map/ppermute | solution.py:437
  23.5 4.8 %attention0.1 = (bf16[128,4096]{1,0:T(8,128)(2,1)}, bf16[128,4096]{1,0:T(8,128)(2,1)}, bf16[128,2048]{1,0:T(8,128)(2,1)S(1)}, bf16[256,256]{1,0:T(8,128)(2,1)S(1...) custom-call(bf16[4096,128]{1,0:T(8,128)(2,1)S(1)} %get-tuple-element, ...), custom_call_target="tpu_custom_call" | custom-call | flops 3355443200 | bytes 3145728 | tf_op jit(solution)/shard_map/attention0/pallas_call | solution.py:367
  28.3 6.4 %collective-permute-start.12 = (bf16[256,256]{1,0:T(8,128)(2,1)S(1)}, bf16[256,256]{1,0:T(8,128)(2,1)S(1)}, u32[]{:S(2)}, u32[]{:S(2)}) collective-permute-start(bf16[256,256]{1,0:T(8,128)(2,1)S(1)} %get-tuple-element.49), channel_id=1, source_target_pairs={{0,14},{1,15},{2,0},{3,1},{4,2},{5,3},{6,4},{7,5},{8,6},{9,7},{10,... | collective-permute-start | bytes 393224 | tf_op jit(solution)/shard_map/ppermute | solution.py:431
  34.7 2.4 %collective-permute-start.14 = (bf16[256,256]{1,0:T(8,128)(2,1)S(1)}, bf16[256,256]{1,0:T(8,128)(2,1)S(1)}, u32[]{:S(2)}, u32[]{:S(2)}) collective-permute-start(bf16[256,256]{1,0:T(8,128)(2,1)S(1)} %get-tuple-element.52), channel_id=1, source_target_pairs={{0,12},{1,13},{2,14},{3,15},{4,0},{5,1},{6,2},{7,3},{8,4},{9,5},{1... | collective-permute-start | bytes 393224 | tf_op jit(solution)/shard_map/ppermute | solution.py:431
  37.2 4.8 %attention1.1 = (bf16[128,4096]{1,0:T(8,128)(2,1)}, bf16[128,4096]{1,0:T(8,128)(2,1)}, bf16[128,2048]{1,0:T(8,128)(2,1)S(1)}, bf16[256,256]{1,0:T(8,128)(2,1)S(1...) custom-call(bf16[4096,128]{1,0:T(8,128)(2,1)S(1)} %get-tuple-element, ...), custom_call_target="tpu_custom_call", output_to_operand_aliasing={{0}: (10, {}), {1}: (11, {})} | custom-call | flops 3355443200 | bytes 3145728 | tf_op jit(solution)/shard_map/attention1/pallas_call | solution.py:367
  42.0 5.0 %collective-permute-start.16 = (bf16[256,256]{1,0:T(8,128)(2,1)S(1)}, bf16[256,256]{1,0:T(8,128)(2,1)S(1)}, u32[]{:S(2)}, u32[]{:S(2)}) collective-permute-start(bf16[256,256]{1,0:T(8,128)(2,1)S(1)} %get-tuple-element.54), channel_id=1, source_target_pairs={{0,14},{1,15},{2,0},{3,1},{4,2},{5,3},{6,4},{7,5},{8,6},{9,7},{10,... | collective-permute-start | bytes 393224 | tf_op jit(solution)/shard_map/ppermute | solution.py:431
  47.0 2.1 %collective-permute-start.18 = (bf16[256,256]{1,0:T(8,128)(2,1)S(1)}, bf16[256,256]{1,0:T(8,128)(2,1)S(1)}, u32[]{:S(2)}, u32[]{:S(2)}) collective-permute-start(bf16[256,256]{1,0:T(8,128)(2,1)S(1)} %get-tuple-element.57), channel_id=1, source_target_pairs={{0,12},{1,13},{2,14},{3,15},{4,0},{5,1},{6,2},{7,3},{8,4},{9,5},{1... | collective-permute-start | bytes 393224 | tf_op jit(solution)/shard_map/ppermute | solution.py:431
  49.7 2.3 %collective-permute-start.15 = (bf16[256,256]{1,0:T(8,128)(2,1)S(1)}, bf16[256,256]{1,0:T(8,128)(2,1)S(1)}, u32[]{:S(2)}, u32[]{:S(2)}) collective-permute-start(bf16[256,256]{1,0:T(8,128)(2,1)S(1)} %fusion.4), channel_id=1, source_target_pairs={{0,12},{1,13},{2,14},{3,15},{4,0},{5,1},{6,2},{7,3},{8,4},{9,5},{1... | collective-permute-start | bytes 393224 | tf_op jit(solution)/shard_map/ppermute | solution.py:431
  52.1 4.0 %collective-permute-start.19 = (bf16[256,256]{1,0:T(8,128)(2,1)S(1)}, bf16[256,256]{1,0:T(8,128)(2,1)S(1)}, u32[]{:S(2)}, u32[]{:S(2)}) collective-permute-start(bf16[256,256]{1,0:T(8,128)(2,1)S(1)} %fusion.9), channel_id=1, source_target_pairs={{0,12},{1,13},{2,14},{3,15},{4,0},{5,1},{6,2},{7,3},{8,4},{9,5},{1... | collective-permute-start | bytes 393224 | tf_op jit(solution)/shard_map/ppermute | solution.py:431
  56.2 2.7 %collective-permute-done.19 = bf16[256,256]{1,0:T(8,128)(2,1)S(1)} collective-permute-done((bf16[256,256]{1,0:T(8,128)(2,1)S(1)}, bf16[256,256]{1,0:T(8,128)(2,1)S(1)}, u32[]{:S(2)}, u32[]{:S(2)}) %collective-permute-start.19) | collective-permute-done | bytes 131104 | tf_op jit(solution)/shard_map/ppermute | solution.py:431
  59.0 1.3 %collective-permute-done.20.refs_3_ = bf16[128,512]{1,0:T(8,128)(2,1)S(1)} collective-permute-done((bf16[128,512]{1,0:T(8,128)(2,1)S(1)}, bf16[128,512]{1,0:T(8,128)(2,1)S(1)}, u32[]{:S(2)}, u32[]{:S(2)}) %collective-permute-start.20) | collective-permute-done | bytes 131104 | tf_op jit(solution)/shard_map/ppermute | solution.py:434
  60.4 1.1 %place.1 = (bf16[128,4096]{1,0:T(8,128)(2,1)}, bf16[128,4096]{1,0:T(8,128)(2,1)}, bf16[128,512]{1,0:T(8,128)(2,1)}, bf16[128,512]{1,0:T(8,128)(2,1)}) custom-call(bf16[128,4096]{1,0:T(8,128)(2,1)} %get-tuple-element.44.o_in, bf16[128,4096]{1,0:T(8,128)(2,1)} %get-tuple-element.45.dq_in, ...), custom_call_target="tpu_custom_call", output_to_operand_aliasing={{0}: (0, {}), {1}: (1, {})} | custom-call | tf_op jit(solution)/shard_map/place/pallas_call | solution.py:405
  (34 shorter events, 1.5 us)
Async XLA Ops:
  2.0 1.5 %collective-permute-start = (bf16[128,512]{1,0:T(8,128)(2,1)S(1)}, bf16[128,512]{1,0:T(8,128)(2,1)S(1)}, u32[]{:S(2)}, u32[]{:S(2)}) collective-permute-start(bf16[128,512]{1,0:T(8,128)(2,1)S(1)} %get-tuple-element.32), channel_id=1, source_target_pairs={{0,1},{1,0},{2,3},{3,2},{4,5},{5,4},{6,7},{7,6},{8,9},{9,8},{10,11... | collective-permute-start | bytes 393224 | tf_op jit(solution)/shard_map/ppermute | solution.py:434
  3.6 13.6 %collective-permute-start.1 = (bf16[128,4096]{1,0:T(8,128)(2,1)S(1)}, bf16[128,4096]{1,0:T(8,128)(2,1)S(1)}, u32[]{:S(2)}, u32[]{:S(2)}) collective-permute-start(bf16[128,4096]{1,0:T(8,128)(2,1)S(1)} %get-tuple-element.34), channel_id=1, source_target_pairs={{0,1},{1,0},{2,3},{3,2},{4,5},{5,4},{6,7},{7,6},{8,9},{9,8},{10,11... | collective-permute-start | bytes 3145736 | tf_op jit(solution)/shard_map/ppermute | solution.py:434
  4.0 9.1 %collective-permute-start.6 = (bf16[256,256]{1,0:T(8,128)(2,1)S(1)}, bf16[256,256]{1,0:T(8,128)(2,1)S(1)}, u32[]{:S(2)}, u32[]{:S(2)}) collective-permute-start(bf16[256,256]{1,0:T(8,128)(2,1)S(1)} %get-tuple-element.41.kv0), channel_id=1, source_target_pairs={{0,4},{1,5},{2,6},{3,7},{4,8},{5,9},{6,10},{7,11},{8,12},{9,13},{1... | collective-permute-start | bytes 393224 | tf_op jit(solution)/shard_map/ppermute | solution.py:431
  6.8 9.4 %collective-permute-start.2 = (bf16[256,256]{1,0:T(8,128)(2,1)S(1)}, bf16[256,256]{1,0:T(8,128)(2,1)S(1)}, u32[]{:S(2)}, u32[]{:S(2)}) collective-permute-start(bf16[256,256]{1,0:T(8,128)(2,1)S(1)} %get-tuple-element.40.kv0), channel_id=1, source_target_pairs={{0,4},{1,5},{2,6},{3,7},{4,8},{5,9},{6,10},{7,11},{8,12},{9,13},{1... | collective-permute-start | bytes 393224 | tf_op jit(solution)/shard_map/ppermute | solution.py:431
  13.1 9.2 %collective-permute-start.8 = (bf16[256,256]{1,0:T(8,128)(2,1)S(1)}, bf16[256,256]{1,0:T(8,128)(2,1)S(1)}, u32[]{:S(2)}, u32[]{:S(2)}) collective-permute-start(bf16[256,256]{1,0:T(8,128)(2,1)S(1)} %broadcast_select_fusion), channel_id=1, source_target_pairs={{0,2},{1,3},{2,4},{3,5},{4,6},{5,7},{6,8},{7,9},{8,10},{9,11},{10,... | collective-permute-start | bytes 393224 | tf_op jit(solution)/shard_map/ppermute | solution.py:431
  14.9 8.7 %collective-permute-start.7 = (bf16[256,256]{1,0:T(8,128)(2,1)S(1)}, bf16[256,256]{1,0:T(8,128)(2,1)S(1)}, u32[]{:S(2)}, u32[]{:S(2)}) collective-permute-start(bf16[256,256]{1,0:T(8,128)(2,1)S(1)} %collective-permute-done.6.kv2), channel_id=1, source_target_pairs={{0,4},{1,5},{2,6},{3,7},{4,8},{5,9},{6,10},{7,11},{8,12},{9,13},{1... | collective-permute-start | bytes 393224 | tf_op jit(solution)/shard_map/ppermute | solution.py:431
  14.9 8.7 %collective-permute-start.9 = (bf16[256,256]{1,0:T(8,128)(2,1)S(1)}, bf16[256,256]{1,0:T(8,128)(2,1)S(1)}, u32[]{:S(2)}, u32[]{:S(2)}) collective-permute-start(bf16[256,256]{1,0:T(8,128)(2,1)S(1)} %collective-permute-done.6.kv2), channel_id=1, source_target_pairs={{0,2},{1,3},{2,0},{3,1},{4,6},{5,7},{6,4},{7,5},{8,10},{9,11},{10,... | collective-permute-start | bytes 393224 | tf_op jit(solution)/shard_map/ppermute | solution.py:437
  16.2 18.5 %collective-permute-start.4 = (bf16[256,256]{1,0:T(8,128)(2,1)S(1)}, bf16[256,256]{1,0:T(8,128)(2,1)S(1)}, u32[]{:S(2)}, u32[]{:S(2)}) collective-permute-start(bf16[256,256]{1,0:T(8,128)(2,1)S(1)} %broadcast_select_fusion.1), channel_id=1, source_target_pairs={{0,2},{1,3},{2,4},{3,5},{4,6},{5,7},{6,8},{7,9},{8,10},{9,11},{10,... | collective-permute-start | bytes 393224 | tf_op jit(solution)/shard_map/ppermute | solution.py:431
  17.2 20.0 %collective-permute-start.3 = (bf16[256,256]{1,0:T(8,128)(2,1)S(1)}, bf16[256,256]{1,0:T(8,128)(2,1)S(1)}, u32[]{:S(2)}, u32[]{:S(2)}) collective-permute-start(bf16[256,256]{1,0:T(8,128)(2,1)S(1)} %collective-permute-done.2.kv2), channel_id=1, source_target_pairs={{0,4},{1,5},{2,6},{3,7},{4,8},{5,9},{6,10},{7,11},{8,12},{9,13},{1... | collective-permute-start | bytes 393224 | tf_op jit(solution)/shard_map/ppermute | solution.py:431
  22.3 14.8 %collective-permute-start.5 = (bf16[256,256]{1,0:T(8,128)(2,1)S(1)}, bf16[256,256]{1,0:T(8,128)(2,1)S(1)}, u32[]{:S(2)}, u32[]{:S(2)}) collective-permute-start(bf16[256,256]{1,0:T(8,128)(2,1)S(1)} %collective-permute-done.2.kv2), channel_id=1, source_target_pairs={{0,2},{1,3},{2,0},{3,1},{4,6},{5,7},{6,4},{7,5},{8,10},{9,11},{10,... | collective-permute-start | bytes 393224 | tf_op jit(solution)/shard_map/ppermute | solution.py:437
  28.3 18.7 %collective-permute-start.12 = (bf16[256,256]{1,0:T(8,128)(2,1)S(1)}, bf16[256,256]{1,0:T(8,128)(2,1)S(1)}, u32[]{:S(2)}, u32[]{:S(2)}) collective-permute-start(bf16[256,256]{1,0:T(8,128)(2,1)S(1)} %get-tuple-element.49), channel_id=1, source_target_pairs={{0,14},{1,15},{2,0},{3,1},{4,2},{5,3},{6,4},{7,5},{8,6},{9,7},{10,... | collective-permute-start | bytes 393224 | tf_op jit(solution)/shard_map/ppermute | solution.py:431
  34.7 14.4 %collective-permute-start.13 = (bf16[256,256]{1,0:T(8,128)(2,1)S(1)}, bf16[256,256]{1,0:T(8,128)(2,1)S(1)}, u32[]{:S(2)}, u32[]{:S(2)}) collective-permute-start(bf16[256,256]{1,0:T(8,128)(2,1)S(1)} %get-tuple-element.51), channel_id=1, source_target_pairs={{0,2},{1,3},{2,0},{3,1},{4,6},{5,7},{6,4},{7,5},{8,10},{9,11},{10,... | collective-permute-start | bytes 393224 | tf_op jit(solution)/shard_map/ppermute | solution.py:437
  34.7 14.4 %collective-permute-start.14 = (bf16[256,256]{1,0:T(8,128)(2,1)S(1)}, bf16[256,256]{1,0:T(8,128)(2,1)S(1)}, u32[]{:S(2)}, u32[]{:S(2)}) collective-permute-start(bf16[256,256]{1,0:T(8,128)(2,1)S(1)} %get-tuple-element.52), channel_id=1, source_target_pairs={{0,12},{1,13},{2,14},{3,15},{4,0},{5,1},{6,2},{7,3},{8,4},{9,5},{1... | collective-permute-start | bytes 393224 | tf_op jit(solution)/shard_map/ppermute | solution.py:431
  42.0 7.7 %collective-permute-start.16 = (bf16[256,256]{1,0:T(8,128)(2,1)S(1)}, bf16[256,256]{1,0:T(8,128)(2,1)S(1)}, u32[]{:S(2)}, u32[]{:S(2)}) collective-permute-start(bf16[256,256]{1,0:T(8,128)(2,1)S(1)} %get-tuple-element.54), channel_id=1, source_target_pairs={{0,14},{1,15},{2,0},{3,1},{4,2},{5,3},{6,4},{7,5},{8,6},{9,7},{10,... | collective-permute-start | bytes 393224 | tf_op jit(solution)/shard_map/ppermute | solution.py:431
  47.0 5.0 %collective-permute-start.17 = (bf16[256,256]{1,0:T(8,128)(2,1)S(1)}, bf16[256,256]{1,0:T(8,128)(2,1)S(1)}, u32[]{:S(2)}, u32[]{:S(2)}) collective-permute-start(bf16[256,256]{1,0:T(8,128)(2,1)S(1)} %get-tuple-element.56), channel_id=1, source_target_pairs={{0,2},{1,3},{2,0},{3,1},{4,6},{5,7},{6,4},{7,5},{8,10},{9,11},{10,... | collective-permute-start | bytes 393224 | tf_op jit(solution)/shard_map/ppermute | solution.py:437
  47.0 5.0 %collective-permute-start.18 = (bf16[256,256]{1,0:T(8,128)(2,1)S(1)}, bf16[256,256]{1,0:T(8,128)(2,1)S(1)}, u32[]{:S(2)}, u32[]{:S(2)}) collective-permute-start(bf16[256,256]{1,0:T(8,128)(2,1)S(1)} %get-tuple-element.57), channel_id=1, source_target_pairs={{0,12},{1,13},{2,14},{3,15},{4,0},{5,1},{6,2},{7,3},{8,4},{9,5},{1... | collective-permute-start | bytes 393224 | tf_op jit(solution)/shard_map/ppermute | solution.py:431
  49.1 11.3 %collective-permute-start.11 = (bf16[128,2048]{1,0:T(8,128)(2,1)S(1)}, bf16[128,2048]{1,0:T(8,128)(2,1)S(1)}, u32[]{:S(2)}, u32[]{:S(2)}) collective-permute-start(bf16[128,2048]{1,0:T(8,128)(2,1)S(1)} %get-tuple-element.47), channel_id=1, source_target_pairs={{0,1},{1,0},{2,3},{3,2},{4,5},{5,4},{6,7},{7,6},{8,9},{9,8},{10,11... | collective-permute-start | bytes 1572872 | tf_op jit(solution)/shard_map/ppermute | solution.py:434
  49.1 11.3 %collective-permute-start.10 = (bf16[128,2048]{1,0:T(8,128)(2,1)S(1)}, bf16[128,2048]{1,0:T(8,128)(2,1)S(1)}, u32[]{:S(2)}, u32[]{:S(2)}) collective-permute-start(bf16[128,2048]{1,0:T(8,128)(2,1)S(1)} %get-tuple-element.46), channel_id=1, source_target_pairs={{0,1},{1,0},{2,3},{3,2},{4,5},{5,4},{6,7},{7,6},{8,9},{9,8},{10,11... | collective-permute-start | bytes 1572872 | tf_op jit(solution)/shard_map/ppermute | solution.py:434
  49.7 6.4 %collective-permute-start.15 = (bf16[256,256]{1,0:T(8,128)(2,1)S(1)}, bf16[256,256]{1,0:T(8,128)(2,1)S(1)}, u32[]{:S(2)}, u32[]{:S(2)}) collective-permute-start(bf16[256,256]{1,0:T(8,128)(2,1)S(1)} %fusion.4), channel_id=1, source_target_pairs={{0,12},{1,13},{2,14},{3,15},{4,0},{5,1},{6,2},{7,3},{8,4},{9,5},{1... | collective-permute-start | bytes 393224 | tf_op jit(solution)/shard_map/ppermute | solution.py:431
  52.1 6.7 %collective-permute-start.19 = (bf16[256,256]{1,0:T(8,128)(2,1)S(1)}, bf16[256,256]{1,0:T(8,128)(2,1)S(1)}, u32[]{:S(2)}, u32[]{:S(2)}) collective-permute-start(bf16[256,256]{1,0:T(8,128)(2,1)S(1)} %fusion.9), channel_id=1, source_target_pairs={{0,12},{1,13},{2,14},{3,15},{4,0},{5,1},{6,2},{7,3},{8,4},{9,5},{1... | collective-permute-start | bytes 393224 | tf_op jit(solution)/shard_map/ppermute | solution.py:431
  59.0 1.4 %collective-permute-start.20 = (bf16[128,512]{1,0:T(8,128)(2,1)S(1)}, bf16[128,512]{1,0:T(8,128)(2,1)S(1)}, u32[]{:S(2)}, u32[]{:S(2)}) collective-permute-start(bf16[128,512]{1,0:T(8,128)(2,1)S(1)} %get-tuple-element.58), channel_id=1, source_target_pairs={{0,1},{1,0},{2,3},{3,2},{4,5},{5,4},{6,7},{7,6},{8,9},{9,8},{10,11... | collective-permute-start | bytes 393224 | tf_op jit(solution)/shard_map/ppermute | solution.py:434

commit v5 on v2

--- a/solution.py
+++ b/solution.py
@@ -195,17 +195,17 @@
             _, keys = window(u)
             store((dot(k_t[:, keys], d_scr[keys, columns(u)]) * (inv * scale)).astype(BF), dq_scr, u)
 
-        first_group = [(b * rows, *one[:3]) for b in range(0, blocks, 3) for one in sums] if whole else []
-        second_group = [(rows + b * rows, *one[:3]) for b in range(0, blocks, 3) for one in sums] if whole else []
+        first_group = [(b * rows, *one[:3]) for b in range(blocks) for one in sums] if whole else []
+        second_group = [(rows + b * rows, *one[:3]) for b in range(blocks) for one in sums] if whole else []
 
         def key_grads(turn):
             if turn > pairs and first_group:
                 at, left, right, acc = first_group.pop(0)
-                at = slice(at, at + 3 * rows)
+                at = slice(at, at + rows)
                 acc[at] = dot(left[at, :half], right[:half])
             elif turn > 3 * pairs // 2 and second_group:
                 at, left, right, acc = second_group.pop(0)
-                at = slice(at, at + 3 * rows)
+                at = slice(at, at + rows)
                 acc[at] += dot(left[at, half:part], right[half:part])
 
         def outputs(u):
@@ -278,11 +278,11 @@
 
     @pl.when(chip >= 2)
     def _():
-        attend(2 * CHUNKS - 1, 3)
+        attend(2 * CHUNKS - 1, 1)
 
     @pl.when(chip < 2)
     def _():
-        attend(4, 2)
+        attend(4, 1)
 
 
 def place_kernel(heads, o_in, dq_in, *refs):

time: 62.2 us -> 61.9 us (level)
  Pallas kernels: 15.3 us -> 14.5 us
    pallas_call x2, Pallas kernels: 10.5 us -> 9.62 us  [head_attention(): pl.pallas_call(functools.partial(attention_kernel, slot, heads), in_specs...]
  transfers between devices with their start and end apart: 21 -> 21, of which waited for: 5 -> 5; matrix products, arithmetic and copies ran while one was open for 1% -> 1% of each run, Pallas kernels for 21% -> 19%
where the time goes in v5:
time: 61.9 us; the launch traced here: 61.8 us
  starting transfers between devices  34.5 us (56%)
  Pallas kernels  14.5 us (23%)
  waiting for transfers between devices  11.5 us (19%)
  between operations  0.94 us (2%)
    ppermute x12, starting transfers between devices, shift(): return lax.ppermute(x, 'context', [(i, (i + by) % n) for i in range(n)])  30.4 us
    pallas_call x2, Pallas kernels, head_attention(): pl.pallas_call(functools.partial(attention_kernel, slot, heads), in_specs...  9.62 us
    ppermute x12, waiting for transfers between devices, shift(): return lax.ppermute(x, 'context', [(i, (i + by) % n) for i in range(n)])  9.16 us
    ppermute x4, starting transfers between devices, across(): return lax.ppermute(x, 'context', [(i, i ^ 2) for i in range(n)])  2.54 us
    ppermute x5, waiting for transfers between devices, swap(): return lax.ppermute(x, 'context', [(i, i ^ 1) for i in range(n)])  2.33 us
    pallas_call x1, Pallas kernels, staged(): pl.pallas_call(functools.partial(stage_kernel, heads), in_specs=[ANYWHERE...  2.29 us
    ppermute x5, starting transfers between devices, swap(): return lax.ppermute(x, 'context', [(i, i ^ 1) for i in range(n)])  1.52 us
    pallas_call x1, Pallas kernels, shares(): pl.pallas_call(share_kernel, in_specs=[ANYWHERE] * 4, out_specs=[VMEM] *...  1.41 us
  transfers between devices with their start and end apart: 21, of which 5 were waited for; matrix products, arithmetic and copies ran while one was open for 1% of the time, Pallas kernels for 19%

profile of v5, /device:TPU:0, one launch (start us, length us, event | category | flops | bytes accessed | tf_op | source)
XLA Modules:
  0.0 61.8 jit_solution(15591451668487147268)
XLA Ops:
  0.6 1.4 %share.1 = (bf16[128,512]{1,0:T(8,128)(2,1)S(1)}, bf16[128,512]{1,0:T(8,128)(2,1)S(1)}, bf16[128,4096]{1,0:T(8,128)(2,1)S(1)}) custom-call(bf16[128,512]{1,0:T(8,128)(2,1)} %k.1, bf16[128,512]{1,0:T(8,128)(2,1)} %v.1, bf16[128,4096]{1,0:T(8,128)(2,1)} %q_all.1, bf16[128,4096]{1,0:T(8,128)(2,1)} %g_all.1), custom_call_target="tpu_custom_call" | custom-call | tf_op jit(solution)/shard_map/share/pallas_call | solution.py:306
  2.0 0.5 collective-permute-start
  2.6 1.0 %collective-permute-done.kv_oth = bf16[128,512]{1,0:T(8,128)(2,1)S(1)} collective-permute-done((bf16[128,512]{1,0:T(8,128)(2,1)S(1)}, bf16[128,512]{1,0:T(8,128)(2,1)S(1)}, u32[]{:S(2)}, u32[]{:S(2)}) %collective-permute-start) | collective-permute-done | bytes 131104 | tf_op jit(solution)/shard_map/ppermute | solution.py:433
  4.0 2.7 %collective-permute-start.6 = (bf16[256,256]{1,0:T(8,128)(2,1)S(1)}, bf16[256,256]{1,0:T(8,128)(2,1)S(1)}, u32[]{:S(2)}, u32[]{:S(2)}) collective-permute-start(bf16[256,256]{1,0:T(8,128)(2,1)S(1)} %get-tuple-element.41.kv0), channel_id=1, source_target_pairs={{0,4},{1,5},{2,6},{3,7},{4,8},{5,9},{6,10},{7,11},{8,12},{9,13},{1... | collective-permute-start | bytes 393224 | tf_op jit(solution)/shard_map/ppermute | solution.py:430
  6.8 1.6 %collective-permute-start.2 = (bf16[256,256]{1,0:T(8,128)(2,1)S(1)}, bf16[256,256]{1,0:T(8,128)(2,1)S(1)}, u32[]{:S(2)}, u32[]{:S(2)}) collective-permute-start(bf16[256,256]{1,0:T(8,128)(2,1)S(1)} %get-tuple-element.40.kv0), channel_id=1, source_target_pairs={{0,4},{1,5},{2,6},{3,7},{4,8},{5,9},{6,10},{7,11},{8,12},{9,13},{1... | collective-permute-start | bytes 393224 | tf_op jit(solution)/shard_map/ppermute | solution.py:430
  8.3 4.8 %collective-permute-done.6.kv2 = bf16[256,256]{1,0:T(8,128)(2,1)S(1)} collective-permute-done((bf16[256,256]{1,0:T(8,128)(2,1)S(1)}, bf16[256,256]{1,0:T(8,128)(2,1)S(1)}, u32[]{:S(2)}, u32[]{:S(2)}) %collective-permute-start.6) | collective-permute-done | bytes 131104 | tf_op jit(solution)/shard_map/ppermute | solution.py:430
  13.1 1.7 %collective-permute-start.8 = (bf16[256,256]{1,0:T(8,128)(2,1)S(1)}, bf16[256,256]{1,0:T(8,128)(2,1)S(1)}, u32[]{:S(2)}, u32[]{:S(2)}) collective-permute-start(bf16[256,256]{1,0:T(8,128)(2,1)S(1)} %broadcast_select_fusion), channel_id=1, source_target_pairs={{0,2},{1,3},{2,4},{3,5},{4,6},{5,7},{6,8},{7,9},{8,10},{9,11},{10,... | collective-permute-start | bytes 393224 | tf_op jit(solution)/shard_map/ppermute | solution.py:430
  14.9 1.3 %collective-permute-start.9 = (bf16[256,256]{1,0:T(8,128)(2,1)S(1)}, bf16[256,256]{1,0:T(8,128)(2,1)S(1)}, u32[]{:S(2)}, u32[]{:S(2)}) collective-permute-start(bf16[256,256]{1,0:T(8,128)(2,1)S(1)} %collective-permute-done.6.kv2), channel_id=1, source_target_pairs={{0,2},{1,3},{2,0},{3,1},{4,6},{5,7},{6,4},{7,5},{8,10},{9,11},{10,... | collective-permute-start | bytes 393224 | tf_op jit(solution)/shard_map/ppermute | solution.py:436
  16.2 1.0 %collective-permute-start.4 = (bf16[256,256]{1,0:T(8,128)(2,1)S(1)}, bf16[256,256]{1,0:T(8,128)(2,1)S(1)}, u32[]{:S(2)}, u32[]{:S(2)}) collective-permute-start(bf16[256,256]{1,0:T(8,128)(2,1)S(1)} %broadcast_select_fusion.1), channel_id=1, source_target_pairs={{0,2},{1,3},{2,4},{3,5},{4,6},{5,7},{6,8},{7,9},{8,10},{9,11},{10,... | collective-permute-start | bytes 393224 | tf_op jit(solution)/shard_map/ppermute | solution.py:430
  17.2 1.2 %collective-permute-start.3 = (bf16[256,256]{1,0:T(8,128)(2,1)S(1)}, bf16[256,256]{1,0:T(8,128)(2,1)S(1)}, u32[]{:S(2)}, u32[]{:S(2)}) collective-permute-start(bf16[256,256]{1,0:T(8,128)(2,1)S(1)} %collective-permute-done.2.kv2), channel_id=1, source_target_pairs={{0,4},{1,5},{2,6},{3,7},{4,8},{5,9},{6,10},{7,11},{8,12},{9,13},{1... | collective-permute-start | bytes 393224 | tf_op jit(solution)/shard_map/ppermute | solution.py:430
  18.3 2.3 %stage.1 = (bf16[4096,128]{1,0:T(8,128)(2,1)S(1)}, bf16[4096,128]{1,0:T(8,128)(2,1)S(1)}, bf16[16,256,256]{2,1,0:T(8,128)(2,1)S(1)}, bf16[16,128,256]{2,1,0:T(8,128)(2,1)S(1)}, bf16[1280,128]{1,0:T(8,128)(2,1)S(1)}) custom-call(s32[5]{0:T(128)} %bounds_in.1, bf16[128,4096]{1,0:T(8,128)(2,1)} %q_all.1, bf16[128,4096]{1,0:T(8,128)(2,1)} %g_all.1, ...), custom_call_target="tpu_custom_call" | custom-call | bytes 4194304 | tf_op jit(solution)/shard_map/stage/pallas_call | solution.py:334
  20.6 1.7 %collective-permute-done.8.kv_edge = bf16[256,256]{1,0:T(8,128)(2,1)S(1)} collective-permute-done((bf16[256,256]{1,0:T(8,128)(2,1)S(1)}, bf16[256,256]{1,0:T(8,128)(2,1)S(1)}, u32[]{:S(2)}, u32[]{:S(2)}) %collective-permute-start.8) | collective-permute-done | bytes 131104 | tf_op jit(solution)/shard_map/ppermute | solution.py:430
  22.3 1.2 %collective-permute-start.5 = (bf16[256,256]{1,0:T(8,128)(2,1)S(1)}, bf16[256,256]{1,0:T(8,128)(2,1)S(1)}, u32[]{:S(2)}, u32[]{:S(2)}) collective-permute-start(bf16[256,256]{1,0:T(8,128)(2,1)S(1)} %collective-permute-done.2.kv2), channel_id=1, source_target_pairs={{0,2},{1,3},{2,0},{3,1},{4,6},{5,7},{6,4},{7,5},{8,10},{9,11},{10,... | collective-permute-start | bytes 393224 | tf_op jit(solution)/shard_map/ppermute | solution.py:436
  23.5 4.8 %attention0.1 = (bf16[128,4096]{1,0:T(8,128)(2,1)}, bf16[128,4096]{1,0:T(8,128)(2,1)}, bf16[128,2048]{1,0:T(8,128)(2,1)S(1)}, bf16[256,256]{1,0:T(8,128)(2,1)S(1...) custom-call(bf16[4096,128]{1,0:T(8,128)(2,1)S(1)} %get-tuple-element, ...), custom_call_target="tpu_custom_call" | custom-call | flops 3355443200 | bytes 3145728 | tf_op jit(solution)/shard_map/attention0/pallas_call | solution.py:366
  28.3 6.5 %collective-permute-start.12 = (bf16[256,256]{1,0:T(8,128)(2,1)S(1)}, bf16[256,256]{1,0:T(8,128)(2,1)S(1)}, u32[]{:S(2)}, u32[]{:S(2)}) collective-permute-start(bf16[256,256]{1,0:T(8,128)(2,1)S(1)} %get-tuple-element.49), channel_id=1, source_target_pairs={{0,14},{1,15},{2,0},{3,1},{4,2},{5,3},{6,4},{7,5},{8,6},{9,7},{10,... | collective-permute-start | bytes 393224 | tf_op jit(solution)/shard_map/ppermute | solution.py:430
  34.9 2.4 %collective-permute-start.14 = (bf16[256,256]{1,0:T(8,128)(2,1)S(1)}, bf16[256,256]{1,0:T(8,128)(2,1)S(1)}, u32[]{:S(2)}, u32[]{:S(2)}) collective-permute-start(bf16[256,256]{1,0:T(8,128)(2,1)S(1)} %get-tuple-element.52), channel_id=1, source_target_pairs={{0,12},{1,13},{2,14},{3,15},{4,0},{5,1},{6,2},{7,3},{8,4},{9,5},{1... | collective-permute-start | bytes 393224 | tf_op jit(solution)/shard_map/ppermute | solution.py:430
  37.3 4.8 %attention1.1 = (bf16[128,4096]{1,0:T(8,128)(2,1)}, bf16[128,4096]{1,0:T(8,128)(2,1)}, bf16[128,2048]{1,0:T(8,128)(2,1)S(1)}, bf16[256,256]{1,0:T(8,128)(2,1)S(1...) custom-call(bf16[4096,128]{1,0:T(8,128)(2,1)S(1)} %get-tuple-element, ...), custom_call_target="tpu_custom_call", output_to_operand_aliasing={{0}: (10, {}), {1}: (11, {})} | custom-call | flops 3355443200 | bytes 3145728 | tf_op jit(solution)/shard_map/attention1/pallas_call | solution.py:366
  42.2 4.9 %collective-permute-start.16 = (bf16[256,256]{1,0:T(8,128)(2,1)S(1)}, bf16[256,256]{1,0:T(8,128)(2,1)S(1)}, u32[]{:S(2)}, u32[]{:S(2)}) collective-permute-start(bf16[256,256]{1,0:T(8,128)(2,1)S(1)} %get-tuple-element.54), channel_id=1, source_target_pairs={{0,14},{1,15},{2,0},{3,1},{4,2},{5,3},{6,4},{7,5},{8,6},{9,7},{10,... | collective-permute-start | bytes 393224 | tf_op jit(solution)/shard_map/ppermute | solution.py:430
  47.1 2.1 %collective-permute-start.18 = (bf16[256,256]{1,0:T(8,128)(2,1)S(1)}, bf16[256,256]{1,0:T(8,128)(2,1)S(1)}, u32[]{:S(2)}, u32[]{:S(2)}) collective-permute-start(bf16[256,256]{1,0:T(8,128)(2,1)S(1)} %get-tuple-element.57), channel_id=1, source_target_pairs={{0,12},{1,13},{2,14},{3,15},{4,0},{5,1},{6,2},{7,3},{8,4},{9,5},{1... | collective-permute-start | bytes 393224 | tf_op jit(solution)/shard_map/ppermute | solution.py:430
  49.8 2.3 %collective-permute-start.15 = (bf16[256,256]{1,0:T(8,128)(2,1)S(1)}, bf16[256,256]{1,0:T(8,128)(2,1)S(1)}, u32[]{:S(2)}, u32[]{:S(2)}) collective-permute-start(bf16[256,256]{1,0:T(8,128)(2,1)S(1)} %fusion.4), channel_id=1, source_target_pairs={{0,12},{1,13},{2,14},{3,15},{4,0},{5,1},{6,2},{7,3},{8,4},{9,5},{1... | collective-permute-start | bytes 393224 | tf_op jit(solution)/shard_map/ppermute | solution.py:430
  52.2 4.0 %collective-permute-start.19 = (bf16[256,256]{1,0:T(8,128)(2,1)S(1)}, bf16[256,256]{1,0:T(8,128)(2,1)S(1)}, u32[]{:S(2)}, u32[]{:S(2)}) collective-permute-start(bf16[256,256]{1,0:T(8,128)(2,1)S(1)} %fusion.9), channel_id=1, source_target_pairs={{0,12},{1,13},{2,14},{3,15},{4,0},{5,1},{6,2},{7,3},{8,4},{9,5},{1... | collective-permute-start | bytes 393224 | tf_op jit(solution)/shard_map/ppermute | solution.py:430
  56.2 2.7 %collective-permute-done.19 = bf16[256,256]{1,0:T(8,128)(2,1)S(1)} collective-permute-done((bf16[256,256]{1,0:T(8,128)(2,1)S(1)}, bf16[256,256]{1,0:T(8,128)(2,1)S(1)}, u32[]{:S(2)}, u32[]{:S(2)}) %collective-permute-start.19) | collective-permute-done | bytes 131104 | tf_op jit(solution)/shard_map/ppermute | solution.py:430
  59.1 1.3 %collective-permute-done.20.refs_3_ = bf16[128,512]{1,0:T(8,128)(2,1)S(1)} collective-permute-done((bf16[128,512]{1,0:T(8,128)(2,1)S(1)}, bf16[128,512]{1,0:T(8,128)(2,1)S(1)}, u32[]{:S(2)}, u32[]{:S(2)}) %collective-permute-start.20) | collective-permute-done | bytes 131104 | tf_op jit(solution)/shard_map/ppermute | solution.py:433
  60.5 1.1 %place.1 = (bf16[128,4096]{1,0:T(8,128)(2,1)}, bf16[128,4096]{1,0:T(8,128)(2,1)}, bf16[128,512]{1,0:T(8,128)(2,1)}, bf16[128,512]{1,0:T(8,128)(2,1)}) custom-call(bf16[128,4096]{1,0:T(8,128)(2,1)} %get-tuple-element.44.o_in, bf16[128,4096]{1,0:T(8,128)(2,1)} %get-tuple-element.45.dq_in, ...), custom_call_target="tpu_custom_call", output_to_operand_aliasing={{0}: (0, {}), {1}: (1, {})} | custom-call | tf_op jit(solution)/shard_map/place/pallas_call | solution.py:404
  (34 shorter events, 1.5 us)
Async XLA Ops:
  2.0 1.5 %collective-permute-start = (bf16[128,512]{1,0:T(8,128)(2,1)S(1)}, bf16[128,512]{1,0:T(8,128)(2,1)S(1)}, u32[]{:S(2)}, u32[]{:S(2)}) collective-permute-start(bf16[128,512]{1,0:T(8,128)(2,1)S(1)} %get-tuple-element.32), channel_id=1, source_target_pairs={{0,1},{1,0},{2,3},{3,2},{4,5},{5,4},{6,7},{7,6},{8,9},{9,8},{10,11... | collective-permute-start | bytes 393224 | tf_op jit(solution)/shard_map/ppermute | solution.py:433
  3.6 13.6 %collective-permute-start.1 = (bf16[128,4096]{1,0:T(8,128)(2,1)S(1)}, bf16[128,4096]{1,0:T(8,128)(2,1)S(1)}, u32[]{:S(2)}, u32[]{:S(2)}) collective-permute-start(bf16[128,4096]{1,0:T(8,128)(2,1)S(1)} %get-tuple-element.34), channel_id=1, source_target_pairs={{0,1},{1,0},{2,3},{3,2},{4,5},{5,4},{6,7},{7,6},{8,9},{9,8},{10,11... | collective-permute-start | bytes 3145736 | tf_op jit(solution)/shard_map/ppermute | solution.py:433
  4.0 9.1 %collective-permute-start.6 = (bf16[256,256]{1,0:T(8,128)(2,1)S(1)}, bf16[256,256]{1,0:T(8,128)(2,1)S(1)}, u32[]{:S(2)}, u32[]{:S(2)}) collective-permute-start(bf16[256,256]{1,0:T(8,128)(2,1)S(1)} %get-tuple-element.41.kv0), channel_id=1, source_target_pairs={{0,4},{1,5},{2,6},{3,7},{4,8},{5,9},{6,10},{7,11},{8,12},{9,13},{1... | collective-permute-start | bytes 393224 | tf_op jit(solution)/shard_map/ppermute | solution.py:430
  6.8 9.4 %collective-permute-start.2 = (bf16[256,256]{1,0:T(8,128)(2,1)S(1)}, bf16[256,256]{1,0:T(8,128)(2,1)S(1)}, u32[]{:S(2)}, u32[]{:S(2)}) collective-permute-start(bf16[256,256]{1,0:T(8,128)(2,1)S(1)} %get-tuple-element.40.kv0), channel_id=1, source_target_pairs={{0,4},{1,5},{2,6},{3,7},{4,8},{5,9},{6,10},{7,11},{8,12},{9,13},{1... | collective-permute-start | bytes 393224 | tf_op jit(solution)/shard_map/ppermute | solution.py:430
  13.1 9.2 %collective-permute-start.8 = (bf16[256,256]{1,0:T(8,128)(2,1)S(1)}, bf16[256,256]{1,0:T(8,128)(2,1)S(1)}, u32[]{:S(2)}, u32[]{:S(2)}) collective-permute-start(bf16[256,256]{1,0:T(8,128)(2,1)S(1)} %broadcast_select_fusion), channel_id=1, source_target_pairs={{0,2},{1,3},{2,4},{3,5},{4,6},{5,7},{6,8},{7,9},{8,10},{9,11},{10,... | collective-permute-start | bytes 393224 | tf_op jit(solution)/shard_map/ppermute | solution.py:430
  14.9 8.7 %collective-permute-start.7 = (bf16[256,256]{1,0:T(8,128)(2,1)S(1)}, bf16[256,256]{1,0:T(8,128)(2,1)S(1)}, u32[]{:S(2)}, u32[]{:S(2)}) collective-permute-start(bf16[256,256]{1,0:T(8,128)(2,1)S(1)} %collective-permute-done.6.kv2), channel_id=1, source_target_pairs={{0,4},{1,5},{2,6},{3,7},{4,8},{5,9},{6,10},{7,11},{8,12},{9,13},{1... | collective-permute-start | bytes 393224 | tf_op jit(solution)/shard_map/ppermute | solution.py:430
  14.9 8.7 %collective-permute-start.9 = (bf16[256,256]{1,0:T(8,128)(2,1)S(1)}, bf16[256,256]{1,0:T(8,128)(2,1)S(1)}, u32[]{:S(2)}, u32[]{:S(2)}) collective-permute-start(bf16[256,256]{1,0:T(8,128)(2,1)S(1)} %collective-permute-done.6.kv2), channel_id=1, source_target_pairs={{0,2},{1,3},{2,0},{3,1},{4,6},{5,7},{6,4},{7,5},{8,10},{9,11},{10,... | collective-permute-start | bytes 393224 | tf_op jit(solution)/shard_map/ppermute | solution.py:436
  16.2 18.7 %collective-permute-start.4 = (bf16[256,256]{1,0:T(8,128)(2,1)S(1)}, bf16[256,256]{1,0:T(8,128)(2,1)S(1)}, u32[]{:S(2)}, u32[]{:S(2)}) collective-permute-start(bf16[256,256]{1,0:T(8,128)(2,1)S(1)} %broadcast_select_fusion.1), channel_id=1, source_target_pairs={{0,2},{1,3},{2,4},{3,5},{4,6},{5,7},{6,8},{7,9},{8,10},{9,11},{10,... | collective-permute-start | bytes 393224 | tf_op jit(solution)/shard_map/ppermute | solution.py:430
  17.2 20.2 %collective-permute-start.3 = (bf16[256,256]{1,0:T(8,128)(2,1)S(1)}, bf16[256,256]{1,0:T(8,128)(2,1)S(1)}, u32[]{:S(2)}, u32[]{:S(2)}) collective-permute-start(bf16[256,256]{1,0:T(8,128)(2,1)S(1)} %collective-permute-done.2.kv2), channel_id=1, source_target_pairs={{0,4},{1,5},{2,6},{3,7},{4,8},{5,9},{6,10},{7,11},{8,12},{9,13},{1... | collective-permute-start | bytes 393224 | tf_op jit(solution)/shard_map/ppermute | solution.py:430
  22.3 15.0 %collective-permute-start.5 = (bf16[256,256]{1,0:T(8,128)(2,1)S(1)}, bf16[256,256]{1,0:T(8,128)(2,1)S(1)}, u32[]{:S(2)}, u32[]{:S(2)}) collective-permute-start(bf16[256,256]{1,0:T(8,128)(2,1)S(1)} %collective-permute-done.2.kv2), channel_id=1, source_target_pairs={{0,2},{1,3},{2,0},{3,1},{4,6},{5,7},{6,4},{7,5},{8,10},{9,11},{10,... | collective-permute-start | bytes 393224 | tf_op jit(solution)/shard_map/ppermute | solution.py:436
  28.3 18.8 %collective-permute-start.12 = (bf16[256,256]{1,0:T(8,128)(2,1)S(1)}, bf16[256,256]{1,0:T(8,128)(2,1)S(1)}, u32[]{:S(2)}, u32[]{:S(2)}) collective-permute-start(bf16[256,256]{1,0:T(8,128)(2,1)S(1)} %get-tuple-element.49), channel_id=1, source_target_pairs={{0,14},{1,15},{2,0},{3,1},{4,2},{5,3},{6,4},{7,5},{8,6},{9,7},{10,... | collective-permute-start | bytes 393224 | tf_op jit(solution)/shard_map/ppermute | solution.py:430
  34.9 14.3 %collective-permute-start.13 = (bf16[256,256]{1,0:T(8,128)(2,1)S(1)}, bf16[256,256]{1,0:T(8,128)(2,1)S(1)}, u32[]{:S(2)}, u32[]{:S(2)}) collective-permute-start(bf16[256,256]{1,0:T(8,128)(2,1)S(1)} %get-tuple-element.51), channel_id=1, source_target_pairs={{0,2},{1,3},{2,0},{3,1},{4,6},{5,7},{6,4},{7,5},{8,10},{9,11},{10,... | collective-permute-start | bytes 393224 | tf_op jit(solution)/shard_map/ppermute | solution.py:436
  34.9 14.3 %collective-permute-start.14 = (bf16[256,256]{1,0:T(8,128)(2,1)S(1)}, bf16[256,256]{1,0:T(8,128)(2,1)S(1)}, u32[]{:S(2)}, u32[]{:S(2)}) collective-permute-start(bf16[256,256]{1,0:T(8,128)(2,1)S(1)} %get-tuple-element.52), channel_id=1, source_target_pairs={{0,12},{1,13},{2,14},{3,15},{4,0},{5,1},{6,2},{7,3},{8,4},{9,5},{1... | collective-permute-start | bytes 393224 | tf_op jit(solution)/shard_map/ppermute | solution.py:430
  42.2 7.6 %collective-permute-start.16 = (bf16[256,256]{1,0:T(8,128)(2,1)S(1)}, bf16[256,256]{1,0:T(8,128)(2,1)S(1)}, u32[]{:S(2)}, u32[]{:S(2)}) collective-permute-start(bf16[256,256]{1,0:T(8,128)(2,1)S(1)} %get-tuple-element.54), channel_id=1, source_target_pairs={{0,14},{1,15},{2,0},{3,1},{4,2},{5,3},{6,4},{7,5},{8,6},{9,7},{10,... | collective-permute-start | bytes 393224 | tf_op jit(solution)/shard_map/ppermute | solution.py:430
  47.1 5.0 %collective-permute-start.17 = (bf16[256,256]{1,0:T(8,128)(2,1)S(1)}, bf16[256,256]{1,0:T(8,128)(2,1)S(1)}, u32[]{:S(2)}, u32[]{:S(2)}) collective-permute-start(bf16[256,256]{1,0:T(8,128)(2,1)S(1)} %get-tuple-element.56), channel_id=1, source_target_pairs={{0,2},{1,3},{2,0},{3,1},{4,6},{5,7},{6,4},{7,5},{8,10},{9,11},{10,... | collective-permute-start | bytes 393224 | tf_op jit(solution)/shard_map/ppermute | solution.py:436
  47.1 5.0 %collective-permute-start.18 = (bf16[256,256]{1,0:T(8,128)(2,1)S(1)}, bf16[256,256]{1,0:T(8,128)(2,1)S(1)}, u32[]{:S(2)}, u32[]{:S(2)}) collective-permute-start(bf16[256,256]{1,0:T(8,128)(2,1)S(1)} %get-tuple-element.57), channel_id=1, source_target_pairs={{0,12},{1,13},{2,14},{3,15},{4,0},{5,1},{6,2},{7,3},{8,4},{9,5},{1... | collective-permute-start | bytes 393224 | tf_op jit(solution)/shard_map/ppermute | solution.py:430
  49.2 11.3 %collective-permute-start.11 = (bf16[128,2048]{1,0:T(8,128)(2,1)S(1)}, bf16[128,2048]{1,0:T(8,128)(2,1)S(1)}, u32[]{:S(2)}, u32[]{:S(2)}) collective-permute-start(bf16[128,2048]{1,0:T(8,128)(2,1)S(1)} %get-tuple-element.47), channel_id=1, source_target_pairs={{0,1},{1,0},{2,3},{3,2},{4,5},{5,4},{6,7},{7,6},{8,9},{9,8},{10,11... | collective-permute-start | bytes 1572872 | tf_op jit(solution)/shard_map/ppermute | solution.py:433
  49.2 11.3 %collective-permute-start.10 = (bf16[128,2048]{1,0:T(8,128)(2,1)S(1)}, bf16[128,2048]{1,0:T(8,128)(2,1)S(1)}, u32[]{:S(2)}, u32[]{:S(2)}) collective-permute-start(bf16[128,2048]{1,0:T(8,128)(2,1)S(1)} %get-tuple-element.46), channel_id=1, source_target_pairs={{0,1},{1,0},{2,3},{3,2},{4,5},{5,4},{6,7},{7,6},{8,9},{9,8},{10,11... | collective-permute-start | bytes 1572872 | tf_op jit(solution)/shard_map/ppermute | solution.py:433
  49.8 6.4 %collective-permute-start.15 = (bf16[256,256]{1,0:T(8,128)(2,1)S(1)}, bf16[256,256]{1,0:T(8,128)(2,1)S(1)}, u32[]{:S(2)}, u32[]{:S(2)}) collective-permute-start(bf16[256,256]{1,0:T(8,128)(2,1)S(1)} %fusion.4), channel_id=1, source_target_pairs={{0,12},{1,13},{2,14},{3,15},{4,0},{5,1},{6,2},{7,3},{8,4},{9,5},{1... | collective-permute-start | bytes 393224 | tf_op jit(solution)/shard_map/ppermute | solution.py:430
  52.2 6.7 %collective-permute-start.19 = (bf16[256,256]{1,0:T(8,128)(2,1)S(1)}, bf16[256,256]{1,0:T(8,128)(2,1)S(1)}, u32[]{:S(2)}, u32[]{:S(2)}) collective-permute-start(bf16[256,256]{1,0:T(8,128)(2,1)S(1)} %fusion.9), channel_id=1, source_target_pairs={{0,12},{1,13},{2,14},{3,15},{4,0},{5,1},{6,2},{7,3},{8,4},{9,5},{1... | collective-permute-start | bytes 393224 | tf_op jit(solution)/shard_map/ppermute | solution.py:430
  59.1 1.4 %collective-permute-start.20 = (bf16[128,512]{1,0:T(8,128)(2,1)S(1)}, bf16[128,512]{1,0:T(8,128)(2,1)S(1)}, u32[]{:S(2)}, u32[]{:S(2)}) collective-permute-start(bf16[128,512]{1,0:T(8,128)(2,1)S(1)} %get-tuple-element.58), channel_id=1, source_target_pairs={{0,1},{1,0},{2,3},{3,2},{4,5},{5,4},{6,7},{7,6},{8,9},{9,8},{10,11... | collective-permute-start | bytes 393224 | tf_op jit(solution)/shard_map/ppermute | solution.py:433
